TPU v7x, 32 devices: a whole 2x2x4 slice. The times are simulated.
32 devices in a mesh: src: 8 (over z, x), snk: 2 (over y), mom: 2 (over core).
Axes of the slice: x: 2, y: 2, z: 4, core: 2. Of those that a mesh axis runs over, the one named last changes fastest.
Arguments:
- peramb: bfloat16 [24, 8, 256, 256], P(None, 'snk', 'src'), may hold values from -0.375 to 0.375
- elem_src: bfloat16 [24, 16, 256, 256], P('src', 'mom'), may hold values from -6 to 6
- elem_snk: bfloat16 [24, 16, 256, 256], P('src', 'mom'), may hold values from -6 to 6
- op_elem: int32 [64], replicated, may hold values from 0 to 15
- hlt_kernel: float32 [8, 128], replicated, may hold values from -2 to 2
Outputs:
- smeared: float32 [64, 16, 128], P('src', 'mom')
All inputs are finite; a program needn't handle non-finite values.
Results may differ from a plain program's by a relative error of at most 0.004.
Values may be sent and summed in bfloat16 or wider, within the bound.
No kernel may reach another device: no remote copies, remote signals or barrier semaphores. Data moves between devices by JAX's collectives and lax.ppermute only.
A program may use at most 128 MiB of HBM per device.

v0:
```python
import math

import jax
import jax.numpy as jnp
from jax import lax
from jax.sharding import PartitionSpec as P


def shifted(value, axis, steps):
    count = lax.axis_size(axis)
    pairs = [(source, (source + steps) % count) for source in range(count)]
    return lax.ppermute(value, axis, pairs)


def body(peramb, elem_src, elem_snk, op_elem, hlt_kernel):
    source_count = peramb.shape[0]
    eigen_count = peramb.shape[3]
    highest = lax.Precision.HIGHEST
    regrouped = lax.all_to_all(peramb, "src", split_axis=0, concat_axis=2, tiled=True)
    half_product = jnp.einsum(
        "rsab,rfbc->rsfac", regrouped, elem_src, preferred_element_type=jnp.float32
    ).astype(jnp.bfloat16)
    sandwich = jnp.einsum(
        "rsfac,rsdc->rsfad", half_product, regrouped, preferred_element_type=jnp.float32
    ).astype(jnp.bfloat16)
    own_count = elem_snk.shape[0]
    sep_local = regrouped.shape[1]
    sep_total = sep_local * lax.axis_size("snk")
    reach_blocks = (own_count + sep_total - 2) // own_count
    blocks = [elem_snk] + [
        shifted(elem_snk, "src", -offset) for offset in range(1, reach_blocks + 1)
    ]
    stacked = jnp.concatenate(blocks, axis=0)
    window = lax.dynamic_slice_in_dim(
        stacked, lax.axis_index("snk") * sep_local, own_count + sep_local - 1, 0
    )
    block_elems = lax.all_gather(window, "mom", axis=1, tiled=True)
    trace_rows = [
        jnp.einsum(
            "seab,sfab->sef",
            block_elems[source_row : source_row + sep_local],
            sandwich[source_row],
            preferred_element_type=jnp.float32,
        )
        for source_row in range(own_count)
    ]
    pair_traces = jnp.stack(trace_rows, axis=0)
    elem_count = pair_traces.shape[2]
    onehot = (op_elem[:, None] == jnp.arange(elem_count, dtype=jnp.int32)[None, :]).astype(
        jnp.float32
    )
    norm_factor = 1.0 / (eigen_count * math.sqrt(source_count))
    correlator = jnp.einsum("oe,rsef->osf", onehot, pair_traces, precision=highest) * norm_factor
    owned_part = lax.psum_scatter(correlator, "src", scatter_dimension=0, tiled=True)
    all_sinks = lax.all_gather(owned_part, "snk", axis=1, tiled=True)
    result = jnp.einsum("otf,tk->ofk", all_sinks, hlt_kernel, precision=highest)
    return result


def solution(mesh):
    placed = (
        P(None, "snk", "src", None),
        P("src", "mom", None, None),
        P("src", "mom", None, None),
        P(),
        P(),
    )
    return jax.shard_map(
        body, mesh=mesh, in_specs=placed, out_specs=P("src", "mom", None), check_vma=False
    )
```

profile of v0, /device:TPU:0, one launch (start us, length us, event | category | flops | bytes accessed | tf_op | source)
XLA Modules:
  0.0 450.5 jit_solution(1892657292677292353)
XLA Ops:
  6.5 0.0 copy-start
  6.5 0.0 all-gather.2.cloned.1.call-start
  6.5 6.0 %collective-permute-start = (bf16[3,8,256,256]{3,2,1,0:T(8,128)(2,1)}, bf16[3,8,256,256]{3,2,1,0:T(8,128)(2,1)}, u32[]{:S(2)}, u32[]{:S(2)}) collective-permute-start(bf16[3,8,256,256]{3,2,1,0:T(8,128)(2,1)} %param.7), channel_id=1, source_target_pairs={{0,28},{4,0},{8,4},{12,8},{16,12},{20,16},{24,20},{28,24},{1,29},{... | collective-permute-start | bytes 9437192 | tf_op jit(solution)/shard_map/ppermute | solution.py:12
  12.5 0.4 collective-permute-start.1
  13.0 0.0 collective-permute-start.2
  13.0 68.4 %collective-permute-done = bf16[3,8,256,256]{3,2,1,0:T(8,128)(2,1)} collective-permute-done((bf16[3,8,256,256]{3,2,1,0:T(8,128)(2,1)}, bf16[3,8,256,256]{3,2,1,0:T(8,128)(2,1)}, u32[]{:S(2)}, u32[]{:S(2)}) %collective-permute-start) | collective-permute-done | bytes 3145760 | tf_op jit(solution)/shard_map/ppermute | solution.py:12
  81.4 67.4 %collective-permute-done.1 = bf16[3,8,256,256]{3,2,1,0:T(8,128)(2,1)} collective-permute-done((bf16[3,8,256,256]{3,2,1,0:T(8,128)(2,1)}, bf16[3,8,256,256]{3,2,1,0:T(8,128)(2,1)}, u32[]{:S(2)}, u32[]{:S(2)}) %collective-permute-start.1) | collective-permute-done | bytes 3145760 | tf_op jit(solution)/shard_map/ppermute | solution.py:12
  148.8 66.3 %collective-permute-done.2 = bf16[3,8,256,256]{3,2,1,0:T(8,128)(2,1)} collective-permute-done((bf16[3,8,256,256]{3,2,1,0:T(8,128)(2,1)}, bf16[3,8,256,256]{3,2,1,0:T(8,128)(2,1)}, u32[]{:S(2)}, u32[]{:S(2)}) %collective-permute-start.2) | collective-permute-done | bytes 3145760 | tf_op jit(solution)/shard_map/ppermute | solution.py:12
  215.1 7.8 %fusion.16 = bf16[6,8,256,256]{3,2,1,0:T(8,128)(2,1)} fusion(s32[]{:T(128)S(6)} %select_n.3, bf16[3,8,256,256]{3,2,1,0:T(8,128)(2,1)} %param.7, bf16[3,8,256,256]{3,2,1,0:T(8,128)(2,1)} %collective-permute-done, bf16[3,8,256,256]{3,2,1,0:T(8,128)(2,1)} %collective-permute-done.1, bf16[3,8,256,256]{3,2,1,0:T(8,128)(2,1)} %collective-permute-done.2), kind=kLoop, calls=%fused_computation.17 | loop fusion | flops 9437184 | bytes 18874372 | tf_op jit(solution)/shard_map/concatenate | solution.py:33
  222.8 0.0 copy-start.6
  222.8 0.0 all-gather.2.cloned.1.call-update
  222.9 73.8 %all-to-all-start = ((bf16[24,4,32,256]{3,2,1,0:T(8,128)(2,1)}), bf16[24,4,32,256]{3,2,1,0:T(8,128)(2,1)}, u32[]{:S(2)}, u32[]{:S(2)}) async-start(bf16[24,4,32,256]{3,2,1,0:T(8,128)(2,1)} %param.5), calls=%async_computation | async-start | bytes 3145728 | tf_op jit(solution)/shard_map/all_to_all | solution.py:19
  296.7 0.0 copy-done.6
  296.7 0.6 dynamic-slice
  298.0 36.0 %all-to-all-done = bf16[24,4,32,256]{3,2,1,0:T(8,128)(2,1)} async-done(((bf16[24,4,32,256]{3,2,1,0:T(8,128)(2,1)}), bf16[24,4,32,256]{3,2,1,0:T(8,128)(2,1)}, u32[]{:S(2)}, u32[]{:S(2)}) %all-to-all-start) | async-done | bytes 1572896 | tf_op jit(solution)/shard_map/all_to_all | solution.py:19
  334.0 2.7 copy.7
  336.7 0.0 copy-done
  336.7 11.2 %fusion.11 = bf16[3,4,8,256,256]{4,3,2,1,0:T(8,128)(2,1)} fusion(bf16[3,4,256,256,1]{3,2,4,1,0:T(8,128)(2,1)} %bitcast.48, bf16[3,8,256,256]{3,2,1,0:T(8,128)(2,1)S(1)} %copy-done), kind=kOutput, calls=%fused_computation.14 | convolution fusion | flops 6455033856 | bytes 17301504 | tf_op jit(solution)/shard_map/rsfac,rsdc->rsfad/dot_general | solution.py:23
  347.9 9.0 %slice_bitcast_fusion.2 = (bf16[4,8,256,256]{3,2,1,0:T(8,128)(2,1)}, bf16[4,8,256,256]{3,2,1,0:T(8,128)(2,1)}, bf16[4,8,256,256]{3,2,1,0:T(8,128)(2,1)}) fusion(bf16[3,4,8,256,256]{4,3,2,1,0:T(8,128)(2,1)} %fusion.11), kind=kLoop, calls=%fused_computation.20 | loop fusion | bytes 25165824 | tf_op jit(solution)/shard_map/squeeze | solution.py:42
  356.9 0.0 all-gather.2.cloned.1.call-done
  356.9 0.0 copy-start.3
  356.9 15.9 %fusion.54 = (bf16[4,16,256,256]{3,2,1,0:T(8,128)(2,1)S(1)}, bf16[4,16,256,256]{3,2,1,0:T(8,128)(2,1)}, bf16[4,16,256,256]{3,2,1,0:T(8,128)(2,1)}) fusion(bf16[6,16,256,256]{3,2,1,0:T(8,128)(2,1)} %all-gather.2.cloned.1.call-done), kind=kLoop, calls=%fused_computation.39 | loop fusion | bytes 50331648 | tf_op jit(solution)/shard_map/slice | solution.py:41
  372.8 0.0 copy-done.3
  372.8 10.0 %fusion.27 = f32[4,16,8]{2,1,0:T(8,128)S(1)} fusion(bf16[4,8,256,256]{3,2,1,0:T(8,128)(2,1)S(1)} %copy-done.3, bf16[4,16,256,256]{3,2,1,0:T(8,128)(2,1)} %get-tuple-element.7), kind=kOutput, calls=%fused_computation.26 | convolution fusion | flops 67108864 | bytes 12584960 | tf_op jit(solution)/shard_map/seab,sfab->sef/dot_general | solution.py:39
  382.8 0.0 copy-start.2
  382.8 11.5 %fusion.32 = f32[4,16,8]{2,1,0:T(8,128)S(1)} fusion(bf16[4,8,256,256]{3,2,1,0:T(8,128)(2,1)} %get-tuple-element.9, bf16[4,16,256,256]{3,2,1,0:T(8,128)(2,1)} %get-tuple-element.6), kind=kOutput, calls=%fused_computation.27 | convolution fusion | flops 67108864 | bytes 12584960 | tf_op jit(solution)/shard_map/seab,sfab->sef/dot_general | solution.py:39
  394.3 0.0 copy-done.2
  394.3 0.0 copy-start.5
  394.3 0.0 copy-start.4
  394.3 0.0 copy-start.1
  394.4 7.1 %fusion.42 = f32[4,16,8]{2,1,0:T(8,128)S(1)} fusion(f32[4,16,8]{2,1,0:T(8,128)S(1)} %fusion.32, f32[4,16,8]{2,1,0:T(8,128)S(1)} %fusion.27, bf16[4,8,256,256]{3,2,1,0:T(8,128)(2,1)S(1)} %copy-done.2, bf16[4,16,256,256]{3,2,1,0:T(8,128)(2,1)S(1)} %get-tuple-element.5), kind=kOutput, calls=%fused_computation.29 | convolution fusion | flops 67109888 | bytes 12589056 | tf_op jit(solution)/shard_map/seab,sfab->sef/dot_general | solution.py:39
  401.5 0.0 copy-done.5
  401.5 0.2 fusion.50
  401.7 0.1 copy.21
  401.9 36.5 %all-reduce = f32[64,4,8]{2,1,0:T(4,128)S(1)} all-reduce(f32[64,4,8]{2,1,0:T(4,128)S(1)} %broadcast_multiply_fusion), channel_id=2, replica_groups=mesh['src'=8,'snk'=2,'mom'=2] {'src'}, use_global_device_ids=true, to_apply=%region_0.0.clone | all-reduce | flops 2048 | bytes 16384
  438.4 4.4 all_gather.7
  442.8 0.0 copy-done.4
  442.8 0.9 fusion.47
  443.7 0.0 copy-done.1
  (3 shorter events, 0.0 us)
Async XLA Ops:
  6.5 330.2 %copy-start = (bf16[3,8,256,256]{3,2,1,0:T(8,128)(2,1)S(1)}, bf16[3,8,256,256]{3,2,1,0:T(8,128)(2,1)}, u32[]{:S(2)}) copy-start(bf16[3,8,256,256]{3,2,1,0:T(8,128)(2,1)} %param.6) | copy-start | bytes 9437188
  6.5 350.4 %all-gather.2.cloned.1.call-start = ((), (), s32[]{:S(2)}) async-start(), calls=%async_computation.1 | async-start | bytes 18874368 | tf_op jit(solution)/shard_map/all_gather | solution.py:37
  6.5 74.8 %collective-permute-start = (bf16[3,8,256,256]{3,2,1,0:T(8,128)(2,1)}, bf16[3,8,256,256]{3,2,1,0:T(8,128)(2,1)}, u32[]{:S(2)}, u32[]{:S(2)}) collective-permute-start(bf16[3,8,256,256]{3,2,1,0:T(8,128)(2,1)} %param.7), channel_id=1, source_target_pairs={{0,28},{4,0},{8,4},{12,8},{16,12},{20,16},{24,20},{28,24},{1,29},{... | collective-permute-start | bytes 9437192 | tf_op jit(solution)/shard_map/ppermute | solution.py:12
  12.5 136.3 %collective-permute-start.1 = (bf16[3,8,256,256]{3,2,1,0:T(8,128)(2,1)}, bf16[3,8,256,256]{3,2,1,0:T(8,128)(2,1)}, u32[]{:S(2)}, u32[]{:S(2)}) collective-permute-start(bf16[3,8,256,256]{3,2,1,0:T(8,128)(2,1)} %param.7), channel_id=1, source_target_pairs={{0,24},{4,28},{8,0},{12,4},{16,8},{20,12},{24,16},{28,20},{1,25},{... | collective-permute-start | bytes 9437192 | tf_op jit(solution)/shard_map/ppermute | solution.py:12
  13.0 202.1 %collective-permute-start.2 = (bf16[3,8,256,256]{3,2,1,0:T(8,128)(2,1)}, bf16[3,8,256,256]{3,2,1,0:T(8,128)(2,1)}, u32[]{:S(2)}, u32[]{:S(2)}) collective-permute-start(bf16[3,8,256,256]{3,2,1,0:T(8,128)(2,1)} %param.7), channel_id=1, source_target_pairs={{0,20},{4,24},{8,28},{12,0},{16,4},{20,8},{24,12},{28,16},{1,21},{... | collective-permute-start | bytes 9437192 | tf_op jit(solution)/shard_map/ppermute | solution.py:12
  222.8 73.9 %copy-start.6 = (u32[32]{0:T(128)S(1)}, u32[32]{0:T(128)}, u32[]{:S(2)}) copy-start(u32[32]{0:T(128)} %constant.17) | copy-start | bytes 388
  222.9 111.1 %all-to-all-start = ((bf16[24,4,32,256]{3,2,1,0:T(8,128)(2,1)}), bf16[24,4,32,256]{3,2,1,0:T(8,128)(2,1)}, u32[]{:S(2)}, u32[]{:S(2)}) async-start(bf16[24,4,32,256]{3,2,1,0:T(8,128)(2,1)} %param.5), calls=%async_computation | async-start | bytes 3145728 | tf_op jit(solution)/shard_map/all_to_all | solution.py:19
  356.9 15.9 %copy-start.3 = (bf16[4,8,256,256]{3,2,1,0:T(8,128)(2,1)S(1)}, bf16[4,8,256,256]{3,2,1,0:T(8,128)(2,1)}, u32[]{:S(2)}) copy-start(bf16[4,8,256,256]{3,2,1,0:T(8,128)(2,1)} %get-tuple-element.10) | copy-start | bytes 12582916
  382.8 11.6 %copy-start.2 = (bf16[4,8,256,256]{3,2,1,0:T(8,128)(2,1)S(1)}, bf16[4,8,256,256]{3,2,1,0:T(8,128)(2,1)}, u32[]{:S(2)}) copy-start(bf16[4,8,256,256]{3,2,1,0:T(8,128)(2,1)} %get-tuple-element.8) | copy-start | bytes 12582916
  394.3 7.2 %copy-start.5 = (s32[64]{0:T(128)S(1)}, s32[64]{0:T(128)}, u32[]{:S(2)}) copy-start(s32[64]{0:T(128)} %param.8) | copy-start | bytes 772
  394.3 48.5 %copy-start.4 = (f32[8,128]{1,0:T(8,128)S(1)}, f32[8,128]{1,0:T(8,128)}, u32[]{:S(2)}) copy-start(f32[8,128]{1,0:T(8,128)} %param.9) | copy-start | bytes 12292
  394.3 49.3 %copy-start.1 = (bf16[3,8,256,256]{3,2,1,0:T(8,128)(2,1)S(1)}, bf16[3,8,256,256]{3,2,1,0:T(8,128)(2,1)}, u32[]{:S(2)}) copy-start(bf16[3,8,256,256]{3,2,1,0:T(8,128)(2,1)} %param.6) | copy-start | bytes 9437188
Sparse Core Ops, SparseCore 0:
  223.0 94.1 all-gather.1
where the time goes:
time: 451 us
  waiting for transfers between devices  238 us (53%)
  starting transfers between devices  80.3 us (18%)
  matrix products  40.9 us (9%)
  blocking collectives  40.9 us (9%)
  local copies, waits for them, and re-layouts  28.3 us (6%)
  between operations  14.1 us (3%)
  other arithmetic  7.82 us (2%)
    ppermute x3, waiting for transfers between devices, shifted(): return lax.ppermute(value, axis, pairs)  202 us
    all_to_all x1, starting transfers between devices, body(): lax.all_to_all(peramb, 'src', split_axis=0, concat_axis=2, tiled=True)  73.8 us
    unnamed x1, blocking collectives  36.5 us
    all_to_all x1, waiting for transfers between devices, body(): lax.all_to_all(peramb, 'src', split_axis=0, concat_axis=2, tiled=True)  36 us
    dot_general x3, matrix products, body(): jnp.einsum('seab,sfab->sef', block_elems[source_row:source_row + sep_loca...  28.6 us
    slice x1, local copies, waits for them, and re-layouts, body(): block_elems[source_row:source_row + sep_local]  15.9 us
    dot_general x1, matrix products, body(): jnp.einsum('rsfac,rsdc->rsfad', half_product, regrouped, preferred_elemen...  11.2 us
  transfers between devices with their start and end apart: 5, of which 4 were waited for; matrix products, arithmetic and copies ran while one was open for 5% of the time, Pallas kernels for 0%

commit v1 on v0

v1 whole, which is shorter than its diff:
```python
import functools
import math

import jax
import jax.numpy as jnp
from jax import lax
from jax.experimental import pallas as pl
from jax.experimental.pallas import tpu as pltpu
from jax.sharding import PartitionSpec as P

BLK = 16
ANY = pl.BlockSpec(memory_space=pl.ANY)


def shifted(value, axis, steps):
    count = lax.axis_size(axis)
    pairs = [(source, (source + steps) % count) for source in range(count)]
    return lax.ppermute(value, axis, pairs)


def swapped(value, axis):
    count = lax.axis_size(axis)
    return lax.ppermute(value, axis, [(source, source ^ 1) for source in range(count)])


def copy_all(copies):
    for copy in copies:
        copy.start()
    for copy in copies:
        copy.wait()


def shear_kernel(n_src, own, seps, peramb_ref, out_ref, sems):
    source_count = peramb_ref.shape[0]
    sep_local = peramb_ref.shape[1]
    first = lax.axis_index("mom") * seps
    sep0 = lax.axis_index("snk") * sep_local + first
    copies = []
    for d in range(n_src):
        for j in range(own):
            for h in range(seps):
                start = lax.rem(own * d + j - h - sep0 + 2 * source_count, source_count)
                copies.append(
                    pltpu.make_async_copy(
                        peramb_ref.at[start, first + h], out_ref.at[d, j, h], sems.at[len(copies)]
                    )
                )
    copy_all(copies)


def shear(peramb, n_src, own, seps):
    rows, cols = peramb.shape[2:]
    return pl.pallas_call(
        functools.partial(shear_kernel, n_src, own, seps),
        out_shape=jax.ShapeDtypeStruct((n_src, own, seps, rows, cols), peramb.dtype),
        in_specs=[ANY],
        out_specs=ANY,
        scratch_shapes=[pltpu.SemaphoreType.DMA((n_src * own * seps,))],
    )(peramb)


def trace_kernel(units, own, nf, n_sep, perm_parts, elem_parts, n_slices, *refs):
    refs = list(refs)
    p_in = [refs.pop(0) for _ in perm_parts]
    s_in = [refs.pop(0) for _ in range(elem_parts)]
    e_in = [refs.pop(0) for _ in range(n_slices)]
    out_ref, p_ref, s_ref, e_ref, w_ref, acc_ref, p_sem, s_sem, e_sem = refs
    nv = p_ref.shape[-1]
    ne_part = s_in[0].shape[1]
    ne = s_ref.shape[1]
    n_snk, n_mom = lax.axis_size("snk"), lax.axis_size("mom")
    sep_local = n_sep // n_snk
    seps = sep_local // n_mom
    y, m = lax.axis_index("snk"), lax.axis_index("mom")
    e_copies = [pltpu.make_async_copy(e_in[n], e_ref.at[n], e_sem.at[n]) for n in range(n_slices)]
    p_copies = []
    for n, (dy, dm) in enumerate(perm_parts):
        at = lax.rem(y + dy, n_snk) * sep_local + lax.rem(m + dm, n_mom) * seps
        p_copies.append(pltpu.make_async_copy(p_in[n], p_ref.at[:, pl.ds(at, seps)], p_sem.at[n]))
    s_copies = [
        pltpu.make_async_copy(s_in[n], s_ref.at[:, pl.ds(n * ne_part, ne_part)], s_sem.at[n])
        for n in range(elem_parts)
    ]
    for copy in p_copies + e_copies + s_copies:
        copy.start()
    for copy in p_copies + e_copies:
        copy.wait()

    by_slice = {}
    for n, (c, j, ts) in enumerate(units):
        by_slice.setdefault(c, []).append((n, j, ts))
    for c, group in by_slice.items():
        props = [p_ref[j, ts] for _, j, ts in group]
        stacked = jnp.concatenate(props, axis=0) if len(group) > 1 else props[0]
        halves = [
            jnp.dot(stacked, e_ref[c, f], preferred_element_type=jnp.float32).astype(jnp.bfloat16)
            for f in range(nf)
        ]
        for at, (n, j, ts) in enumerate(group):
            half = jnp.concatenate([h[at * nv : (at + 1) * nv] for h in halves], axis=0)
            sandwich = lax.dot_general(
                half, props[at], (((1,), (1,)), ((), ())), preferred_element_type=jnp.float32
            )
            w_ref[n] = sandwich.astype(jnp.bfloat16).reshape(nf, nv, nv)
    for copy in s_copies:
        copy.wait()

    acc_ref[...] = jnp.zeros_like(acc_ref)
    width = nf * BLK
    for j in range(own):
        group = [(n, ts) for n, (_, jj, ts) in enumerate(units) if jj == j]
        if not group:
            continue
        left = jnp.concatenate(
            [
                jnp.concatenate(
                    [w_ref[n, :, a : a + BLK, :].reshape(width, nv) for n, _ in group], axis=0
                )
                for a in range(0, nv, BLK)
            ],
            axis=1,
        )
        right = jnp.concatenate(
            [s_ref[j, :, a : a + BLK, :].reshape(ne * BLK, nv) for a in range(0, nv, BLK)], axis=1
        )
        part = lax.dot_general(
            left, right, (((1,), (1,)), ((), ())), preferred_element_type=jnp.float32
        )
        for at, (_, ts) in enumerate(group):
            acc_ref[ts * width : (ts + 1) * width] += part[at * width : (at + 1) * width]
    total = acc_ref[...]
    row = lax.broadcasted_iota(jnp.int32, total.shape, 0)
    col = lax.broadcasted_iota(jnp.int32, total.shape, 1)
    kept = jnp.where(lax.rem(row, BLK) == lax.rem(col, BLK), total, 0.0)
    kept = jnp.sum(kept.reshape(n_sep * nf, BLK, ne * BLK), axis=1)
    picked = lax.broadcasted_iota(jnp.int32, (ne * BLK, ne), 0)
    elem = lax.broadcasted_iota(jnp.int32, (ne * BLK, ne), 1)
    group_sum = jnp.where(lax.div(picked, BLK) == elem, 1.0, 0.0).astype(jnp.float32)
    out_ref[...] = jnp.dot(
        kept, group_sum, precision=lax.Precision.HIGHEST, preferred_element_type=jnp.float32
    )


def traces_of(units, slices, perms, elems, n_sep):
    own, ne_part, nv = elems[0].shape[0], elems[0].shape[1], elems[0].shape[2]
    nf = slices[0].shape[0]
    ne = ne_part * len(elems)
    flops = 2 * len(units) * nf * nv * nv * (2 * nv + ne * BLK)
    moved = 2 * nv * nv * (own * n_sep + own * ne + len(slices) * nf)
    return pl.pallas_call(
        functools.partial(
            trace_kernel, units, own, nf, n_sep, tuple(perms), len(elems), len(slices)
        ),
        out_shape=jax.ShapeDtypeStruct((n_sep * nf, ne), jnp.float32),
        in_specs=[ANY] * (len(perms) + len(elems) + len(slices)),
        out_specs=pl.BlockSpec(memory_space=pltpu.VMEM),
        scratch_shapes=[
            pltpu.VMEM((own, n_sep, nv, nv), jnp.bfloat16),
            pltpu.VMEM((own, ne, nv, nv), jnp.bfloat16),
            pltpu.VMEM((len(slices), nf, nv, nv), jnp.bfloat16),
            pltpu.VMEM((len(units), nf, nv, nv), jnp.bfloat16),
            pltpu.VMEM((n_sep * nf * BLK, ne * BLK), jnp.float32),
            pltpu.SemaphoreType.DMA((len(perms),)),
            pltpu.SemaphoreType.DMA((len(elems),)),
            pltpu.SemaphoreType.DMA((len(slices),)),
        ],
        compiler_params=pltpu.CompilerParams(vmem_limit_bytes=56 << 20),
        cost_estimate=pl.CostEstimate(flops=flops, bytes_accessed=moved, transcendentals=0),
    )(*perms.values(), *elems, *slices)


def body(peramb, elem_src, elem_snk, op_elem, hlt_kernel):
    source_count, sep_local, rows, nv = peramb.shape
    n_src, n_snk, n_mom = (lax.axis_size(axis) for axis in ("src", "snk", "mom"))
    s, y, m = (lax.axis_index(axis) for axis in ("src", "snk", "mom"))
    n_sep = sep_local * n_snk
    seps = sep_local // n_mom
    own, ne_part = elem_snk.shape[:2]
    nf = ne_part // n_snk
    highest = lax.Precision.HIGHEST
    even = s % 2 == 0

    quarter = lax.dynamic_slice_in_dim(elem_src, y * nf, nf, 1)
    sheared = shear(peramb, n_src, own, seps)

    def needed(block, i):
        return [(j, own * block + j - i) for j in range(own) if 0 <= own * block + j - i < n_sep]

    reach = -(-(n_sep - 1) // own)
    hops = reach // 2 + 1
    chain = [{i: quarter[i] for i in range(own)}]
    for hop in range(1, hops + 1):
        wanted = [i for i in range(own) if needed(2 * hop - 1, i)]
        chain.append({i: shifted(chain[-1][i], "src", 2) for i in reversed(wanted)})
    blocks = {}
    for block in range(reach + 1):
        for i in reversed(range(own)):
            if not needed(block, i):
                continue
            if block % 2 == 0:
                blocks[block, i] = chain[block // 2][i]
            else:
                low, high = chain[block // 2][i], chain[block // 2 + 1][i]
                blocks[block, i] = swapped(jnp.where(even, low, high), "src")

    rows_in = lax.all_to_all(sheared, "src", 0, 0)
    mine = jnp.transpose(rows_in, (1, 2, 0, 3, 4)).reshape(own, seps, n_src * rows, nv)
    perms = {(0, 0): mine}
    for dy in range(1, n_snk):
        perms[dy, 0] = shifted(mine, "snk", -dy)
    for dy in range(n_snk):
        for dm in range(1, n_mom):
            perms[dy, dm] = shifted(perms[dy, 0], "mom", -dm)
    elems = [elem_snk] + [shifted(elem_snk, "mom", -dm) for dm in range(1, n_mom)]

    order = sorted(blocks, key=lambda b: (b[0] > 0, -b[1]))
    groups = [[b for b in order if b[0] == 0 or b[1] == own - 1]]
    groups += [[b for b in order if b[0] > 0 and b[1] == i] for i in reversed(range(own - 1))]
    total = 0.0
    for group in groups:
        units = [(c, j, ts) for c, (k, i) in enumerate(group) for j, ts in needed(k, i)]
        total = total + traces_of(units, [blocks[b] for b in group], perms, elems, n_sep)

    if n_src == 8:
        for step in (1, 2, 4):
            total = total + lax.ppermute(total, "src", [(i, i ^ step) for i in range(n_src)])
    else:
        total = lax.psum(total, "src")
    gathered = lax.all_gather(total, "snk", axis=0)
    pair_traces = gathered.reshape(n_snk, n_sep, nf, ne_part * n_mom)
    n_ops = op_elem.shape[0] // n_src
    ops = lax.dynamic_slice_in_dim(op_elem, s * n_ops, n_ops, 0)
    names = (jnp.arange(n_mom * ne_part, dtype=jnp.int32) + m * ne_part) % (n_mom * ne_part)
    onehot = (ops[:, None] == names[None, :]).astype(jnp.float32)
    norm_factor = 1.0 / (nv * math.sqrt(source_count))
    correlator = jnp.einsum("oe,ytfe->otyf", onehot, pair_traces, precision=highest) * norm_factor
    correlator = correlator.reshape(n_ops, n_sep, ne_part)
    return jnp.einsum("otf,tk->ofk", correlator, hlt_kernel, precision=highest)


def solution(mesh):
    placed = (
        P(None, "snk", "src", None),
        P("src", "mom", None, None),
        P("src", "mom", None, None),
        P(),
        P(),
    )
    return jax.shard_map(
        body, mesh=mesh, in_specs=placed, out_specs=P("src", "mom", None), check_vma=False
    )
```

time: 451 us -> 174 us (0.39)
  waiting for transfers between devices: 238 us -> 61.4 us
  starting transfers between devices: 80.3 us -> 11.5 us
  Pallas kernels: 0 us -> 56.6 us
  matrix products: 40.9 us -> 0.98 us
  local copies, waits for them, and re-layouts: 28.3 us -> 7.13 us
  between operations: 14.1 us -> 0.17 us
  blocking collectives: 40.9 us -> 31.9 us
    ppermute x3 -> x8, waiting for transfers between devices: 202 us -> 42.2 us  [shifted(): return lax.ppermute(value, axis, pairs)]
    all_to_all x1 -> x0, starting transfers between devices: 73.8 us -> none  [body(): lax.all_to_all(peramb, 'src', split_axis=0, concat_axis=2, tiled=True)]
    pallas_call x0 -> x4, Pallas kernels: none -> 56.6 us  [the longest x3 31.3 us: traces_of(): pl.pallas_call(functools.partial(trace_kernel, units, own, nf, n_sep, tup...]
    dot_general x6 -> x2, matrix products: 40.9 us -> 0.98 us  [the longest x1 0.78 us: body(): return jnp.einsum('otf,tk->ofk', correlator, hlt_kernel, precision=highest)]
    unnamed x1 -> x0, blocking collectives: 36.5 us -> none
    all_to_all x1 -> x0, waiting for transfers between devices: 36 us -> none  [body(): lax.all_to_all(peramb, 'src', split_axis=0, concat_axis=2, tiled=True)]
    all_to_all x0 -> x1, blocking collectives: none -> 27.6 us  [body(): rows_in = lax.all_to_all(sheared, 'src', 0, 0)]
    ppermute x0 -> x7, waiting for transfers between devices: none -> 19.3 us  [the longest x3 10.3 us: body(): lax.ppermute(total, 'src', [(i, i ^ step) for i in range(n_src)])]
  transfers between devices with their start and end apart: 5 -> 15, of which waited for: 4 -> 9; matrix products, arithmetic and copies ran while one was open for 5% -> 4% of each run, Pallas kernels for 0% -> 25%
where the time goes in v1:
time: 174 us
  waiting for transfers between devices  61.4 us (35%)
  Pallas kernels  56.6 us (33%)
  blocking collectives  31.9 us (18%)
  starting transfers between devices  11.5 us (7%)
  local copies, waits for them, and re-layouts  7.13 us (4%)
  other arithmetic  4.3 us (2%)
    ppermute x8, waiting for transfers between devices, shifted(): return lax.ppermute(value, axis, pairs)  42.2 us
    pallas_call x3, Pallas kernels, traces_of(): pl.pallas_call(functools.partial(trace_kernel, units, own, nf, n_sep, tup...  31.3 us
    all_to_all x1, blocking collectives, body(): rows_in = lax.all_to_all(sheared, 'src', 0, 0)  27.6 us
    pallas_call x1, Pallas kernels, shear(): pl.pallas_call(functools.partial(shear_kernel, n_src, own, seps), out_sha...  25.4 us
    ppermute x3, waiting for transfers between devices, body(): lax.ppermute(total, 'src', [(i, i ^ step) for i in range(n_src)])  10.3 us
    ppermute x4, waiting for transfers between devices, swapped(): lax.ppermute(value, axis, [(source, source ^ 1) for source in range(count)])  8.97 us
    ppermute x4, starting transfers between devices, swapped(): lax.ppermute(value, axis, [(source, source ^ 1) for source in range(count)])  5.02 us
    ppermute x8, starting transfers between devices, shifted(): return lax.ppermute(value, axis, pairs)  4.79 us
  transfers between devices with their start and end apart: 15, of which 9 were waited for; matrix products, arithmetic and copies ran while one was open for 4% of the time, Pallas kernels for 25%

profile of v1, /device:TPU:0, one launch (start us, length us, event | category | flops | bytes accessed | tf_op | source)
XLA Modules:
  0.0 174.1 jit_solution(3419529441068332244)
XLA Ops:
  0.0 0.0 copy-start
  0.0 0.5 collective-permute-start.3
  0.5 25.4 %shard_map.55 = bf16[8,3,2,32,256]{4,3,2,1,0:T(8,128)(2,1)} custom-call(bf16[24,4,32,256]{3,2,1,0:T(8,128)(2,1)} %peramb_ref.1), custom_call_target="tpu_custom_call" | custom-call | tf_op jit(solution)/shard_map/pallas_call | solution.py:53
  25.8 27.6 %all_to_all.5 = bf16[8,3,2,32,256]{4,3,2,1,0:T(8,128)(2,1)S(1)} all-to-all(bf16[8,3,2,32,256]{4,3,2,1,0:T(8,128)(2,1)} %shard_map.55), channel_id=1, replica_groups=mesh['src'=8,'snk'=2,'mom'=2] {'src'}, dimensions={0} | all-to-all | bytes 1572864 | tf_op jit(solution)/shard_map/all_to_all | solution.py:206
  53.4 1.0 copy.12
  54.4 1.5 collective-permute-start
  55.9 2.5 %dynamic-slice_bitcast_fusion.1 = (bf16[4,256,256]{2,1,0:T(8,128)(2,1)}, bf16[4,256,256]{2,1,0:T(8,128)(2,1)}, bf16[4,256,256]{2,1,0:T(8,128)(2,1)}) fusion(bf16[3,8,256,256]{3,2,1,0:T(8,128)(2,1)} %param.6, s32[]{:T(128)S(6)} %add.57, s32[]{:T(128)S(6)} %select_n.43, s32[]{:T(128)S(6)} %add.56), kind=kLoop, calls=%fused_computation.2 | loop fusion | bytes 3145740 | tf_op jit(solution)/shard_map/squeeze | solution.py:191
  58.4 1.1 collective-permute-start.4
  59.5 0.3 collective-permute-start.10
  59.8 0.9 collective-permute-start.8
  60.7 14.7 %collective-permute-done.4.refs_10_ = bf16[4,256,256]{2,1,0:T(8,128)(2,1)} collective-permute-done((bf16[4,256,256]{2,1,0:T(8,128)(2,1)}, bf16[4,256,256]{2,1,0:T(8,128)(2,1)}, u32[]{:S(2)}, u32[]{:S(2)}) %collective-permute-start.4) | collective-permute-done | bytes 524320 | tf_op jit(solution)/shard_map/ppermute | solution.py:18
  75.4 0.0 collective-permute-start.6
  75.4 11.2 %collective-permute-done.10.refs_7_ = bf16[4,256,256]{2,1,0:T(8,128)(2,1)} collective-permute-done((bf16[4,256,256]{2,1,0:T(8,128)(2,1)}, bf16[4,256,256]{2,1,0:T(8,128)(2,1)}, u32[]{:S(2)}, u32[]{:S(2)}) %collective-permute-start.10) | collective-permute-done | bytes 524320 | tf_op jit(solution)/shard_map/ppermute | solution.py:18
  86.6 0.0 collective-permute-start.1
  86.6 0.0 collective-permute-done.refs_1_
  86.6 0.5 collective-permute-start.2
  87.1 1.1 broadcast_select_fusion
  88.3 9.6 %collective-permute-done.8.refs_7_ = bf16[4,256,256]{2,1,0:T(8,128)(2,1)} collective-permute-done((bf16[4,256,256]{2,1,0:T(8,128)(2,1)}, bf16[4,256,256]{2,1,0:T(8,128)(2,1)}, u32[]{:S(2)}, u32[]{:S(2)}) %collective-permute-start.8) | collective-permute-done | bytes 524320 | tf_op jit(solution)/shard_map/ppermute | solution.py:18
  97.9 1.5 collective-permute-start.11
  99.3 1.1 broadcast_select_fusion.1
  100.4 6.6 %collective-permute-done.6 = bf16[4,256,256]{2,1,0:T(8,128)(2,1)S(1)} collective-permute-done((bf16[4,256,256]{2,1,0:T(8,128)(2,1)}, bf16[4,256,256]{2,1,0:T(8,128)(2,1)S(1)}, u32[]{:S(2)}, u32[]{:S(2)}) %collective-permute-start.6) | collective-permute-done | bytes 524320 | tf_op jit(solution)/shard_map/ppermute | solution.py:18
  107.1 1.5 collective-permute-start.9
  108.5 1.4 broadcast_select_fusion.2
  109.9 0.0 collective-permute-done.11.refs_6_
  109.9 0.0 copy-start.4
  109.9 0.5 collective-permute-start.5
  110.4 0.0 collective-permute-done.1.refs_2_
  110.4 1.6 collective-permute-start.7
  112.0 0.0 collective-permute-done.2.refs_3_
  112.0 0.0 collective-permute-done.3.refs_5_
  112.0 0.0 copy-done.4
  112.0 0.0 copy-done.2
  112.0 0.9 copy-done.3
  112.9 1.6 copy-done.1
  114.5 8.5 %shard_map.58 = f32[32,16]{1,0:T(8,128)} custom-call(bf16[3,2,256,256]{3,2,1,0:T(8,128)(2,1)} %bitcast.1.refs_0_, bf16[3,2,256,256]{3,2,1,0:T(8,128)(2,1)} %collective-permute-done.refs_1_, bf16[3,2,256,256]{3,2,1,0:T(8,128)(2,1)} %copy-done.2, bf16[3,2,256,256]{3,2,1,0:T(8,128)(2,1)} %copy-done.3, bf16[3,8,256,256]{3,2,1,0:T(8,128)(2,1)} %refs_4_.5, ...), custom_call_target="tpu_custom_call" | custom-call | flops 2013265920 | bytes 10485760 | tf_op jit(solution)/shard_map/pallas_call | solution.py:150
  123.1 0.0 collective-permute-done.9.refs_6_
  123.1 0.0 copy-start.5
  123.1 0.8 copy-done.5
  123.9 8.9 %shard_map.57 = f32[32,16]{1,0:T(8,128)} custom-call(bf16[3,2,256,256]{3,2,1,0:T(8,128)(2,1)} %bitcast.1.refs_0_, bf16[3,2,256,256]{3,2,1,0:T(8,128)(2,1)} %collective-permute-done.refs_1_, bf16[3,2,256,256]{3,2,1,0:T(8,128)(2,1)} %copy-done.2, bf16[3,2,256,256]{3,2,1,0:T(8,128)(2,1)} %copy-done.3, bf16[3,8,256,256]{3,2,1,0:T(8,128)(2,1)} %refs_4_.5, ...), custom_call_target="tpu_custom_call" | custom-call | flops 2415919104 | bytes 10485760 | tf_op jit(solution)/shard_map/pallas_call | solution.py:150
  132.8 0.0 copy-start.6
  132.8 0.0 copy-start.7
  132.8 0.0 copy-start.9
  132.8 0.4 collective-permute-done.5.refs_9_
  133.2 8.6 %collective-permute-done.7.refs_11_ = bf16[4,256,256]{2,1,0:T(8,128)(2,1)} collective-permute-done((bf16[4,256,256]{2,1,0:T(8,128)(2,1)S(1)}, bf16[4,256,256]{2,1,0:T(8,128)(2,1)}, u32[]{:S(2)}, u32[]{:S(2)}) %collective-permute-start.7) | collective-permute-done | bytes 524320 | tf_op jit(solution)/shard_map/ppermute | solution.py:23
  141.8 0.0 copy-done.8
  141.8 13.9 %shard_map.56 = f32[32,16]{1,0:T(8,128)} custom-call(bf16[3,2,256,256]{3,2,1,0:T(8,128)(2,1)} %bitcast.1.refs_0_, bf16[3,2,256,256]{3,2,1,0:T(8,128)(2,1)} %collective-permute-done.refs_1_, bf16[3,2,256,256]{3,2,1,0:T(8,128)(2,1)} %copy-done.2, bf16[3,2,256,256]{3,2,1,0:T(8,128)(2,1)} %copy-done.3, bf16[3,8,256,256]{3,2,1,0:T(8,128)(2,1)} %refs_4_.5, ...), custom_call_target="tpu_custom_call" | custom-call | flops 5234491392 | bytes 12582912 | tf_op jit(solution)/shard_map/pallas_call | solution.py:150
  155.6 0.0 copy-done.6
  155.6 0.0 copy-done.7
  155.7 0.7 add_add_fusion
  156.4 1.5 collective-permute-start.12
  157.8 2.3 %collective-permute-done.12 = f32[32,16]{1,0:T(8,128)S(1)} collective-permute-done((f32[32,16]{1,0:T(8,128)S(1)}, f32[32,16]{1,0:T(8,128)S(1)}, u32[]{:S(2)}, u32[]{:S(2)}) %collective-permute-start.12) | collective-permute-done | bytes 2080 | tf_op jit(solution)/shard_map/ppermute | solution.py:226
  160.1 0.0 collective-permute-start.13
  160.1 3.7 %collective-permute-done.13 = f32[32,16]{1,0:T(8,128)S(1)} collective-permute-done((f32[32,16]{1,0:T(8,128)S(1)}, f32[32,16]{1,0:T(8,128)S(1)}, u32[]{:S(2)}, u32[]{:S(2)}) %collective-permute-start.13) | collective-permute-done | bytes 2080 | tf_op jit(solution)/shard_map/ppermute | solution.py:226
  163.9 0.2 collective-permute-start.14
  164.1 0.0 copy-done.9
  164.1 0.1 dynamic_slice.7
  164.2 4.3 %collective-permute-done.14 = f32[32,16]{1,0:T(8,128)S(1)} collective-permute-done((f32[32,16]{1,0:T(8,128)S(1)}, f32[32,16]{1,0:T(8,128)S(1)}, u32[]{:S(2)}, u32[]{:S(2)}) %collective-permute-start.14) | collective-permute-done | bytes 2080 | tf_op jit(solution)/shard_map/ppermute | solution.py:226
  168.5 0.1 copy.13
  168.6 4.4 %all-gather.1 = f32[2,32,16]{1,2,0:T(8,128)S(1)} all-gather(f32[1,32,16]{1,2,0:T(8,128)S(1)} %copy.13), channel_id=2, replica_groups=mesh['src'=8,'snk'=2,'mom'=2] {'snk'}, dimensions={0}, use_global_device_ids=true | all-gather | bytes 6144 | tf_op jit(solution)/shard_map/all_gather | solution.py:229
  172.9 0.1 copy.14
  173.0 0.2 convolution_multiply_fusion
  173.2 0.1 copy.16
  173.3 0.0 copy-done
  173.3 0.8 fusion.1
  (8 shorter events, 0.0 us)
Async XLA Ops:
  0.0 173.3 %copy-start = (f32[8,128]{1,0:T(8,128)S(1)}, f32[8,128]{1,0:T(8,128)}, u32[]{:S(2)}) copy-start(f32[8,128]{1,0:T(8,128)} %param.9) | copy-start | bytes 12292
  0.0 112.0 %collective-permute-start.3 = (bf16[3,8,256,256]{3,2,1,0:T(8,128)(2,1)}, bf16[3,8,256,256]{3,2,1,0:T(8,128)(2,1)S(1)}, u32[]{:S(2)}, u32[]{:S(2)}) collective-permute-start(bf16[3,8,256,256]{3,2,1,0:T(8,128)(2,1)} %refs_4_.5), channel_id=1, source_target_pairs={{0,1},{1,0},{2,3},{3,2},{4,5},{5,4},{6,7},{7,6},{8,9},{9,8},{10,11... | collective-permute-start | bytes 9437192 | tf_op jit(solution)/shard_map/ppermute | solution.py:18
  54.4 32.3 %collective-permute-start = (bf16[3,2,256,256]{3,2,1,0:T(8,128)(2,1)}, bf16[3,2,256,256]{3,2,1,0:T(8,128)(2,1)}, u32[]{:S(2)}, u32[]{:S(2)}) collective-permute-start(bf16[3,2,256,256]{3,2,1,0:T(8,128)(2,1)} %bitcast.1.refs_0_), channel_id=1, source_target_pairs={{0,2},{2,0},{1,3},{3,1},{4,6},{6,4},{5,7},{7,5},{8,10},{10,8},{9,1... | collective-permute-start | bytes 2359304 | tf_op jit(solution)/shard_map/ppermute | solution.py:18
  58.4 17.0 %collective-permute-start.4 = (bf16[4,256,256]{2,1,0:T(8,128)(2,1)}, bf16[4,256,256]{2,1,0:T(8,128)(2,1)}, u32[]{:S(2)}, u32[]{:S(2)}) collective-permute-start(bf16[4,256,256]{2,1,0:T(8,128)(2,1)} %get-tuple-element.6.refs_6_), channel_id=1, source_target_pairs={{0,8},{4,12},{8,16},{12,20},{16,24},{20,28},{24,0},{28,4},{1,9},{5... | collective-permute-start | bytes 1572872 | tf_op jit(solution)/shard_map/ppermute | solution.py:18
  59.5 27.1 %collective-permute-start.10 = (bf16[4,256,256]{2,1,0:T(8,128)(2,1)}, bf16[4,256,256]{2,1,0:T(8,128)(2,1)}, u32[]{:S(2)}, u32[]{:S(2)}) collective-permute-start(bf16[4,256,256]{2,1,0:T(8,128)(2,1)} %get-tuple-element.7.refs_8_), channel_id=1, source_target_pairs={{0,8},{4,12},{8,16},{12,20},{16,24},{20,28},{24,0},{28,4},{1,9},{5... | collective-permute-start | bytes 1572872 | tf_op jit(solution)/shard_map/ppermute | solution.py:18
  59.8 38.1 %collective-permute-start.8 = (bf16[4,256,256]{2,1,0:T(8,128)(2,1)}, bf16[4,256,256]{2,1,0:T(8,128)(2,1)}, u32[]{:S(2)}, u32[]{:S(2)}) collective-permute-start(bf16[4,256,256]{2,1,0:T(8,128)(2,1)} %get-tuple-element.5.refs_7_), channel_id=1, source_target_pairs={{0,8},{4,12},{8,16},{12,20},{16,24},{20,28},{24,0},{28,4},{1,9},{5... | collective-permute-start | bytes 1572872 | tf_op jit(solution)/shard_map/ppermute | solution.py:18
  75.4 31.7 %collective-permute-start.6 = (bf16[4,256,256]{2,1,0:T(8,128)(2,1)}, bf16[4,256,256]{2,1,0:T(8,128)(2,1)S(1)}, u32[]{:S(2)}, u32[]{:S(2)}) collective-permute-start(bf16[4,256,256]{2,1,0:T(8,128)(2,1)} %collective-permute-done.4.refs_10_), channel_id=1, source_target_pairs={{0,8},{4,12},{8,16},{12,20},{16,24},{20,28},{24,0},{28,4},{1,9},{5... | collective-permute-start | bytes 1572872 | tf_op jit(solution)/shard_map/ppermute | solution.py:18
  86.6 23.7 %collective-permute-start.1 = (bf16[3,2,256,256]{3,2,1,0:T(8,128)(2,1)}, bf16[3,2,256,256]{3,2,1,0:T(8,128)(2,1)S(1)}, u32[]{:S(2)}, u32[]{:S(2)}) collective-permute-start(bf16[3,2,256,256]{3,2,1,0:T(8,128)(2,1)} %bitcast.1.refs_0_), channel_id=1, source_target_pairs={{0,1},{1,0},{2,3},{3,2},{4,5},{5,4},{6,7},{7,6},{8,9},{9,8},{10,11... | collective-permute-start | bytes 2359304 | tf_op jit(solution)/shard_map/ppermute | solution.py:18
  86.6 25.4 %collective-permute-start.2 = (bf16[3,2,256,256]{3,2,1,0:T(8,128)(2,1)}, bf16[3,2,256,256]{3,2,1,0:T(8,128)(2,1)S(1)}, u32[]{:S(2)}, u32[]{:S(2)}) collective-permute-start(bf16[3,2,256,256]{3,2,1,0:T(8,128)(2,1)} %collective-permute-done.refs_1_), channel_id=1, source_target_pairs={{0,1},{1,0},{2,3},{3,2},{4,5},{5,4},{6,7},{7,6},{8,9},{9,8},{10,11... | collective-permute-start | bytes 2359304 | tf_op jit(solution)/shard_map/ppermute | solution.py:18
  97.9 12.0 %collective-permute-start.11 = (bf16[4,256,256]{2,1,0:T(8,128)(2,1)S(1)}, bf16[4,256,256]{2,1,0:T(8,128)(2,1)S(1)}, u32[]{:S(2)}, u32[]{:S(2)}) collective-permute-start(bf16[4,256,256]{2,1,0:T(8,128)(2,1)S(1)} %broadcast_select_fusion), channel_id=1, source_target_pairs={{0,4},{4,0},{8,12},{12,8},{16,20},{20,16},{24,28},{28,24},{1,5},{5... | collective-permute-start | bytes 1572872 | tf_op jit(solution)/shard_map/ppermute | solution.py:23
  107.1 16.0 %collective-permute-start.9 = (bf16[4,256,256]{2,1,0:T(8,128)(2,1)S(1)}, bf16[4,256,256]{2,1,0:T(8,128)(2,1)S(1)}, u32[]{:S(2)}, u32[]{:S(2)}) collective-permute-start(bf16[4,256,256]{2,1,0:T(8,128)(2,1)S(1)} %broadcast_select_fusion.1), channel_id=1, source_target_pairs={{0,4},{4,0},{8,12},{12,8},{16,20},{20,16},{24,28},{28,24},{1,5},{5... | collective-permute-start | bytes 1572872 | tf_op jit(solution)/shard_map/ppermute | solution.py:23
  109.9 2.1 %copy-start.4 = (bf16[4,256,256]{2,1,0:T(8,128)(2,1)}, bf16[4,256,256]{2,1,0:T(8,128)(2,1)S(1)}, u32[]{:S(2)}) copy-start(bf16[4,256,256]{2,1,0:T(8,128)(2,1)S(1)} %collective-permute-done.11.refs_6_) | copy-start | bytes 1572868
  109.9 23.3 %collective-permute-start.5 = (bf16[4,256,256]{2,1,0:T(8,128)(2,1)S(1)}, bf16[4,256,256]{2,1,0:T(8,128)(2,1)S(1)}, u32[]{:S(2)}, u32[]{:S(2)}) collective-permute-start(bf16[4,256,256]{2,1,0:T(8,128)(2,1)S(1)} %get-tuple-element.9), channel_id=1, source_target_pairs={{0,4},{4,0},{8,12},{12,8},{16,20},{20,16},{24,28},{28,24},{1,5},{5... | collective-permute-start | bytes 1572872 | tf_op jit(solution)/shard_map/ppermute | solution.py:23
  110.4 1.6 copy-start.2
  110.4 31.4 %collective-permute-start.7 = (bf16[4,256,256]{2,1,0:T(8,128)(2,1)S(1)}, bf16[4,256,256]{2,1,0:T(8,128)(2,1)}, u32[]{:S(2)}, u32[]{:S(2)}) collective-permute-start(bf16[4,256,256]{2,1,0:T(8,128)(2,1)S(1)} %get-tuple-element.8), channel_id=1, source_target_pairs={{0,4},{4,0},{8,12},{12,8},{16,20},{20,16},{24,28},{28,24},{1,5},{5... | collective-permute-start | bytes 1572872 | tf_op jit(solution)/shard_map/ppermute | solution.py:23
  112.0 0.9 copy-start.3
  112.9 1.6 copy-start.1
  123.1 0.8 copy-start.5
  132.8 22.9 %copy-start.6 = (f32[32,16]{1,0:T(8,128)S(1)}, f32[32,16]{1,0:T(8,128)}, u32[]{:S(2)}) copy-start(f32[32,16]{1,0:T(8,128)} %shard_map.58) | copy-start | bytes 6148
  132.8 22.9 %copy-start.7 = (f32[32,16]{1,0:T(8,128)S(1)}, f32[32,16]{1,0:T(8,128)}, u32[]{:S(2)}) copy-start(f32[32,16]{1,0:T(8,128)} %shard_map.57) | copy-start | bytes 6148
  132.8 31.4 %copy-start.9 = (s32[64]{0:T(128)S(1)}, s32[64]{0:T(128)}, u32[]{:S(2)}) copy-start(s32[64]{0:T(128)} %param.8) | copy-start | bytes 772
  133.2 8.6 %copy-start.8 = (bf16[4,256,256]{2,1,0:T(8,128)(2,1)}, bf16[4,256,256]{2,1,0:T(8,128)(2,1)S(1)}, u32[]{:S(2)}) copy-start(bf16[4,256,256]{2,1,0:T(8,128)(2,1)S(1)} %collective-permute-done.5.refs_9_) | copy-start | bytes 1572868
  156.4 3.7 %collective-permute-start.12 = (f32[32,16]{1,0:T(8,128)S(1)}, f32[32,16]{1,0:T(8,128)S(1)}, u32[]{:S(2)}, u32[]{:S(2)}) collective-permute-start(f32[32,16]{1,0:T(8,128)S(1)} %add_add_fusion), channel_id=1, source_target_pairs={{0,4},{4,0},{8,12},{12,8},{16,20},{20,16},{24,28},{28,24},{1,5},{5... | collective-permute-start | bytes 6152 | tf_op jit(solution)/shard_map/ppermute | solution.py:226
  160.1 3.7 %collective-permute-start.13 = (f32[32,16]{1,0:T(8,128)S(1)}, f32[32,16]{1,0:T(8,128)S(1)}, u32[]{:S(2)}, u32[]{:S(2)}) collective-permute-start(f32[32,16]{1,0:T(8,128)S(1)} %add.49), channel_id=1, source_target_pairs={{0,8},{4,12},{8,0},{12,4},{16,24},{20,28},{24,16},{28,20},{1,9},{5... | collective-permute-start | bytes 6152 | tf_op jit(solution)/shard_map/ppermute | solution.py:226
  163.9 4.6 %collective-permute-start.14 = (f32[32,16]{1,0:T(8,128)S(1)}, f32[32,16]{1,0:T(8,128)S(1)}, u32[]{:S(2)}, u32[]{:S(2)}) collective-permute-start(f32[32,16]{1,0:T(8,128)S(1)} %add.50), channel_id=1, source_target_pairs={{0,16},{4,20},{8,24},{12,28},{16,0},{20,4},{24,8},{28,12},{1,17},{... | collective-permute-start | bytes 6152 | tf_op jit(solution)/shard_map/ppermute | solution.py:226

commit v2 on v1

v2 whole, which is shorter than its diff:
```python
import functools
import math

import jax
import jax.numpy as jnp
from jax import lax
from jax.experimental import pallas as pl
from jax.experimental.pallas import tpu as pltpu
from jax.sharding import PartitionSpec as P

BLK = 16
VMEM = pl.BlockSpec(memory_space=pltpu.VMEM)


def shifted(value, axis, steps):
    count = lax.axis_size(axis)
    pairs = [(source, (source + steps) % count) for source in range(count)]
    return lax.ppermute(value, axis, pairs)


def crossed(value, axis, mask):
    count = lax.axis_size(axis)
    return lax.ppermute(value, axis, [(source, source ^ mask) for source in range(count)])


def sent(value, steps, parity=None):
    count = lax.axis_size("src")
    sources = [at for at in range(count) if parity is None or at % 2 == parity]
    return lax.ppermute(value, "src", [(at, (at + steps) % count) for at in sources])


def after(value, *first):
    return lax.optimization_barrier((value, *first))[0]


def shear_kernel(peramb_ref, out_ref):
    source_count, sep_local = peramb_ref.shape[:2]
    n_src, own, seps = out_ref.shape[:3]
    first = lax.axis_index("mom") * seps
    sep0 = lax.axis_index("snk") * sep_local + first
    for d in range(n_src):
        for j in range(own):
            for h in range(seps):
                start = lax.rem(own * d + j - h - sep0 + 2 * source_count, source_count)
                out_ref[d, j, h] = peramb_ref[start, first + h]


def shear(peramb, n_src, own, seps):
    return pl.pallas_call(
        shear_kernel,
        out_shape=jax.ShapeDtypeStruct((n_src, own, seps) + peramb.shape[2:], peramb.dtype),
        in_specs=[VMEM],
        out_specs=VMEM,
        compiler_params=pltpu.CompilerParams(vmem_limit_bytes=16 << 20),
    )(peramb)


def ordered_kernel(parts, *refs):
    *p_in, out_ref = refs
    n_snk, n_mom = lax.axis_size("snk"), lax.axis_size("mom")
    y, m = lax.axis_index("snk"), lax.axis_index("mom")
    own, seps = p_in[0].shape[:2]
    for part, (dy, dm) in zip(p_in, parts):
        at = (lax.rem(y + dy, n_snk) * n_mom + lax.rem(m + dm, n_mom)) * seps
        for j in range(own):
            for h in range(seps):
                out_ref[j, at + h] = part[j, h]


def ordered(perms):
    own, seps, nv = next(iter(perms.values())).shape[:3]
    return pl.pallas_call(
        functools.partial(ordered_kernel, tuple(perms)),
        out_shape=jax.ShapeDtypeStruct((own, seps * len(perms), nv, nv), jnp.bfloat16),
        in_specs=[VMEM] * len(perms),
        out_specs=VMEM,
        compiler_params=pltpu.CompilerParams(vmem_limit_bytes=8 << 20),
    )(*perms.values())


def trace_kernel(units, has_before, elem_parts, slice_parts, last, *refs):
    refs = list(refs)
    before_ref = refs.pop(0) if has_before else None
    p_ref = refs.pop(0)
    s_refs = [refs.pop(0) for _ in range(elem_parts)]
    e_refs = [[refs.pop(0) for _ in range(parts)] for parts in slice_parts]
    out_ref, w_ref, *rest = refs
    acc_ref = rest.pop(0) if last else out_ref
    own, n_sep, nv = p_ref.shape[:3]
    ne_part = s_refs[0].shape[1]
    ne = ne_part * elem_parts
    nf = w_ref.shape[1]
    even = lax.rem(lax.axis_index("src"), 2) == 0
    for c, parts in enumerate(e_refs):
        if len(parts) == 2:
            one, two = parts

            @pl.when(jnp.logical_not(even))
            def _():
                one[...] = two[...]

    for n, (c, j, ts) in enumerate(units):
        prop = p_ref[j, ts]
        for f in range(nf):
            half = jnp.dot(prop, e_refs[c][0][f], preferred_element_type=jnp.float32)
            sandwich = lax.dot_general(
                half.astype(jnp.bfloat16),
                prop,
                (((1,), (1,)), ((), ())),
                preferred_element_type=jnp.float32,
            )
            w_ref[n, f] = sandwich.astype(jnp.bfloat16)

    if has_before:
        acc_ref[...] = before_ref[...]
    else:
        acc_ref[...] = jnp.zeros_like(acc_ref)
    width = nf * BLK
    for j in range(own):
        group = [(n, ts) for n, (_, jj, ts) in enumerate(units) if jj == j]
        if not group:
            continue
        left = jnp.concatenate(
            [
                jnp.concatenate(
                    [w_ref[n, :, a : a + BLK, :].reshape(width, nv) for n, _ in group], axis=0
                )
                for a in range(0, nv, BLK)
            ],
            axis=1,
        )
        right = jnp.concatenate(
            [
                jnp.concatenate(
                    [ref[j, :, a : a + BLK, :].reshape(ne_part * BLK, nv) for ref in s_refs], axis=0
                )
                for a in range(0, nv, BLK)
            ],
            axis=1,
        )
        part = lax.dot_general(
            left, right, (((1,), (1,)), ((), ())), preferred_element_type=jnp.float32
        )
        for at, (_, ts) in enumerate(group):
            acc_ref[ts * width : (ts + 1) * width] += part[at * width : (at + 1) * width]
    if not last:
        return
    total = acc_ref[...]
    row = lax.broadcasted_iota(jnp.int32, total.shape, 0)
    col = lax.broadcasted_iota(jnp.int32, total.shape, 1)
    kept = jnp.where((row & (BLK - 1)) == (col & (BLK - 1)), total, 0.0)
    kept = jnp.sum(kept.reshape(n_sep * nf, BLK, ne * BLK), axis=1)
    picked = lax.broadcasted_iota(jnp.int32, (ne * BLK, ne), 0)
    elem = lax.broadcasted_iota(jnp.int32, (ne * BLK, ne), 1)
    group_sum = jnp.where((picked >> (BLK.bit_length() - 1)) == elem, 1.0, 0.0).astype(jnp.float32)
    out_ref[...] = jnp.dot(
        kept, group_sum, precision=lax.Precision.HIGHEST, preferred_element_type=jnp.float32
    )


def add_traces(before, units, slices, perm, elems, last):
    own, n_sep, nv = perm.shape[:3]
    nf = slices[0][0].shape[0]
    ne = elems[0].shape[1] * len(elems)
    flops = 2 * len(units) * nf * nv * nv * (2 * nv + ne * BLK)
    moved = 2 * nv * nv * (own * n_sep + own * ne + len(slices) * nf)
    slice_parts = [len(parts) for parts in slices]
    flat = [part for parts in slices for part in parts]
    acc = (n_sep * nf * BLK, ne * BLK)
    before = [] if before is None else [before]
    scratch = [pltpu.VMEM((len(units), nf, nv, nv), jnp.bfloat16)]
    if last:
        scratch.append(pltpu.VMEM(acc, jnp.float32))
    return pl.pallas_call(
        functools.partial(trace_kernel, units, bool(before), len(elems), slice_parts, last),
        out_shape=jax.ShapeDtypeStruct((n_sep * nf, ne) if last else acc, jnp.float32),
        in_specs=[VMEM] * (len(before) + 1 + len(elems) + len(flat)),
        out_specs=VMEM,
        scratch_shapes=scratch,
        compiler_params=pltpu.CompilerParams(vmem_limit_bytes=24 << 20),
        cost_estimate=pl.CostEstimate(flops=flops, bytes_accessed=moved, transcendentals=0),
    )(*before, perm, *elems, *flat)


def body(peramb, elem_src, elem_snk, op_elem, hlt_kernel):
    source_count, sep_local, rows, nv = peramb.shape
    n_src, n_snk, n_mom = (lax.axis_size(axis) for axis in ("src", "snk", "mom"))
    s, y, m = (lax.axis_index(axis) for axis in ("src", "snk", "mom"))
    n_sep = sep_local * n_snk
    seps = sep_local // n_mom
    own, ne_part = elem_snk.shape[:2]
    nf = ne_part // n_snk
    highest = lax.Precision.HIGHEST

    def needed(block, i):
        return [(j, own * block + j - i) for j in range(own) if 0 <= own * block + j - i < n_sep]

    reach = -(-(n_sep - 1) // own)
    quarter = lax.dynamic_slice_in_dim(elem_src, y * nf, nf, 1)
    start = [quarter[i] for i in range(own)]
    peramb, *start = lax.optimization_barrier((peramb, *start))
    behind = crossed(start[0], "src", 1)
    sheared = shear(peramb, n_src, own, seps)
    rows_in = lax.all_to_all(sheared, "src", 0, 0)
    start = [after(value, rows_in) for value in start]
    mine = jnp.transpose(rows_in, (1, 2, 0, 3, 4)).reshape(own, seps, n_src * rows, nv)
    blocks = {}
    done = {}
    for i in reversed(range(own)):
        last = max(block for block in range(reach + 1) if needed(block, i))
        chain = [start[i]]
        value = after(start[i], done[i + 2]) if i + 2 in done else start[i]
        while 2 * len(chain) <= last + (1 if i else 0):
            value = sent(value, 2, 1 if 2 * len(chain) > last else None)
            chain.append(value)
        done[i] = chain[1]
        for hop, value in enumerate(chain[: last // 2 + 1]):
            blocks[2 * hop, i] = (value,)
        if i:
            for block in range(1, last + 1, 2):
                low, high = chain[block // 2], chain[block // 2 + 1]
                blocks[block, i] = (sent(high, -1, 1), sent(low, 1, 0))
        else:
            lower = behind
            for block in range(1, last + 1, 2):
                value = after(lower, done[1]) if lower is behind and 1 in done else lower
                upper = sent(value, 2, 0 if block + 2 > last else None)
                blocks[block, i] = (upper, lower)
                lower = upper

    perms = {(0, 0): mine}
    for dy in range(1, n_snk):
        perms[dy, 0] = shifted(mine, "snk", -dy)
    for dy in range(n_snk):
        for dm in range(1, n_mom):
            perms[dy, dm] = shifted(perms[dy, 0], "mom", -dm)
    elems = [elem_snk] + [shifted(elem_snk, "mom", -dm) for dm in range(1, n_mom)]

    groups = [[], [], []]
    for block, i in blocks:
        early = block == 0 or (i == own - 1 and block < 3)
        groups[0 if early else 2 if i == 0 or block > 2 else 1].append((block, i))
    perm = ordered(perms)
    total = None
    for group in groups:
        units = [(c, j, ts) for c, (k, i) in enumerate(group) for j, ts in needed(k, i)]
        slices = [blocks[b] for b in group]
        total = add_traces(total, units, slices, perm, elems, group is groups[-1])

    if n_src == 8:
        for step in (1, 2, 4):
            total = total + crossed(total, "src", step)
    else:
        total = lax.psum(total, "src")
    gathered = lax.all_gather(total, "snk", axis=0)
    pair_traces = gathered.reshape(n_snk, n_sep, nf, ne_part * n_mom)
    n_ops = op_elem.shape[0] // n_src
    ops = lax.dynamic_slice_in_dim(op_elem, s * n_ops, n_ops, 0)
    names = (jnp.arange(n_mom * ne_part, dtype=jnp.int32) + m * ne_part) % (n_mom * ne_part)
    onehot = (ops[:, None] == names[None, :]).astype(jnp.float32)
    norm_factor = 1.0 / (nv * math.sqrt(source_count))
    correlator = jnp.einsum("oe,ytfe->otyf", onehot, pair_traces, precision=highest) * norm_factor
    correlator = correlator.reshape(n_ops, n_sep, ne_part)
    return jnp.einsum("otf,tk->ofk", correlator, hlt_kernel, precision=highest)


def solution(mesh):
    placed = (
        P(None, "snk", "src", None),
        P("src", "mom", None, None),
        P("src", "mom", None, None),
        P(),
        P(),
    )
    return jax.shard_map(
        body, mesh=mesh, in_specs=placed, out_specs=P("src", "mom", None), check_vma=False
    )
```

time: 174 us -> 122 us (0.70)
  Pallas kernels: 56.6 us -> 15.7 us
  waiting for transfers between devices: 61.4 us -> 44.1 us
  starting transfers between devices: 11.5 us -> 26.5 us
  local copies, waits for them, and re-layouts: 7.13 us -> 2.25 us
  other arithmetic: 4.3 us -> 0.02 us
    ppermute x8 -> x4, waiting for transfers between devices: 42.2 us -> 0.91 us  [shifted(): return lax.ppermute(value, axis, pairs)]
    pallas_call x4 -> x5, Pallas kernels: 56.6 us -> 15.7 us  [the longest x3 15.4 us: add_traces(): pl.pallas_call(functools.partial(trace_kernel, units, bool(before), len(e...]
    ppermute x7 -> x15, waiting for transfers between devices: 19.3 us -> 43.2 us  [the longest x11 21.7 us: sent(): lax.ppermute(value, 'src', [(at, (at + steps) % count) for at in sources])]
    ppermute x7 -> x15, starting transfers between devices: 6.74 us -> 24.4 us  [the longest x11 20.1 us: sent(): lax.ppermute(value, 'src', [(at, (at + steps) % count) for at in sources])]
    select_n x3 -> x0, other arithmetic: 3.55 us -> none  [body(): blocks[block, i] = swapped(jnp.where(even, low, high), 'src')]
    unnamed x21 -> x9, local copies, waits for them, and re-layouts: 3.4 us -> 0.39 us
    ppermute x8 -> x4, starting transfers between devices: 4.79 us -> 2.04 us  [shifted(): return lax.ppermute(value, axis, pairs)]
  transfers between devices with their start and end apart: 15 -> 19, of which waited for: 9 -> 8; matrix products, arithmetic and copies ran while one was open for 4% -> 1% of each run, Pallas kernels for 25% -> 9%
where the time goes in v2:
time: 122 us
  waiting for transfers between devices  44.1 us (36%)
  blocking collectives  31.7 us (26%)
  starting transfers between devices  26.5 us (22%)
  Pallas kernels  15.7 us (13%)
  local copies, waits for them, and re-layouts  2.25 us (2%)
    all_to_all x1, blocking collectives, body(): rows_in = lax.all_to_all(sheared, 'src', 0, 0)  27.4 us
    ppermute x11, waiting for transfers between devices, sent(): lax.ppermute(value, 'src', [(at, (at + steps) % count) for at in sources])  21.7 us
    ppermute x4, waiting for transfers between devices, crossed(): lax.ppermute(value, axis, [(source, source ^ mask) for source in range(co...  21.4 us
    ppermute x11, starting transfers between devices, sent(): lax.ppermute(value, 'src', [(at, (at + steps) % count) for at in sources])  20.1 us
    pallas_call x3, Pallas kernels, add_traces(): pl.pallas_call(functools.partial(trace_kernel, units, bool(before), len(e...  15.4 us
    all_gather x1, blocking collectives, body(): gathered = lax.all_gather(total, 'snk', axis=0)  4.36 us
    ppermute x4, starting transfers between devices, crossed(): lax.ppermute(value, axis, [(source, source ^ mask) for source in range(co...  4.33 us
  transfers between devices with their start and end apart: 19, of which 8 were waited for; matrix products, arithmetic and copies ran while one was open for 1% of the time, Pallas kernels for 9%

profile of v2, /device:TPU:0, one launch (start us, length us, event | category | flops | bytes accessed | tf_op | source)
XLA Modules:
  0.0 121.5 jit_solution(15428256243244069101)
XLA Ops:
  0.0 0.0 copy-start
  0.0 0.5 collective-permute-start.3
  0.5 0.0 copy-start.2
  0.5 1.6 %dynamic-slice_bitcast_fusion = (bf16[4,256,256]{2,1,0:T(8,128)(2,1)S(1)}, bf16[4,256,256]{2,1,0:T(8,128)(2,1)S(1)}, bf16[4,256,256]{2,1,0:T(8,128)(2,1)S(1)}) fusion(bf16[3,8,256,256]{3,2,1,0:T(8,128)(2,1)} %param.6, s32[]{:T(128)S(6)} %add.44, s32[]{:T(128)S(6)} %select_n.17, s32[]{:T(128)S(6)} %add.43), kind=kLoop, calls=%fused_computation.1 | loop fusion | bytes 3145740 | tf_op jit(solution)/shard_map/squeeze | solution.py:200
  2.0 0.3 copy-done.2
  2.3 0.1 shard_map.55
  2.4 27.4 %all_to_all.5 = bf16[8,3,2,32,256]{4,3,2,1,0:T(8,128)(2,1)S(1)} all-to-all(bf16[8,3,2,32,256]{4,3,2,1,0:T(8,128)(2,1)S(1)} %shard_map.55), channel_id=1, replica_groups=mesh['src'=8,'snk'=2,'mom'=2] {'src'}, dimensions={0} | all-to-all | bytes 1572864 | tf_op jit(solution)/shard_map/all_to_all | solution.py:204
  29.8 0.1 copy.12
  29.8 0.0 copy-start.1
  29.8 1.6 %collective-permute-start = (bf16[3,2,256,256]{3,2,1,0:T(8,128)(2,1)S(1)}, bf16[3,2,256,256]{3,2,1,0:T(8,128)(2,1)S(1)}, u32[]{:S(2)}, u32[]{:S(2)}) collective-permute-start(bf16[3,2,256,256]{3,2,1,0:T(8,128)(2,1)S(1)} %bitcast.23), channel_id=1, source_target_pairs={{0,2},{2,0},{1,3},{3,1},{4,6},{6,4},{5,7},{7,5},{8,10},{10,8},{9,1... | collective-permute-start | bytes 2359304 | tf_op jit(solution)/shard_map/ppermute | solution.py:18
  31.4 1.5 %collective-permute-start.14 = (bf16[4,256,256]{2,1,0:T(8,128)(2,1)S(1)}, bf16[4,256,256]{2,1,0:T(8,128)(2,1)S(1)}, u32[]{:S(2)}, u32[]{:S(2)}) collective-permute-start(bf16[4,256,256]{2,1,0:T(8,128)(2,1)S(1)} %get-tuple-element.21.refs_8_), channel_id=1, source_target_pairs={{0,4},{4,0},{8,12},{12,8},{16,20},{20,16},{24,28},{28,24},{1,5},{5... | collective-permute-start | bytes 1572872 | tf_op jit(solution)/shard_map/ppermute | solution.py:23
  32.9 0.0 collective-permute-start.4
  32.9 0.0 collective-permute-start.1
  32.9 11.5 %collective-permute-done.14.refs_8_ = bf16[4,256,256]{2,1,0:T(8,128)(2,1)S(1)} collective-permute-done((bf16[4,256,256]{2,1,0:T(8,128)(2,1)S(1)}, bf16[4,256,256]{2,1,0:T(8,128)(2,1)S(1)}, u32[]{:S(2)}, u32[]{:S(2)}) %collective-permute-start.14) | collective-permute-done | bytes 524320 | tf_op jit(solution)/shard_map/ppermute | solution.py:23
  44.4 3.4 %collective-permute-start.6 = (bf16[4,256,256]{2,1,0:T(8,128)(2,1)S(1)}, bf16[4,256,256]{2,1,0:T(8,128)(2,1)S(1)}, u32[]{:S(2)}, u32[]{:S(2)}) collective-permute-start(bf16[4,256,256]{2,1,0:T(8,128)(2,1)S(1)} %get-tuple-element.16.refs_3_), channel_id=1, source_target_pairs={{0,4},{8,12},{16,20},{24,28},{1,5},{9,13},{17,21},{25,29},{2,6},{1... | collective-permute-start | bytes 1572872 | tf_op jit(solution)/shard_map/ppermute | solution.py:29
  47.8 0.0 collective-permute-done.4.refs_4_
  47.8 0.1 collective-permute-start.7
  47.9 0.9 collective-permute-done.refs_1_
  48.8 0.0 collective-permute-start.2
  48.8 8.5 %collective-permute-done.6.refs_6_ = bf16[4,256,256]{2,1,0:T(8,128)(2,1)S(1)} collective-permute-done((bf16[4,256,256]{2,1,0:T(8,128)(2,1)S(1)}, bf16[4,256,256]{2,1,0:T(8,128)(2,1)S(1)}, u32[]{:S(2)}, u32[]{:S(2)}) %collective-permute-start.6) | collective-permute-done | bytes 524320 | tf_op jit(solution)/shard_map/ppermute | solution.py:29
  57.3 4.4 %collective-permute-start.9 = (bf16[4,256,256]{2,1,0:T(8,128)(2,1)S(1)}, bf16[4,256,256]{2,1,0:T(8,128)(2,1)S(1)}, u32[]{:S(2)}, u32[]{:S(2)}) collective-permute-start(bf16[4,256,256]{2,1,0:T(8,128)(2,1)S(1)} %get-tuple-element.18.refs_7_), channel_id=1, source_target_pairs={{0,4},{8,12},{16,20},{24,28},{1,5},{9,13},{17,21},{25,29},{2,6},{1... | collective-permute-start | bytes 1572872 | tf_op jit(solution)/shard_map/ppermute | solution.py:29
  61.7 0.0 collective-permute-done.7.refs_4_
  61.7 1.3 %collective-permute-start.5 = (bf16[4,256,256]{2,1,0:T(8,128)(2,1)S(1)}, bf16[4,256,256]{2,1,0:T(8,128)(2,1)S(1)}, u32[]{:S(2)}, u32[]{:S(2)}) collective-permute-start(bf16[4,256,256]{2,1,0:T(8,128)(2,1)S(1)} %collective-permute-done.4.refs_4_), channel_id=1, source_target_pairs={{4,0},{12,8},{20,16},{28,24},{5,1},{13,9},{21,17},{29,25},{6,2},{1... | collective-permute-start | bytes 1572872 | tf_op jit(solution)/shard_map/ppermute | solution.py:29
  63.0 0.0 collective-permute-done.1.refs_2_
  63.0 0.7 collective-permute-start.10
  63.7 0.0 collective-permute-done.2.refs_3_
  63.7 1.3 %collective-permute-start.8 = (bf16[4,256,256]{2,1,0:T(8,128)(2,1)S(1)}, bf16[4,256,256]{2,1,0:T(8,128)(2,1)S(1)}, u32[]{:S(2)}, u32[]{:S(2)}) collective-permute-start(bf16[4,256,256]{2,1,0:T(8,128)(2,1)S(1)} %collective-permute-done.7.refs_4_), channel_id=1, source_target_pairs={{4,0},{12,8},{20,16},{28,24},{5,1},{13,9},{21,17},{29,25},{6,2},{1... | collective-permute-start | bytes 1572872 | tf_op jit(solution)/shard_map/ppermute | solution.py:29
  65.0 0.2 shard_map.56.refs_0_.refs_1_
  65.2 5.0 %collective-permute-done.9.refs_6_ = bf16[4,256,256]{2,1,0:T(8,128)(2,1)S(1)} collective-permute-done((bf16[4,256,256]{2,1,0:T(8,128)(2,1)S(1)}, bf16[4,256,256]{2,1,0:T(8,128)(2,1)S(1)}, u32[]{:S(2)}, u32[]{:S(2)}) %collective-permute-start.9) | collective-permute-done | bytes 524320 | tf_op jit(solution)/shard_map/ppermute | solution.py:29
  70.3 0.0 collective-permute-start.13
  70.3 8.2 %collective-permute-done.5.refs_5_ = bf16[4,256,256]{2,1,0:T(8,128)(2,1)S(1)} collective-permute-done((bf16[4,256,256]{2,1,0:T(8,128)(2,1)S(1)}, bf16[4,256,256]{2,1,0:T(8,128)(2,1)S(1)}, u32[]{:S(2)}, u32[]{:S(2)}) %collective-permute-start.5) | collective-permute-done | bytes 524320 | tf_op jit(solution)/shard_map/ppermute | solution.py:29
  78.4 1.9 %collective-permute-start.15 = (bf16[4,256,256]{2,1,0:T(8,128)(2,1)S(1)}, bf16[4,256,256]{2,1,0:T(8,128)(2,1)S(1)}, u32[]{:S(2)}, u32[]{:S(2)}) collective-permute-start(bf16[4,256,256]{2,1,0:T(8,128)(2,1)S(1)} %collective-permute-done.14.refs_8_), channel_id=1, source_target_pairs={{0,8},{8,16},{16,24},{24,0},{1,9},{9,17},{17,25},{25,1},{2,10},{10... | collective-permute-start | bytes 1572872 | tf_op jit(solution)/shard_map/ppermute | solution.py:29
  80.4 0.0 collective-permute-done.10
  80.4 5.8 %collective-permute-start.12 = (bf16[4,256,256]{2,1,0:T(8,128)(2,1)S(1)}, bf16[4,256,256]{2,1,0:T(8,128)(2,1)S(1)}, u32[]{:S(2)}, u32[]{:S(2)}) collective-permute-start(bf16[4,256,256]{2,1,0:T(8,128)(2,1)S(1)} %collective-permute-done.4.refs_4_), channel_id=1, source_target_pairs={{0,4},{8,12},{16,20},{24,28},{1,5},{9,13},{17,21},{25,29},{2,6},{1... | collective-permute-start | bytes 1572872 | tf_op jit(solution)/shard_map/ppermute | solution.py:29
  86.2 0.0 collective-permute-done.3.refs_2_.refs_3_
  86.2 1.3 %collective-permute-start.11 = (bf16[4,256,256]{2,1,0:T(8,128)(2,1)S(1)}, bf16[4,256,256]{2,1,0:T(8,128)(2,1)S(1)}, u32[]{:S(2)}, u32[]{:S(2)}) collective-permute-start(bf16[4,256,256]{2,1,0:T(8,128)(2,1)S(1)} %collective-permute-done.10), channel_id=1, source_target_pairs={{4,0},{12,8},{20,16},{28,24},{5,1},{13,9},{21,17},{29,25},{6,2},{1... | collective-permute-start | bytes 1572872 | tf_op jit(solution)/shard_map/ppermute | solution.py:29
  87.5 0.0 copy-done.1
  87.5 6.0 %shard_map.57.refs_0_ = f32[512,256]{1,0:T(8,128)S(1)} custom-call(bf16[3,8,256,256]{3,2,1,0:T(8,128)(2,1)S(1)} %shard_map.56.refs_0_.refs_1_, bf16[3,8,256,256]{3,2,1,0:T(8,128)(2,1)S(1)} %copy-done.1, bf16[3,8,256,256]{3,2,1,0:T(8,128)(2,1)S(1)} %collective-permute-done.3.refs_2_.refs_3_, bf16[4,256,256]{2,1,0:T(8,128)(2,1)S(1)} %get-tuple-element.16.refs_3_, ...), custom_call_target="tpu_custom_call" | custom-call | flops 4831838208 | bytes 12058624 | tf_op jit(solution)/shard_map/pallas_call | solution.py:174
  93.5 0.0 collective-permute-done.8.refs_5_
  93.5 4.5 %shard_map.58.refs_0_ = f32[512,256]{1,0:T(8,128)S(1)} custom-call(f32[512,256]{1,0:T(8,128)S(1)} %shard_map.57.refs_0_, bf16[3,8,256,256]{3,2,1,0:T(8,128)(2,1)S(1)} %shard_map.56.refs_0_.refs_1_, bf16[3,8,256,256]{3,2,1,0:T(8,128)(2,1)S(1)} %copy-done.1, bf16[3,8,256,256]{3,2,1,0:T(8,128)(2,1)S(1)} %collective-permute-done.3.refs_2_.refs_3_, ...), custom_call_target="tpu_custom_call" | custom-call | flops 2415919104 | bytes 10485760 | tf_op jit(solution)/shard_map/pallas_call | solution.py:174
  98.1 0.0 copy-start.3
  98.1 0.0 collective-permute-done.13.refs_6_
  98.1 0.0 collective-permute-done.15.refs_7_
  98.1 0.0 collective-permute-done.12.refs_5_
  98.1 0.0 collective-permute-done.11.refs_4_
  98.2 4.8 %shard_map.59 = f32[32,16]{1,0:T(8,128)S(1)} custom-call(f32[512,256]{1,0:T(8,128)S(1)} %shard_map.58.refs_0_, bf16[3,8,256,256]{3,2,1,0:T(8,128)(2,1)S(1)} %shard_map.56.refs_0_.refs_1_, bf16[3,8,256,256]{3,2,1,0:T(8,128)(2,1)S(1)} %copy-done.1, bf16[3,8,256,256]{3,2,1,0:T(8,128)(2,1)S(1)} %collective-permute-done.3.refs_2_.refs_3_, ...), custom_call_target="tpu_custom_call" | custom-call | flops 2415919104 | bytes 11010048 | tf_op jit(solution)/shard_map/pallas_call | solution.py:174
  103.0 2.9 %collective-permute-start.16 = (f32[32,16]{1,0:T(8,128)S(1)}, f32[32,16]{1,0:T(8,128)S(1)}, u32[]{:S(2)}, u32[]{:S(2)}) collective-permute-start(f32[32,16]{1,0:T(8,128)S(1)} %shard_map.59), channel_id=1, source_target_pairs={{0,4},{4,0},{8,12},{12,8},{16,20},{20,16},{24,28},{28,24},{1,5},{5... | collective-permute-start | bytes 6152 | tf_op jit(solution)/shard_map/ppermute | solution.py:23
  105.8 1.7 %collective-permute-done.16 = f32[32,16]{1,0:T(8,128)S(1)} collective-permute-done((f32[32,16]{1,0:T(8,128)S(1)}, f32[32,16]{1,0:T(8,128)S(1)}, u32[]{:S(2)}, u32[]{:S(2)}) %collective-permute-start.16) | collective-permute-done | bytes 2080 | tf_op jit(solution)/shard_map/ppermute | solution.py:23
  107.6 0.0 collective-permute-start.17
  107.6 3.7 %collective-permute-done.17 = f32[32,16]{1,0:T(8,128)S(1)} collective-permute-done((f32[32,16]{1,0:T(8,128)S(1)}, f32[32,16]{1,0:T(8,128)S(1)}, u32[]{:S(2)}, u32[]{:S(2)}) %collective-permute-start.17) | collective-permute-done | bytes 2080 | tf_op jit(solution)/shard_map/ppermute | solution.py:23
  111.3 0.0 collective-permute-start.18
  111.3 0.0 copy-done.3
  111.3 0.1 dynamic_slice.7
  111.4 4.5 %collective-permute-done.18 = f32[32,16]{1,0:T(8,128)S(1)} collective-permute-done((f32[32,16]{1,0:T(8,128)S(1)}, f32[32,16]{1,0:T(8,128)S(1)}, u32[]{:S(2)}, u32[]{:S(2)}) %collective-permute-start.18) | collective-permute-done | bytes 2080 | tf_op jit(solution)/shard_map/ppermute | solution.py:23
  115.9 0.1 copy.13
  116.0 4.4 %all-gather.1 = f32[2,32,16]{1,2,0:T(8,128)S(1)} all-gather(f32[1,32,16]{1,2,0:T(8,128)S(1)} %copy.13), channel_id=2, replica_groups=mesh['src'=8,'snk'=2,'mom'=2] {'snk'}, dimensions={0}, use_global_device_ids=true | all-gather | bytes 6144 | tf_op jit(solution)/shard_map/all_gather | solution.py:255
  120.4 0.1 copy.14
  120.4 0.2 convolution_multiply_fusion
  120.7 0.1 copy.16
  120.7 0.0 copy-done
  120.7 0.8 fusion.1
  (4 shorter events, 0.0 us)
Async XLA Ops:
  0.0 120.7 %copy-start = (f32[8,128]{1,0:T(8,128)S(1)}, f32[8,128]{1,0:T(8,128)}, u32[]{:S(2)}) copy-start(f32[8,128]{1,0:T(8,128)} %param.9) | copy-start | bytes 12292
  0.0 86.2 %collective-permute-start.3 = (bf16[3,8,256,256]{3,2,1,0:T(8,128)(2,1)}, bf16[3,8,256,256]{3,2,1,0:T(8,128)(2,1)S(1)}, u32[]{:S(2)}, u32[]{:S(2)}) collective-permute-start(bf16[3,8,256,256]{3,2,1,0:T(8,128)(2,1)} %refs_2_.3), channel_id=1, source_target_pairs={{0,1},{1,0},{2,3},{3,2},{4,5},{5,4},{6,7},{7,6},{8,9},{9,8},{10,11... | collective-permute-start | bytes 9437192 | tf_op jit(solution)/shard_map/ppermute | solution.py:18
  0.5 1.9 %copy-start.2 = (bf16[24,4,32,256]{3,2,1,0:T(8,128)(2,1)S(1)}, bf16[24,4,32,256]{3,2,1,0:T(8,128)(2,1)}, u32[]{:S(2)}) copy-start(bf16[24,4,32,256]{3,2,1,0:T(8,128)(2,1)} %peramb_ref) | copy-start | bytes 4718596
  29.8 57.6 %copy-start.1 = (bf16[3,8,256,256]{3,2,1,0:T(8,128)(2,1)S(1)}, bf16[3,8,256,256]{3,2,1,0:T(8,128)(2,1)}, u32[]{:S(2)}) copy-start(bf16[3,8,256,256]{3,2,1,0:T(8,128)(2,1)} %refs_2_.3) | copy-start | bytes 9437188
  29.8 18.9 %collective-permute-start = (bf16[3,2,256,256]{3,2,1,0:T(8,128)(2,1)S(1)}, bf16[3,2,256,256]{3,2,1,0:T(8,128)(2,1)S(1)}, u32[]{:S(2)}, u32[]{:S(2)}) collective-permute-start(bf16[3,2,256,256]{3,2,1,0:T(8,128)(2,1)S(1)} %bitcast.23), channel_id=1, source_target_pairs={{0,2},{2,0},{1,3},{3,1},{4,6},{6,4},{5,7},{7,5},{8,10},{10,8},{9,1... | collective-permute-start | bytes 2359304 | tf_op jit(solution)/shard_map/ppermute | solution.py:18
  31.4 12.9 %collective-permute-start.14 = (bf16[4,256,256]{2,1,0:T(8,128)(2,1)S(1)}, bf16[4,256,256]{2,1,0:T(8,128)(2,1)S(1)}, u32[]{:S(2)}, u32[]{:S(2)}) collective-permute-start(bf16[4,256,256]{2,1,0:T(8,128)(2,1)S(1)} %get-tuple-element.21.refs_8_), channel_id=1, source_target_pairs={{0,4},{4,0},{8,12},{12,8},{16,20},{20,16},{24,28},{28,24},{1,5},{5... | collective-permute-start | bytes 1572872 | tf_op jit(solution)/shard_map/ppermute | solution.py:23
  32.9 14.9 %collective-permute-start.4 = (bf16[4,256,256]{2,1,0:T(8,128)(2,1)S(1)}, bf16[4,256,256]{2,1,0:T(8,128)(2,1)S(1)}, u32[]{:S(2)}, u32[]{:S(2)}) collective-permute-start(bf16[4,256,256]{2,1,0:T(8,128)(2,1)S(1)} %get-tuple-element.16.refs_3_), channel_id=1, source_target_pairs={{0,8},{4,12},{8,16},{12,20},{16,24},{20,28},{24,0},{28,4},{1,9},{5... | collective-permute-start | bytes 1572872 | tf_op jit(solution)/shard_map/ppermute | solution.py:29
  32.9 30.1 %collective-permute-start.1 = (bf16[3,2,256,256]{3,2,1,0:T(8,128)(2,1)S(1)}, bf16[3,2,256,256]{3,2,1,0:T(8,128)(2,1)S(1)}, u32[]{:S(2)}, u32[]{:S(2)}) collective-permute-start(bf16[3,2,256,256]{3,2,1,0:T(8,128)(2,1)S(1)} %bitcast.24), channel_id=1, source_target_pairs={{0,1},{1,0},{2,3},{3,2},{4,5},{5,4},{6,7},{7,6},{8,9},{9,8},{10,11... | collective-permute-start | bytes 2359304 | tf_op jit(solution)/shard_map/ppermute | solution.py:18
  44.4 12.9 %collective-permute-start.6 = (bf16[4,256,256]{2,1,0:T(8,128)(2,1)S(1)}, bf16[4,256,256]{2,1,0:T(8,128)(2,1)S(1)}, u32[]{:S(2)}, u32[]{:S(2)}) collective-permute-start(bf16[4,256,256]{2,1,0:T(8,128)(2,1)S(1)} %get-tuple-element.16.refs_3_), channel_id=1, source_target_pairs={{0,4},{8,12},{16,20},{24,28},{1,5},{9,13},{17,21},{25,29},{2,6},{1... | collective-permute-start | bytes 1572872 | tf_op jit(solution)/shard_map/ppermute | solution.py:29
  47.8 13.9 %collective-permute-start.7 = (bf16[4,256,256]{2,1,0:T(8,128)(2,1)S(1)}, bf16[4,256,256]{2,1,0:T(8,128)(2,1)S(1)}, u32[]{:S(2)}, u32[]{:S(2)}) collective-permute-start(bf16[4,256,256]{2,1,0:T(8,128)(2,1)S(1)} %get-tuple-element.18.refs_7_), channel_id=1, source_target_pairs={{0,8},{4,12},{8,16},{12,20},{16,24},{20,28},{24,0},{28,4},{1,9},{5... | collective-permute-start | bytes 1572872 | tf_op jit(solution)/shard_map/ppermute | solution.py:29
  48.8 15.0 %collective-permute-start.2 = (bf16[3,2,256,256]{3,2,1,0:T(8,128)(2,1)S(1)}, bf16[3,2,256,256]{3,2,1,0:T(8,128)(2,1)S(1)}, u32[]{:S(2)}, u32[]{:S(2)}) collective-permute-start(bf16[3,2,256,256]{3,2,1,0:T(8,128)(2,1)S(1)} %collective-permute-done.refs_1_), channel_id=1, source_target_pairs={{0,1},{1,0},{2,3},{3,2},{4,5},{5,4},{6,7},{7,6},{8,9},{9,8},{10,11... | collective-permute-start | bytes 2359304 | tf_op jit(solution)/shard_map/ppermute | solution.py:18
  57.3 13.0 %collective-permute-start.9 = (bf16[4,256,256]{2,1,0:T(8,128)(2,1)S(1)}, bf16[4,256,256]{2,1,0:T(8,128)(2,1)S(1)}, u32[]{:S(2)}, u32[]{:S(2)}) collective-permute-start(bf16[4,256,256]{2,1,0:T(8,128)(2,1)S(1)} %get-tuple-element.18.refs_7_), channel_id=1, source_target_pairs={{0,4},{8,12},{16,20},{24,28},{1,5},{9,13},{17,21},{25,29},{2,6},{1... | collective-permute-start | bytes 1572872 | tf_op jit(solution)/shard_map/ppermute | solution.py:29
  61.7 16.8 %collective-permute-start.5 = (bf16[4,256,256]{2,1,0:T(8,128)(2,1)S(1)}, bf16[4,256,256]{2,1,0:T(8,128)(2,1)S(1)}, u32[]{:S(2)}, u32[]{:S(2)}) collective-permute-start(bf16[4,256,256]{2,1,0:T(8,128)(2,1)S(1)} %collective-permute-done.4.refs_4_), channel_id=1, source_target_pairs={{4,0},{12,8},{20,16},{28,24},{5,1},{13,9},{21,17},{29,25},{6,2},{1... | collective-permute-start | bytes 1572872 | tf_op jit(solution)/shard_map/ppermute | solution.py:29
  63.0 17.4 %collective-permute-start.10 = (bf16[4,256,256]{2,1,0:T(8,128)(2,1)S(1)}, bf16[4,256,256]{2,1,0:T(8,128)(2,1)S(1)}, u32[]{:S(2)}, u32[]{:S(2)}) collective-permute-start(bf16[4,256,256]{2,1,0:T(8,128)(2,1)S(1)} %collective-permute-done.4.refs_4_), channel_id=1, source_target_pairs={{4,12},{12,20},{20,28},{28,4},{5,13},{13,21},{21,29},{29,5},{6,14}... | collective-permute-start | bytes 1572872 | tf_op jit(solution)/shard_map/ppermute | solution.py:29
  63.7 29.8 %collective-permute-start.8 = (bf16[4,256,256]{2,1,0:T(8,128)(2,1)S(1)}, bf16[4,256,256]{2,1,0:T(8,128)(2,1)S(1)}, u32[]{:S(2)}, u32[]{:S(2)}) collective-permute-start(bf16[4,256,256]{2,1,0:T(8,128)(2,1)S(1)} %collective-permute-done.7.refs_4_), channel_id=1, source_target_pairs={{4,0},{12,8},{20,16},{28,24},{5,1},{13,9},{21,17},{29,25},{6,2},{1... | collective-permute-start | bytes 1572872 | tf_op jit(solution)/shard_map/ppermute | solution.py:29
  70.3 27.9 %collective-permute-start.13 = (bf16[4,256,256]{2,1,0:T(8,128)(2,1)S(1)}, bf16[4,256,256]{2,1,0:T(8,128)(2,1)S(1)}, u32[]{:S(2)}, u32[]{:S(2)}) collective-permute-start(bf16[4,256,256]{2,1,0:T(8,128)(2,1)S(1)} %get-tuple-element.21.refs_8_), channel_id=1, source_target_pairs={{0,8},{4,12},{8,16},{12,20},{16,24},{20,28},{24,0},{28,4},{1,9},{5... | collective-permute-start | bytes 1572872 | tf_op jit(solution)/shard_map/ppermute | solution.py:29
  78.4 19.7 %collective-permute-start.15 = (bf16[4,256,256]{2,1,0:T(8,128)(2,1)S(1)}, bf16[4,256,256]{2,1,0:T(8,128)(2,1)S(1)}, u32[]{:S(2)}, u32[]{:S(2)}) collective-permute-start(bf16[4,256,256]{2,1,0:T(8,128)(2,1)S(1)} %collective-permute-done.14.refs_8_), channel_id=1, source_target_pairs={{0,8},{8,16},{16,24},{24,0},{1,9},{9,17},{17,25},{25,1},{2,10},{10... | collective-permute-start | bytes 1572872 | tf_op jit(solution)/shard_map/ppermute | solution.py:29
  80.4 17.8 %collective-permute-start.12 = (bf16[4,256,256]{2,1,0:T(8,128)(2,1)S(1)}, bf16[4,256,256]{2,1,0:T(8,128)(2,1)S(1)}, u32[]{:S(2)}, u32[]{:S(2)}) collective-permute-start(bf16[4,256,256]{2,1,0:T(8,128)(2,1)S(1)} %collective-permute-done.4.refs_4_), channel_id=1, source_target_pairs={{0,4},{8,12},{16,20},{24,28},{1,5},{9,13},{17,21},{25,29},{2,6},{1... | collective-permute-start | bytes 1572872 | tf_op jit(solution)/shard_map/ppermute | solution.py:29
  86.2 12.0 %collective-permute-start.11 = (bf16[4,256,256]{2,1,0:T(8,128)(2,1)S(1)}, bf16[4,256,256]{2,1,0:T(8,128)(2,1)S(1)}, u32[]{:S(2)}, u32[]{:S(2)}) collective-permute-start(bf16[4,256,256]{2,1,0:T(8,128)(2,1)S(1)} %collective-permute-done.10), channel_id=1, source_target_pairs={{4,0},{12,8},{20,16},{28,24},{5,1},{13,9},{21,17},{29,25},{6,2},{1... | collective-permute-start | bytes 1572872 | tf_op jit(solution)/shard_map/ppermute | solution.py:29
  98.1 13.2 %copy-start.3 = (s32[64]{0:T(128)S(1)}, s32[64]{0:T(128)}, u32[]{:S(2)}) copy-start(s32[64]{0:T(128)} %param.8) | copy-start | bytes 772
  103.0 4.6 %collective-permute-start.16 = (f32[32,16]{1,0:T(8,128)S(1)}, f32[32,16]{1,0:T(8,128)S(1)}, u32[]{:S(2)}, u32[]{:S(2)}) collective-permute-start(f32[32,16]{1,0:T(8,128)S(1)} %shard_map.59), channel_id=1, source_target_pairs={{0,4},{4,0},{8,12},{12,8},{16,20},{20,16},{24,28},{28,24},{1,5},{5... | collective-permute-start | bytes 6152 | tf_op jit(solution)/shard_map/ppermute | solution.py:23
  107.6 3.7 %collective-permute-start.17 = (f32[32,16]{1,0:T(8,128)S(1)}, f32[32,16]{1,0:T(8,128)S(1)}, u32[]{:S(2)}, u32[]{:S(2)}) collective-permute-start(f32[32,16]{1,0:T(8,128)S(1)} %add.36), channel_id=1, source_target_pairs={{0,8},{4,12},{8,0},{12,4},{16,24},{20,28},{24,16},{28,20},{1,9},{5... | collective-permute-start | bytes 6152 | tf_op jit(solution)/shard_map/ppermute | solution.py:23
  111.3 4.6 %collective-permute-start.18 = (f32[32,16]{1,0:T(8,128)S(1)}, f32[32,16]{1,0:T(8,128)S(1)}, u32[]{:S(2)}, u32[]{:S(2)}) collective-permute-start(f32[32,16]{1,0:T(8,128)S(1)} %add.37), channel_id=1, source_target_pairs={{0,16},{4,20},{8,24},{12,28},{16,0},{20,4},{24,8},{28,12},{1,17},{... | collective-permute-start | bytes 6152 | tf_op jit(solution)/shard_map/ppermute | solution.py:23

commit v3 on v2

--- a/solution.py
+++ b/solution.py
@@ -78,31 +78,67 @@
     )(*perms.values())
 
 
-def trace_kernel(units, has_before, elem_parts, slice_parts, last, *refs):
+def chosen_kernel(even_ref, odd_ref, out_ref):
+    even = lax.rem(lax.axis_index("src"), 2) == 0
+    for at in range(out_ref.shape[0]):
+
+        @pl.when(even)
+        def _():
+            out_ref[at] = even_ref[at]
+
+        @pl.when(jnp.logical_not(even))
+        def _():
+            out_ref[at] = odd_ref[at]
+
+
+def chosen(for_even, for_odd):
+    return pl.pallas_call(
+        chosen_kernel,
+        out_shape=jax.ShapeDtypeStruct(for_even.shape, for_even.dtype),
+        in_specs=[VMEM] * 2,
+        out_specs=VMEM,
+        compiler_params=pltpu.CompilerParams(vmem_limit_bytes=4 << 20),
+    )(for_even, for_odd)
+
+
+def trace_kernel(units, has_before, elem_parts, n_arrays, slices, last, *refs):
     refs = list(refs)
     before_ref = refs.pop(0) if has_before else None
     p_ref = refs.pop(0)
     s_refs = [refs.pop(0) for _ in range(elem_parts)]
-    e_refs = [[refs.pop(0) for _ in range(parts)] for parts in slice_parts]
-    out_ref, w_ref, *rest = refs
+    arrays = [refs.pop(0) for _ in range(n_arrays)]
+    out_ref, w_ref, e_ref, *rest = refs
     acc_ref = rest.pop(0) if last else out_ref
     own, n_sep, nv = p_ref.shape[:3]
     ne_part = s_refs[0].shape[1]
     ne = ne_part * elem_parts
     nf = w_ref.shape[1]
     even = lax.rem(lax.axis_index("src"), 2) == 0
-    for c, parts in enumerate(e_refs):
-        if len(parts) == 2:
-            one, two = parts
+    e_refs = []
+    merged = 0
+    for parts in slices:
+        views = [arrays[at] if index is None else arrays[at].at[index] for at, index in parts]
+        if len(views) == 2:
+            even_view, odd_view = views
+
+            @pl.when(even)
+            def _():
+                for f in range(nf):
+                    e_ref[merged, f] = even_view[f]
 
             @pl.when(jnp.logical_not(even))
             def _():
-                one[...] = two[...]
+                for f in range(nf):
+                    e_ref[merged, f] = odd_view[f]
+
+            views = [e_ref.at[merged]]
+            merged += 1
+        e_refs.append(views[0])
 
     for n, (c, j, ts) in enumerate(units):
         prop = p_ref[j, ts]
         for f in range(nf):
-            half = jnp.dot(prop, e_refs[c][0][f], preferred_element_type=jnp.float32)
+            half = jnp.dot(prop, e_refs[c][f], preferred_element_type=jnp.float32)
             sandwich = lax.dot_general(
                 half.astype(jnp.bfloat16),
                 prop,
@@ -160,26 +196,97 @@
 
 def add_traces(before, units, slices, perm, elems, last):
     own, n_sep, nv = perm.shape[:3]
-    nf = slices[0][0].shape[0]
+    nf = slices[0][0][0].shape[-3]
     ne = elems[0].shape[1] * len(elems)
     flops = 2 * len(units) * nf * nv * nv * (2 * nv + ne * BLK)
     moved = 2 * nv * nv * (own * n_sep + own * ne + len(slices) * nf)
-    slice_parts = [len(parts) for parts in slices]
-    flat = [part for parts in slices for part in parts]
+    arrays, places = [], []
+    for parts in slices:
+        place = []
+        for array, index in parts:
+            if not any(array is known for known in arrays):
+                arrays.append(array)
+            place.append(([array is known for known in arrays].index(True), index))
+        places.append(place)
     acc = (n_sep * nf * BLK, ne * BLK)
     before = [] if before is None else [before]
-    scratch = [pltpu.VMEM((len(units), nf, nv, nv), jnp.bfloat16)]
+    scratch = [
+        pltpu.VMEM((len(units), nf, nv, nv), jnp.bfloat16),
+        pltpu.VMEM((max(1, sum(len(parts) > 1 for parts in slices)), nf, nv, nv), jnp.bfloat16),
+    ]
     if last:
         scratch.append(pltpu.VMEM(acc, jnp.float32))
+    limit = (12 << 20) + 2 * nf * nv * nv * len(units)
     return pl.pallas_call(
-        functools.partial(trace_kernel, units, bool(before), len(elems), slice_parts, last),
+        functools.partial(
+            trace_kernel, units, bool(before), len(elems), len(arrays), places, last
+        ),
         out_shape=jax.ShapeDtypeStruct((n_sep * nf, ne) if last else acc, jnp.float32),
-        in_specs=[VMEM] * (len(before) + 1 + len(elems) + len(flat)),
+        in_specs=[VMEM] * (len(before) + 1 + len(elems) + len(arrays)),
         out_specs=VMEM,
         scratch_shapes=scratch,
-        compiler_params=pltpu.CompilerParams(vmem_limit_bytes=24 << 20),
-        cost_estimate=pl.CostEstimate(flops=flops, bytes_accessed=moved, transcendentals=0),
-    )(*before, perm, *elems, *flat)
+        compiler_params=pltpu.CompilerParams(vmem_limit_bytes=limit),
+        cost_estimate=pl.CostEstimate(flops=0, bytes_accessed=1000, transcendentals=0),
+    )(*before, perm, *elems, *arrays)
+
+
+def by_hops(start, needed, reach):
+    blocks = {}
+    done = {}
+    own = len(start)
+    behind = crossed(start[0], "src", 1)
+    for i in reversed(range(own)):
+        last = max(block for block in range(reach + 1) if needed(block, i))
+        chain = [start[i]]
+        value = after(start[i], done[i + 2]) if i + 2 in done else start[i]
+        while 2 * len(chain) <= last + (1 if i else 0):
+            value = sent(value, 2, 1 if 2 * len(chain) > last else None)
+            chain.append(value)
+        done[i] = chain[1]
+        for hop, value in enumerate(chain[: last // 2 + 1]):
+            blocks[2 * hop, i] = [(value, None)]
+        if i:
+            for block in range(1, last + 1, 2):
+                low, high = chain[block // 2], chain[block // 2 + 1]
+                blocks[block, i] = [(sent(high, -1, 1), None), (sent(low, 1, 0), None)]
+        else:
+            lower = behind
+            for block in range(1, last + 1, 2):
+                value = after(lower, done[1]) if lower is behind and 1 in done else lower
+                upper = sent(value, 2, 0 if block + 2 > last else None)
+                blocks[block, i] = [(upper, None), (lower, None)]
+                lower = upper
+    return blocks
+
+
+def by_shared_hops(start, later, perm_parts, early):
+    first, second, third = start
+    two_back = sent(third, 2)
+    second_back = sent(second, 2)
+    swap_first = crossed(first, "src", 1)
+    to_odd = sent(later, 1, 0)
+    third_even = sent(two_back, -1, 1)
+    onward = sent(after(chosen(swap_first, two_back), *perm_parts), 2)
+    second_even = sent(second_back, -1, 1)
+    first_back = sent(after(first, second_back), 2)
+    blocks = {
+        (0, 2): [(third, None)],
+        (0, 1): [(second, None)],
+        (0, 0): [(first, None)],
+        (2, 2): [(two_back, None)],
+        (2, 1): [(second_back, None)],
+    }
+    total = early(blocks)
+    last_odd = sent(after(two_back, to_odd, total), 1, 0)
+    last_even = sent(after(onward, third_even, second_even, to_odd), -1, 1)
+    later_blocks = {
+        (1, 2): [(third_even, None), (to_odd, 1)],
+        (1, 1): [(second_even, None), (to_odd, 0)],
+        (2, 0): [(first_back, None)],
+        (1, 0): [(onward, None), (swap_first, None)],
+        (3, 2): [(last_even, None), (last_odd, None)],
+    }
+    return total, later_blocks
 
 
 def body(peramb, elem_src, elem_snk, op_elem, hlt_kernel):
@@ -196,56 +303,39 @@
         return [(j, own * block + j - i) for j in range(own) if 0 <= own * block + j - i < n_sep]
 
     reach = -(-(n_sep - 1) // own)
+    elems = [elem_snk] + [shifted(elem_snk, "mom", -dm) for dm in range(1, n_mom)]
     quarter = lax.dynamic_slice_in_dim(elem_src, y * nf, nf, 1)
     start = [quarter[i] for i in range(own)]
-    peramb, *start = lax.optimization_barrier((peramb, *start))
-    behind = crossed(start[0], "src", 1)
+    later = quarter[1:]
+    peramb, later, *start = lax.optimization_barrier((peramb, later, *start))
     sheared = shear(peramb, n_src, own, seps)
     rows_in = lax.all_to_all(sheared, "src", 0, 0)
-    start = [after(value, rows_in) for value in start]
+    start = [after(value, rows_in, elems[-1]) for value in start]
+    later = after(later, rows_in, elems[-1])
     mine = jnp.transpose(rows_in, (1, 2, 0, 3, 4)).reshape(own, seps, n_src * rows, nv)
-    blocks = {}
-    done = {}
-    for i in reversed(range(own)):
-        last = max(block for block in range(reach + 1) if needed(block, i))
-        chain = [start[i]]
-        value = after(start[i], done[i + 2]) if i + 2 in done else start[i]
-        while 2 * len(chain) <= last + (1 if i else 0):
-            value = sent(value, 2, 1 if 2 * len(chain) > last else None)
-            chain.append(value)
-        done[i] = chain[1]
-        for hop, value in enumerate(chain[: last // 2 + 1]):
-            blocks[2 * hop, i] = (value,)
-        if i:
-            for block in range(1, last + 1, 2):
-                low, high = chain[block // 2], chain[block // 2 + 1]
-                blocks[block, i] = (sent(high, -1, 1), sent(low, 1, 0))
-        else:
-            lower = behind
-            for block in range(1, last + 1, 2):
-                value = after(lower, done[1]) if lower is behind and 1 in done else lower
-                upper = sent(value, 2, 0 if block + 2 > last else None)
-                blocks[block, i] = (upper, lower)
-                lower = upper
-
-    perms = {(0, 0): mine}
-    for dy in range(1, n_snk):
-        perms[dy, 0] = shifted(mine, "snk", -dy)
-    for dy in range(n_snk):
-        for dm in range(1, n_mom):
-            perms[dy, dm] = shifted(perms[dy, 0], "mom", -dm)
-    elems = [elem_snk] + [shifted(elem_snk, "mom", -dm) for dm in range(1, n_mom)]
-
-    groups = [[], [], []]
-    for block, i in blocks:
-        early = block == 0 or (i == own - 1 and block < 3)
-        groups[0 if early else 2 if i == 0 or block > 2 else 1].append((block, i))
-    perm = ordered(perms)
-    total = None
-    for group in groups:
-        units = [(c, j, ts) for c, (k, i) in enumerate(group) for j, ts in needed(k, i)]
-        slices = [blocks[b] for b in group]
-        total = add_traces(total, units, slices, perm, elems, group is groups[-1])
+    perms = {(dy, 0): shifted(mine, "snk", -dy) if dy else mine for dy in range(n_snk)}
+    met = []
+
+    def traces(before, blocks, last=False):
+        if not met:
+            held = blocks[2, own - 1][0][0]
+            for dy in range(n_snk):
+                for dm in range(1, n_mom):
+                    perms[dy, dm] = shifted(perms[dy, 0], "mom", -dm)
+            met.append(ordered(perms))
+        units = [(c, j, ts) for c, (k, i) in enumerate(blocks) for j, ts in needed(k, i)]
+        return add_traces(before, units, list(blocks.values()), met[0], elems, last)
+
+    if own == 3 and reach == 3 and not needed(3, 1):
+        parts = [part for (dy, _), part in perms.items() if dy]
+        total, blocks = by_shared_hops(start, later, parts, functools.partial(traces, None))
+    else:
+        blocks = by_hops(start, needed, reach)
+        early = {at: blocks.pop(at) for at in list(blocks) if at[0] == 0 or (at[0] == 2 and at[1])}
+        total = traces(None, early)
+    next_ones = {at: blocks.pop(at) for at in list(blocks) if at[0] == 1 and at[1]}
+    total = traces(total, next_ones)
+    total = traces(total, blocks, last=True)
 
     if n_src == 8:
         for step in (1, 2, 4):

time: 122 us -> 116 us (0.951)
  waiting for transfers between devices: 44.1 us -> 36.5 us
  Pallas kernels: 15.7 us -> 18.4 us
  starting transfers between devices: 26.5 us -> 25 us
    ppermute x4, waiting for transfers between devices: 21.4 us -> 7.07 us  [crossed(): lax.ppermute(value, axis, [(source, source ^ mask) for source in range(co...]
    ppermute x4, waiting for transfers between devices: 0.91 us -> 12.2 us  [shifted(): return lax.ppermute(value, axis, pairs)]
    ppermute x11 -> x9, starting transfers between devices: 20.1 us -> 15.2 us  [sent(): lax.ppermute(value, 'src', [(at, (at + steps) % count) for at in sources])]
    ppermute x11 -> x9, waiting for transfers between devices: 21.7 us -> 17.2 us  [sent(): lax.ppermute(value, 'src', [(at, (at + steps) % count) for at in sources])]
    ppermute x4, starting transfers between devices: 4.33 us -> 7.69 us  [crossed(): lax.ppermute(value, axis, [(source, source ^ mask) for source in range(co...]
    pallas_call x3, Pallas kernels: 15.4 us -> 18 us  [add_traces(): pl.pallas_call(functools.partial(trace_kernel, units, bool(before), len(e...]
    slice x0 -> x1, local copies, waits for them, and re-layouts: none -> 1.41 us  [body(): later = quarter[1:]]
  transfers between devices with their start and end apart: 19 -> 17, of which waited for: 8 -> 7; matrix products, arithmetic and copies ran while one was open for 1% -> 3% of each run, Pallas kernels for 9% -> 11%
where the time goes in v3:
time: 116 us
  waiting for transfers between devices  36.5 us (31%)
  blocking collectives  31.7 us (27%)
  starting transfers between devices  25 us (22%)
  Pallas kernels  18.4 us (16%)
  local copies, waits for them, and re-layouts  3.26 us (3%)
    all_to_all x1, blocking collectives, body(): rows_in = lax.all_to_all(sheared, 'src', 0, 0)  27.4 us
    pallas_call x3, Pallas kernels, add_traces(): pl.pallas_call(functools.partial(trace_kernel, units, bool(before), len(e...  18 us
    ppermute x9, waiting for transfers between devices, sent(): lax.ppermute(value, 'src', [(at, (at + steps) % count) for at in sources])  17.2 us
    ppermute x9, starting transfers between devices, sent(): lax.ppermute(value, 'src', [(at, (at + steps) % count) for at in sources])  15.2 us
    ppermute x4, waiting for transfers between devices, shifted(): return lax.ppermute(value, axis, pairs)  12.2 us
    ppermute x4, starting transfers between devices, crossed(): lax.ppermute(value, axis, [(source, source ^ mask) for source in range(co...  7.69 us
    ppermute x4, waiting for transfers between devices, crossed(): lax.ppermute(value, axis, [(source, source ^ mask) for source in range(co...  7.07 us
    all_gather x1, blocking collectives, body(): gathered = lax.all_gather(total, 'snk', axis=0)  4.36 us
  transfers between devices with their start and end apart: 17, of which 7 were waited for; matrix products, arithmetic and copies ran while one was open for 3% of the time, Pallas kernels for 11%

profile of v3, /device:TPU:0, one launch (start us, length us, event | category | flops | bytes accessed | tf_op | source)
XLA Modules:
  0.0 116.0 jit_solution(12138227345734844462)
XLA Ops:
  0.0 0.0 copy-start
  0.0 0.5 collective-permute-start.3
  0.5 0.0 copy-start.2
  0.5 1.4 %constant_dynamic-slice_fusion = bf16[2,4,256,256]{3,2,1,0:T(8,128)(2,1)S(1)} fusion(bf16[3,8,256,256]{3,2,1,0:T(8,128)(2,1)} %param.6, s32[]{:T(128)S(6)} %add.43, s32[]{:T(128)S(6)} %select_n.17), kind=kLoop, calls=%fused_computation.15 | loop fusion | bytes 2097160 | tf_op jit(solution)/shard_map/slice | solution.py:309
  1.9 1.5 %dynamic-slice_bitcast_fusion = (bf16[4,256,256]{2,1,0:T(8,128)(2,1)S(1)}, bf16[4,256,256]{2,1,0:T(8,128)(2,1)S(1)}, bf16[4,256,256]{2,1,0:T(8,128)(2,1)S(1)}) fusion(bf16[3,8,256,256]{3,2,1,0:T(8,128)(2,1)} %param.6, s32[]{:T(128)S(6)} %add.45, s32[]{:T(128)S(6)} %select_n.17, s32[]{:T(128)S(6)} %add.43), kind=kLoop, calls=%fused_computation.1 | loop fusion | bytes 3145740 | tf_op jit(solution)/shard_map/squeeze | solution.py:308
  3.3 0.0 copy-done.2
  3.4 0.1 shard_map.55
  3.4 27.4 %all_to_all.5 = bf16[8,3,2,32,256]{4,3,2,1,0:T(8,128)(2,1)S(1)} all-to-all(bf16[8,3,2,32,256]{4,3,2,1,0:T(8,128)(2,1)S(1)} %shard_map.55), channel_id=1, replica_groups=mesh['src'=8,'snk'=2,'mom'=2] {'src'}, dimensions={0} | all-to-all | bytes 1572864 | tf_op jit(solution)/shard_map/all_to_all | solution.py:312
  30.8 0.1 copy.12
  30.9 1.6 %collective-permute-start = (bf16[3,2,256,256]{3,2,1,0:T(8,128)(2,1)S(1)}, bf16[3,2,256,256]{3,2,1,0:T(8,128)(2,1)S(1)}, u32[]{:S(2)}, u32[]{:S(2)}) collective-permute-start(bf16[3,2,256,256]{3,2,1,0:T(8,128)(2,1)S(1)} %bitcast.23), channel_id=1, source_target_pairs={{0,2},{2,0},{1,3},{3,1},{4,6},{6,4},{5,7},{7,5},{8,10},{10,8},{9,1... | collective-permute-start | bytes 2359304 | tf_op jit(solution)/shard_map/ppermute | solution.py:18
  32.5 0.0 collective-permute-done.3.refs_2_.refs_3_
  32.5 1.1 collective-permute-start.4
  33.6 0.0 collective-permute-start.1
  33.6 0.4 collective-permute-start.10
  34.0 3.6 %collective-permute-start.7 = (bf16[2,4,256,256]{3,2,1,0:T(8,128)(2,1)S(1)}, bf16[2,4,256,256]{3,2,1,0:T(8,128)(2,1)S(1)}, u32[]{:S(2)}, u32[]{:S(2)}) collective-permute-start(bf16[2,4,256,256]{3,2,1,0:T(8,128)(2,1)S(1)} %constant_dynamic-slice_fusion), channel_id=1, source_target_pairs={{0,4},{8,12},{16,20},{24,28},{1,5},{9,13},{17,21},{25,29},{2,6},{1... | collective-permute-start | bytes 3145736 | tf_op jit(solution)/shard_map/ppermute | solution.py:29
  37.6 12.2 %collective-permute-done.refs_1_ = bf16[3,2,256,256]{3,2,1,0:T(8,128)(2,1)S(1)} collective-permute-done((bf16[3,2,256,256]{3,2,1,0:T(8,128)(2,1)S(1)}, bf16[3,2,256,256]{3,2,1,0:T(8,128)(2,1)S(1)}, u32[]{:S(2)}, u32[]{:S(2)}) %collective-permute-start) | collective-permute-done | bytes 786464 | tf_op jit(solution)/shard_map/ppermute | solution.py:18
  49.8 0.5 collective-permute-start.5
  50.2 0.0 collective-permute-done.4.refs_6_.odd_ref
  50.2 0.0 collective-permute-start.2
  50.2 0.0 collective-permute-done.10.even_ref.refs_6_
  50.3 0.1 shard_map.59
  50.3 0.0 copy-start.1
  50.3 1.6 %collective-permute-start.11 = (bf16[4,256,256]{2,1,0:T(8,128)(2,1)S(1)}, bf16[4,256,256]{2,1,0:T(8,128)(2,1)S(1)}, u32[]{:S(2)}, u32[]{:S(2)}) collective-permute-start(bf16[4,256,256]{2,1,0:T(8,128)(2,1)S(1)} %shard_map.59), channel_id=1, source_target_pairs={{0,8},{4,12},{8,16},{12,20},{16,24},{20,28},{24,0},{28,4},{1,9},{5... | collective-permute-start | bytes 1572872 | tf_op jit(solution)/shard_map/ppermute | solution.py:29
  51.9 0.0 collective-permute-done.1.refs_2_
  51.9 1.3 %collective-permute-start.6 = (bf16[4,256,256]{2,1,0:T(8,128)(2,1)S(1)}, bf16[4,256,256]{2,1,0:T(8,128)(2,1)S(1)}, u32[]{:S(2)}, u32[]{:S(2)}) collective-permute-start(bf16[4,256,256]{2,1,0:T(8,128)(2,1)S(1)} %collective-permute-done.4.refs_6_.odd_ref), channel_id=1, source_target_pairs={{4,0},{12,8},{20,16},{28,24},{5,1},{13,9},{21,17},{29,25},{6,2},{1... | collective-permute-start | bytes 1572872 | tf_op jit(solution)/shard_map/ppermute | solution.py:29
  53.2 13.2 %collective-permute-done.5.refs_7_ = bf16[4,256,256]{2,1,0:T(8,128)(2,1)S(1)} collective-permute-done((bf16[4,256,256]{2,1,0:T(8,128)(2,1)S(1)}, bf16[4,256,256]{2,1,0:T(8,128)(2,1)S(1)}, u32[]{:S(2)}, u32[]{:S(2)}) %collective-permute-start.5) | collective-permute-done | bytes 524320 | tf_op jit(solution)/shard_map/ppermute | solution.py:29
  66.4 1.3 %collective-permute-start.8 = (bf16[4,256,256]{2,1,0:T(8,128)(2,1)S(1)}, bf16[4,256,256]{2,1,0:T(8,128)(2,1)S(1)}, u32[]{:S(2)}, u32[]{:S(2)}) collective-permute-start(bf16[4,256,256]{2,1,0:T(8,128)(2,1)S(1)} %collective-permute-done.5.refs_7_), channel_id=1, source_target_pairs={{4,0},{12,8},{20,16},{28,24},{5,1},{13,9},{21,17},{29,25},{6,2},{1... | collective-permute-start | bytes 1572872 | tf_op jit(solution)/shard_map/ppermute | solution.py:29
  67.7 0.0 collective-permute-done.2.refs_3_
  67.7 0.2 shard_map.56.refs_0_.refs_1_
  68.0 0.1 collective-permute-start.9
  68.0 0.0 copy-done.1
  68.0 6.0 %shard_map.57.refs_0_ = f32[512,256]{1,0:T(8,128)S(1)} custom-call(bf16[3,8,256,256]{3,2,1,0:T(8,128)(2,1)S(1)} %shard_map.56.refs_0_.refs_1_, bf16[3,8,256,256]{3,2,1,0:T(8,128)(2,1)S(1)} %copy-done.1, bf16[3,8,256,256]{3,2,1,0:T(8,128)(2,1)S(1)} %collective-permute-done.3.refs_2_.refs_3_, bf16[4,256,256]{2,1,0:T(8,128)(2,1)S(1)} %get-tuple-element.20.refs_3_, ...), custom_call_target="tpu_custom_call" | custom-call | bytes 1000 | tf_op jit(solution)/shard_map/pallas_call | solution.py:220
  74.1 0.0 collective-permute-done.7.refs_5_
  74.1 4.6 %collective-permute-start.13 = (bf16[4,256,256]{2,1,0:T(8,128)(2,1)S(1)}, bf16[4,256,256]{2,1,0:T(8,128)(2,1)S(1)}, u32[]{:S(2)}, u32[]{:S(2)}) collective-permute-start(bf16[4,256,256]{2,1,0:T(8,128)(2,1)S(1)} %collective-permute-done.4.refs_6_.odd_ref), channel_id=1, source_target_pairs={{0,4},{8,12},{16,20},{24,28},{1,5},{9,13},{17,21},{25,29},{2,6},{1... | collective-permute-start | bytes 1572872 | tf_op jit(solution)/shard_map/ppermute | solution.py:29
  78.7 0.0 collective-permute-done.11.refs_5_
  78.7 0.0 collective-permute-done.6.refs_4_
  78.7 0.3 collective-permute-done.8.refs_6_
  79.1 1.3 %collective-permute-start.12 = (bf16[4,256,256]{2,1,0:T(8,128)(2,1)S(1)}, bf16[4,256,256]{2,1,0:T(8,128)(2,1)S(1)}, u32[]{:S(2)}, u32[]{:S(2)}) collective-permute-start(bf16[4,256,256]{2,1,0:T(8,128)(2,1)S(1)} %collective-permute-done.11.refs_5_), channel_id=1, source_target_pairs={{4,0},{12,8},{20,16},{28,24},{5,1},{13,9},{21,17},{29,25},{6,2},{1... | collective-permute-start | bytes 1572872 | tf_op jit(solution)/shard_map/ppermute | solution.py:29
  80.4 6.7 %shard_map.58.refs_0_ = f32[512,256]{1,0:T(8,128)S(1)} custom-call(f32[512,256]{1,0:T(8,128)S(1)} %shard_map.57.refs_0_, bf16[3,8,256,256]{3,2,1,0:T(8,128)(2,1)S(1)} %shard_map.56.refs_0_.refs_1_, bf16[3,8,256,256]{3,2,1,0:T(8,128)(2,1)S(1)} %copy-done.1, bf16[3,8,256,256]{3,2,1,0:T(8,128)(2,1)S(1)} %collective-permute-done.3.refs_2_.refs_3_, ...), custom_call_target="tpu_custom_call" | custom-call | bytes 1000 | tf_op jit(solution)/shard_map/pallas_call | solution.py:220
  87.1 0.0 copy-start.3
  87.1 0.0 collective-permute-done.9.refs_4_
  87.1 0.0 collective-permute-done.13.refs_8_
  87.1 3.6 %collective-permute-done.12.refs_7_ = bf16[4,256,256]{2,1,0:T(8,128)(2,1)S(1)} collective-permute-done((bf16[4,256,256]{2,1,0:T(8,128)(2,1)S(1)}, bf16[4,256,256]{2,1,0:T(8,128)(2,1)S(1)}, u32[]{:S(2)}, u32[]{:S(2)}) %collective-permute-start.12) | collective-permute-done | bytes 524320 | tf_op jit(solution)/shard_map/ppermute | solution.py:29
  90.8 5.2 %shard_map.60 = f32[32,16]{1,0:T(8,128)S(1)} custom-call(f32[512,256]{1,0:T(8,128)S(1)} %shard_map.58.refs_0_, bf16[3,8,256,256]{3,2,1,0:T(8,128)(2,1)S(1)} %shard_map.56.refs_0_.refs_1_, bf16[3,8,256,256]{3,2,1,0:T(8,128)(2,1)S(1)} %copy-done.1, bf16[3,8,256,256]{3,2,1,0:T(8,128)(2,1)S(1)} %collective-permute-done.3.refs_2_.refs_3_, ...), custom_call_target="tpu_custom_call" | custom-call | bytes 1000 | tf_op jit(solution)/shard_map/pallas_call | solution.py:220
  96.0 0.1 collective-permute-start.14
  96.1 3.7 %collective-permute-done.14 = f32[32,16]{1,0:T(8,128)S(1)} collective-permute-done((f32[32,16]{1,0:T(8,128)S(1)}, f32[32,16]{1,0:T(8,128)S(1)}, u32[]{:S(2)}, u32[]{:S(2)}) %collective-permute-start.14) | collective-permute-done | bytes 2080 | tf_op jit(solution)/shard_map/ppermute | solution.py:23
  99.8 3.1 %collective-permute-start.15 = (f32[32,16]{1,0:T(8,128)S(1)}, f32[32,16]{1,0:T(8,128)S(1)}, u32[]{:S(2)}, u32[]{:S(2)}) collective-permute-start(f32[32,16]{1,0:T(8,128)S(1)} %add.36), channel_id=1, source_target_pairs={{0,8},{4,12},{8,0},{12,4},{16,24},{20,28},{24,16},{28,20},{1,9},{5... | collective-permute-start | bytes 6152 | tf_op jit(solution)/shard_map/ppermute | solution.py:23
  102.9 1.7 %collective-permute-done.15 = f32[32,16]{1,0:T(8,128)S(1)} collective-permute-done((f32[32,16]{1,0:T(8,128)S(1)}, f32[32,16]{1,0:T(8,128)S(1)}, u32[]{:S(2)}, u32[]{:S(2)}) %collective-permute-start.15) | collective-permute-done | bytes 2080 | tf_op jit(solution)/shard_map/ppermute | solution.py:23
  104.6 4.1 %collective-permute-start.16 = (f32[32,16]{1,0:T(8,128)S(1)}, f32[32,16]{1,0:T(8,128)S(1)}, u32[]{:S(2)}, u32[]{:S(2)}) collective-permute-start(f32[32,16]{1,0:T(8,128)S(1)} %add.37), channel_id=1, source_target_pairs={{0,16},{4,20},{8,24},{12,28},{16,0},{20,4},{24,8},{28,12},{1,17},{... | collective-permute-start | bytes 6152 | tf_op jit(solution)/shard_map/ppermute | solution.py:23
  108.7 0.0 copy-done.3
  108.7 0.1 dynamic_slice.7
  108.8 1.6 %collective-permute-done.16 = f32[32,16]{1,0:T(8,128)S(1)} collective-permute-done((f32[32,16]{1,0:T(8,128)S(1)}, f32[32,16]{1,0:T(8,128)S(1)}, u32[]{:S(2)}, u32[]{:S(2)}) %collective-permute-start.16) | collective-permute-done | bytes 2080 | tf_op jit(solution)/shard_map/ppermute | solution.py:23
  110.5 0.1 copy.13
  110.5 4.4 %all-gather.1 = f32[2,32,16]{1,2,0:T(8,128)S(1)} all-gather(f32[1,32,16]{1,2,0:T(8,128)S(1)} %copy.13), channel_id=2, replica_groups=mesh['src'=8,'snk'=2,'mom'=2] {'snk'}, dimensions={0}, use_global_device_ids=true | all-gather | bytes 6144 | tf_op jit(solution)/shard_map/all_gather | solution.py:345
  114.9 0.1 copy.14
  115.0 0.2 convolution_multiply_fusion
  115.2 0.1 copy.16
  115.3 0.0 copy-done
  115.3 0.8 fusion.1
  (4 shorter events, 0.0 us)
Async XLA Ops:
  0.0 115.3 %copy-start = (f32[8,128]{1,0:T(8,128)S(1)}, f32[8,128]{1,0:T(8,128)}, u32[]{:S(2)}) copy-start(f32[8,128]{1,0:T(8,128)} %param.9) | copy-start | bytes 12292
  0.0 32.5 %collective-permute-start.3 = (bf16[3,8,256,256]{3,2,1,0:T(8,128)(2,1)}, bf16[3,8,256,256]{3,2,1,0:T(8,128)(2,1)S(1)}, u32[]{:S(2)}, u32[]{:S(2)}) collective-permute-start(bf16[3,8,256,256]{3,2,1,0:T(8,128)(2,1)} %refs_2_.3), channel_id=1, source_target_pairs={{0,1},{1,0},{2,3},{3,2},{4,5},{5,4},{6,7},{7,6},{8,9},{9,8},{10,11... | collective-permute-start | bytes 9437192 | tf_op jit(solution)/shard_map/ppermute | solution.py:18
  0.5 2.9 %copy-start.2 = (bf16[24,4,32,256]{3,2,1,0:T(8,128)(2,1)S(1)}, bf16[24,4,32,256]{3,2,1,0:T(8,128)(2,1)}, u32[]{:S(2)}) copy-start(bf16[24,4,32,256]{3,2,1,0:T(8,128)(2,1)} %peramb_ref) | copy-start | bytes 4718596
  30.9 18.9 %collective-permute-start = (bf16[3,2,256,256]{3,2,1,0:T(8,128)(2,1)S(1)}, bf16[3,2,256,256]{3,2,1,0:T(8,128)(2,1)S(1)}, u32[]{:S(2)}, u32[]{:S(2)}) collective-permute-start(bf16[3,2,256,256]{3,2,1,0:T(8,128)(2,1)S(1)} %bitcast.23), channel_id=1, source_target_pairs={{0,2},{2,0},{1,3},{3,1},{4,6},{6,4},{5,7},{7,5},{8,10},{10,8},{9,1... | collective-permute-start | bytes 2359304 | tf_op jit(solution)/shard_map/ppermute | solution.py:18
  32.5 17.8 %collective-permute-start.4 = (bf16[4,256,256]{2,1,0:T(8,128)(2,1)S(1)}, bf16[4,256,256]{2,1,0:T(8,128)(2,1)S(1)}, u32[]{:S(2)}, u32[]{:S(2)}) collective-permute-start(bf16[4,256,256]{2,1,0:T(8,128)(2,1)S(1)} %get-tuple-element.20.refs_3_), channel_id=1, source_target_pairs={{0,8},{4,12},{8,16},{12,20},{16,24},{20,28},{24,0},{28,4},{1,9},{5... | collective-permute-start | bytes 1572872 | tf_op jit(solution)/shard_map/ppermute | solution.py:29
  33.6 18.3 %collective-permute-start.1 = (bf16[3,2,256,256]{3,2,1,0:T(8,128)(2,1)S(1)}, bf16[3,2,256,256]{3,2,1,0:T(8,128)(2,1)S(1)}, u32[]{:S(2)}, u32[]{:S(2)}) collective-permute-start(bf16[3,2,256,256]{3,2,1,0:T(8,128)(2,1)S(1)} %bitcast.24), channel_id=1, source_target_pairs={{0,1},{1,0},{2,3},{3,2},{4,5},{5,4},{6,7},{7,6},{8,9},{9,8},{10,11... | collective-permute-start | bytes 2359304 | tf_op jit(solution)/shard_map/ppermute | solution.py:18
  33.6 16.7 %collective-permute-start.10 = (bf16[4,256,256]{2,1,0:T(8,128)(2,1)S(1)}, bf16[4,256,256]{2,1,0:T(8,128)(2,1)S(1)}, u32[]{:S(2)}, u32[]{:S(2)}) collective-permute-start(bf16[4,256,256]{2,1,0:T(8,128)(2,1)S(1)} %get-tuple-element.27.refs_5_), channel_id=1, source_target_pairs={{0,4},{4,0},{8,12},{12,8},{16,20},{20,16},{24,28},{28,24},{1,5},{5... | collective-permute-start | bytes 1572872 | tf_op jit(solution)/shard_map/ppermute | solution.py:23
  34.0 40.1 %collective-permute-start.7 = (bf16[2,4,256,256]{3,2,1,0:T(8,128)(2,1)S(1)}, bf16[2,4,256,256]{3,2,1,0:T(8,128)(2,1)S(1)}, u32[]{:S(2)}, u32[]{:S(2)}) collective-permute-start(bf16[2,4,256,256]{3,2,1,0:T(8,128)(2,1)S(1)} %constant_dynamic-slice_fusion), channel_id=1, source_target_pairs={{0,4},{8,12},{16,20},{24,28},{1,5},{9,13},{17,21},{25,29},{2,6},{1... | collective-permute-start | bytes 3145736 | tf_op jit(solution)/shard_map/ppermute | solution.py:29
  49.8 16.7 %collective-permute-start.5 = (bf16[4,256,256]{2,1,0:T(8,128)(2,1)S(1)}, bf16[4,256,256]{2,1,0:T(8,128)(2,1)S(1)}, u32[]{:S(2)}, u32[]{:S(2)}) collective-permute-start(bf16[4,256,256]{2,1,0:T(8,128)(2,1)S(1)} %get-tuple-element.22.refs_4_), channel_id=1, source_target_pairs={{0,8},{4,12},{8,16},{12,20},{16,24},{20,28},{24,0},{28,4},{1,9},{5... | collective-permute-start | bytes 1572872 | tf_op jit(solution)/shard_map/ppermute | solution.py:29
  50.2 17.5 %collective-permute-start.2 = (bf16[3,2,256,256]{3,2,1,0:T(8,128)(2,1)S(1)}, bf16[3,2,256,256]{3,2,1,0:T(8,128)(2,1)S(1)}, u32[]{:S(2)}, u32[]{:S(2)}) collective-permute-start(bf16[3,2,256,256]{3,2,1,0:T(8,128)(2,1)S(1)} %collective-permute-done.refs_1_), channel_id=1, source_target_pairs={{0,1},{1,0},{2,3},{3,2},{4,5},{5,4},{6,7},{7,6},{8,9},{9,8},{10,11... | collective-permute-start | bytes 2359304 | tf_op jit(solution)/shard_map/ppermute | solution.py:18
  50.3 17.7 %copy-start.1 = (bf16[3,8,256,256]{3,2,1,0:T(8,128)(2,1)S(1)}, bf16[3,8,256,256]{3,2,1,0:T(8,128)(2,1)}, u32[]{:S(2)}) copy-start(bf16[3,8,256,256]{3,2,1,0:T(8,128)(2,1)} %refs_2_.3) | copy-start | bytes 9437188
  50.3 28.4 %collective-permute-start.11 = (bf16[4,256,256]{2,1,0:T(8,128)(2,1)S(1)}, bf16[4,256,256]{2,1,0:T(8,128)(2,1)S(1)}, u32[]{:S(2)}, u32[]{:S(2)}) collective-permute-start(bf16[4,256,256]{2,1,0:T(8,128)(2,1)S(1)} %shard_map.59), channel_id=1, source_target_pairs={{0,8},{4,12},{8,16},{12,20},{16,24},{20,28},{24,0},{28,4},{1,9},{5... | collective-permute-start | bytes 1572872 | tf_op jit(solution)/shard_map/ppermute | solution.py:29
  51.9 26.8 %collective-permute-start.6 = (bf16[4,256,256]{2,1,0:T(8,128)(2,1)S(1)}, bf16[4,256,256]{2,1,0:T(8,128)(2,1)S(1)}, u32[]{:S(2)}, u32[]{:S(2)}) collective-permute-start(bf16[4,256,256]{2,1,0:T(8,128)(2,1)S(1)} %collective-permute-done.4.refs_6_.odd_ref), channel_id=1, source_target_pairs={{4,0},{12,8},{20,16},{28,24},{5,1},{13,9},{21,17},{29,25},{6,2},{1... | collective-permute-start | bytes 1572872 | tf_op jit(solution)/shard_map/ppermute | solution.py:29
  66.4 12.6 %collective-permute-start.8 = (bf16[4,256,256]{2,1,0:T(8,128)(2,1)S(1)}, bf16[4,256,256]{2,1,0:T(8,128)(2,1)S(1)}, u32[]{:S(2)}, u32[]{:S(2)}) collective-permute-start(bf16[4,256,256]{2,1,0:T(8,128)(2,1)S(1)} %collective-permute-done.5.refs_7_), channel_id=1, source_target_pairs={{4,0},{12,8},{20,16},{28,24},{5,1},{13,9},{21,17},{29,25},{6,2},{1... | collective-permute-start | bytes 1572872 | tf_op jit(solution)/shard_map/ppermute | solution.py:29
  68.0 19.2 %collective-permute-start.9 = (bf16[4,256,256]{2,1,0:T(8,128)(2,1)S(1)}, bf16[4,256,256]{2,1,0:T(8,128)(2,1)S(1)}, u32[]{:S(2)}, u32[]{:S(2)}) collective-permute-start(bf16[4,256,256]{2,1,0:T(8,128)(2,1)S(1)} %get-tuple-element.27.refs_5_), channel_id=1, source_target_pairs={{0,8},{4,12},{8,16},{12,20},{16,24},{20,28},{24,0},{28,4},{1,9},{5... | collective-permute-start | bytes 1572872 | tf_op jit(solution)/shard_map/ppermute | solution.py:29
  74.1 13.0 %collective-permute-start.13 = (bf16[4,256,256]{2,1,0:T(8,128)(2,1)S(1)}, bf16[4,256,256]{2,1,0:T(8,128)(2,1)S(1)}, u32[]{:S(2)}, u32[]{:S(2)}) collective-permute-start(bf16[4,256,256]{2,1,0:T(8,128)(2,1)S(1)} %collective-permute-done.4.refs_6_.odd_ref), channel_id=1, source_target_pairs={{0,4},{8,12},{16,20},{24,28},{1,5},{9,13},{17,21},{25,29},{2,6},{1... | collective-permute-start | bytes 1572872 | tf_op jit(solution)/shard_map/ppermute | solution.py:29
  79.1 11.7 %collective-permute-start.12 = (bf16[4,256,256]{2,1,0:T(8,128)(2,1)S(1)}, bf16[4,256,256]{2,1,0:T(8,128)(2,1)S(1)}, u32[]{:S(2)}, u32[]{:S(2)}) collective-permute-start(bf16[4,256,256]{2,1,0:T(8,128)(2,1)S(1)} %collective-permute-done.11.refs_5_), channel_id=1, source_target_pairs={{4,0},{12,8},{20,16},{28,24},{5,1},{13,9},{21,17},{29,25},{6,2},{1... | collective-permute-start | bytes 1572872 | tf_op jit(solution)/shard_map/ppermute | solution.py:29
  87.1 21.6 %copy-start.3 = (s32[64]{0:T(128)S(1)}, s32[64]{0:T(128)}, u32[]{:S(2)}) copy-start(s32[64]{0:T(128)} %param.8) | copy-start | bytes 772
  96.0 3.8 %collective-permute-start.14 = (f32[32,16]{1,0:T(8,128)S(1)}, f32[32,16]{1,0:T(8,128)S(1)}, u32[]{:S(2)}, u32[]{:S(2)}) collective-permute-start(f32[32,16]{1,0:T(8,128)S(1)} %shard_map.60), channel_id=1, source_target_pairs={{0,4},{4,0},{8,12},{12,8},{16,20},{20,16},{24,28},{28,24},{1,5},{5... | collective-permute-start | bytes 6152 | tf_op jit(solution)/shard_map/ppermute | solution.py:23
  99.8 4.8 %collective-permute-start.15 = (f32[32,16]{1,0:T(8,128)S(1)}, f32[32,16]{1,0:T(8,128)S(1)}, u32[]{:S(2)}, u32[]{:S(2)}) collective-permute-start(f32[32,16]{1,0:T(8,128)S(1)} %add.36), channel_id=1, source_target_pairs={{0,8},{4,12},{8,0},{12,4},{16,24},{20,28},{24,16},{28,20},{1,9},{5... | collective-permute-start | bytes 6152 | tf_op jit(solution)/shard_map/ppermute | solution.py:23
  104.6 5.9 %collective-permute-start.16 = (f32[32,16]{1,0:T(8,128)S(1)}, f32[32,16]{1,0:T(8,128)S(1)}, u32[]{:S(2)}, u32[]{:S(2)}) collective-permute-start(f32[32,16]{1,0:T(8,128)S(1)} %add.37), channel_id=1, source_target_pairs={{0,16},{4,20},{8,24},{12,28},{16,0},{20,4},{24,8},{28,12},{1,17},{... | collective-permute-start | bytes 6152 | tf_op jit(solution)/shard_map/ppermute | solution.py:23

commit v4 on v3

--- a/solution.py
+++ b/solution.py
@@ -333,7 +333,7 @@
         blocks = by_hops(start, needed, reach)
         early = {at: blocks.pop(at) for at in list(blocks) if at[0] == 0 or (at[0] == 2 and at[1])}
         total = traces(None, early)
-    next_ones = {at: blocks.pop(at) for at in list(blocks) if at[0] == 1 and at[1]}
+    next_ones = {at: blocks.pop(at) for at in list(blocks) if at[0] == 1}
     total = traces(total, next_ones)
     total = traces(total, blocks, last=True)
 

time: 116 us -> 116 us (level)
  waiting for transfers between devices: 36.5 us -> 34.1 us
    ppermute x9, waiting for transfers between devices: 17.2 us -> 15.5 us  [sent(): lax.ppermute(value, 'src', [(at, (at + steps) % count) for at in sources])]
  transfers between devices with their start and end apart: 17 -> 17, of which waited for: 7 -> 7; matrix products, arithmetic and copies ran while one was open for 3% -> 3% of each run, Pallas kernels for 11% -> 13%
where the time goes in v4:
time: 116 us; the launch traced here: 115 us
  waiting for transfers between devices  34.1 us (29%)
  blocking collectives  31.7 us (27%)
  starting transfers between devices  25.7 us (22%)
  Pallas kernels  19.3 us (17%)
  local copies, waits for them, and re-layouts  3.26 us (3%)
    all_to_all x1, blocking collectives, body(): rows_in = lax.all_to_all(sheared, 'src', 0, 0)  27.4 us
    pallas_call x3, Pallas kernels, add_traces(): pl.pallas_call(functools.partial(trace_kernel, units, bool(before), len(e...  18.9 us
    ppermute x9, waiting for transfers between devices, sent(): lax.ppermute(value, 'src', [(at, (at + steps) % count) for at in sources])  15.5 us
    ppermute x9, starting transfers between devices, sent(): lax.ppermute(value, 'src', [(at, (at + steps) % count) for at in sources])  15.2 us
    ppermute x4, waiting for transfers between devices, shifted(): return lax.ppermute(value, axis, pairs)  12.2 us
    ppermute x4, starting transfers between devices, crossed(): lax.ppermute(value, axis, [(source, source ^ mask) for source in range(co...  8.43 us
    ppermute x4, waiting for transfers between devices, crossed(): lax.ppermute(value, axis, [(source, source ^ mask) for source in range(co...  6.34 us
    all_gather x1, blocking collectives, body(): gathered = lax.all_gather(total, 'snk', axis=0)  4.36 us
  transfers between devices with their start and end apart: 17, of which 7 were waited for; matrix products, arithmetic and copies ran while one was open for 3% of the time, Pallas kernels for 13%

profile of v4, /device:TPU:0, one launch (start us, length us, event | category | flops | bytes accessed | tf_op | source)
XLA Modules:
  0.0 115.3 jit_solution(6096859323059213334)
XLA Ops:
  0.0 0.0 copy-start
  0.0 0.5 collective-permute-start.3
  0.5 0.0 copy-start.2
  0.5 1.4 %constant_dynamic-slice_fusion = bf16[2,4,256,256]{3,2,1,0:T(8,128)(2,1)S(1)} fusion(bf16[3,8,256,256]{3,2,1,0:T(8,128)(2,1)} %param.6, s32[]{:T(128)S(6)} %add.43, s32[]{:T(128)S(6)} %select_n.17), kind=kLoop, calls=%fused_computation.15 | loop fusion | bytes 2097160 | tf_op jit(solution)/shard_map/slice | solution.py:309
  1.9 1.5 %dynamic-slice_bitcast_fusion = (bf16[4,256,256]{2,1,0:T(8,128)(2,1)S(1)}, bf16[4,256,256]{2,1,0:T(8,128)(2,1)S(1)}, bf16[4,256,256]{2,1,0:T(8,128)(2,1)S(1)}) fusion(bf16[3,8,256,256]{3,2,1,0:T(8,128)(2,1)} %param.6, s32[]{:T(128)S(6)} %add.45, s32[]{:T(128)S(6)} %select_n.17, s32[]{:T(128)S(6)} %add.43), kind=kLoop, calls=%fused_computation.1 | loop fusion | bytes 3145740 | tf_op jit(solution)/shard_map/squeeze | solution.py:308
  3.3 0.0 copy-done.2
  3.4 0.1 shard_map.55
  3.4 27.4 %all_to_all.5 = bf16[8,3,2,32,256]{4,3,2,1,0:T(8,128)(2,1)S(1)} all-to-all(bf16[8,3,2,32,256]{4,3,2,1,0:T(8,128)(2,1)S(1)} %shard_map.55), channel_id=1, replica_groups=mesh['src'=8,'snk'=2,'mom'=2] {'src'}, dimensions={0} | all-to-all | bytes 1572864 | tf_op jit(solution)/shard_map/all_to_all | solution.py:312
  30.8 0.1 copy.12
  30.9 1.6 %collective-permute-start = (bf16[3,2,256,256]{3,2,1,0:T(8,128)(2,1)S(1)}, bf16[3,2,256,256]{3,2,1,0:T(8,128)(2,1)S(1)}, u32[]{:S(2)}, u32[]{:S(2)}) collective-permute-start(bf16[3,2,256,256]{3,2,1,0:T(8,128)(2,1)S(1)} %bitcast.23), channel_id=1, source_target_pairs={{0,2},{2,0},{1,3},{3,1},{4,6},{6,4},{5,7},{7,5},{8,10},{10,8},{9,1... | collective-permute-start | bytes 2359304 | tf_op jit(solution)/shard_map/ppermute | solution.py:18
  32.5 0.0 collective-permute-done.3.refs_2_.refs_3_
  32.5 1.1 collective-permute-start.4
  33.6 0.0 collective-permute-start.1
  33.6 0.4 collective-permute-start.9
  34.0 3.6 %collective-permute-start.7 = (bf16[2,4,256,256]{3,2,1,0:T(8,128)(2,1)S(1)}, bf16[2,4,256,256]{3,2,1,0:T(8,128)(2,1)S(1)}, u32[]{:S(2)}, u32[]{:S(2)}) collective-permute-start(bf16[2,4,256,256]{3,2,1,0:T(8,128)(2,1)S(1)} %constant_dynamic-slice_fusion), channel_id=1, source_target_pairs={{0,4},{8,12},{16,20},{24,28},{1,5},{9,13},{17,21},{25,29},{2,6},{1... | collective-permute-start | bytes 3145736 | tf_op jit(solution)/shard_map/ppermute | solution.py:29
  37.6 12.2 %collective-permute-done.refs_1_ = bf16[3,2,256,256]{3,2,1,0:T(8,128)(2,1)S(1)} collective-permute-done((bf16[3,2,256,256]{3,2,1,0:T(8,128)(2,1)S(1)}, bf16[3,2,256,256]{3,2,1,0:T(8,128)(2,1)S(1)}, u32[]{:S(2)}, u32[]{:S(2)}) %collective-permute-start) | collective-permute-done | bytes 786464 | tf_op jit(solution)/shard_map/ppermute | solution.py:18
  49.8 0.5 collective-permute-start.5
  50.2 0.0 collective-permute-done.4.refs_6_.odd_ref
  50.2 0.0 collective-permute-start.2
  50.2 0.0 collective-permute-done.9.even_ref.refs_8_
  50.3 0.1 shard_map.58
  50.3 0.0 copy-start.1
  50.3 1.6 %collective-permute-start.10 = (bf16[4,256,256]{2,1,0:T(8,128)(2,1)S(1)}, bf16[4,256,256]{2,1,0:T(8,128)(2,1)S(1)}, u32[]{:S(2)}, u32[]{:S(2)}) collective-permute-start(bf16[4,256,256]{2,1,0:T(8,128)(2,1)S(1)} %shard_map.58), channel_id=1, source_target_pairs={{0,8},{4,12},{8,16},{12,20},{16,24},{20,28},{24,0},{28,4},{1,9},{5... | collective-permute-start | bytes 1572872 | tf_op jit(solution)/shard_map/ppermute | solution.py:29
  51.9 0.0 collective-permute-done.1.refs_2_
  51.9 1.3 %collective-permute-start.6 = (bf16[4,256,256]{2,1,0:T(8,128)(2,1)S(1)}, bf16[4,256,256]{2,1,0:T(8,128)(2,1)S(1)}, u32[]{:S(2)}, u32[]{:S(2)}) collective-permute-start(bf16[4,256,256]{2,1,0:T(8,128)(2,1)S(1)} %collective-permute-done.4.refs_6_.odd_ref), channel_id=1, source_target_pairs={{4,0},{12,8},{20,16},{28,24},{5,1},{13,9},{21,17},{29,25},{6,2},{1... | collective-permute-start | bytes 1572872 | tf_op jit(solution)/shard_map/ppermute | solution.py:29
  53.2 13.2 %collective-permute-done.5.refs_7_ = bf16[4,256,256]{2,1,0:T(8,128)(2,1)S(1)} collective-permute-done((bf16[4,256,256]{2,1,0:T(8,128)(2,1)S(1)}, bf16[4,256,256]{2,1,0:T(8,128)(2,1)S(1)}, u32[]{:S(2)}, u32[]{:S(2)}) %collective-permute-start.5) | collective-permute-done | bytes 524320 | tf_op jit(solution)/shard_map/ppermute | solution.py:29
  66.4 1.3 %collective-permute-start.8 = (bf16[4,256,256]{2,1,0:T(8,128)(2,1)S(1)}, bf16[4,256,256]{2,1,0:T(8,128)(2,1)S(1)}, u32[]{:S(2)}, u32[]{:S(2)}) collective-permute-start(bf16[4,256,256]{2,1,0:T(8,128)(2,1)S(1)} %collective-permute-done.5.refs_7_), channel_id=1, source_target_pairs={{4,0},{12,8},{20,16},{28,24},{5,1},{13,9},{21,17},{29,25},{6,2},{1... | collective-permute-start | bytes 1572872 | tf_op jit(solution)/shard_map/ppermute | solution.py:29
  67.7 0.0 collective-permute-done.2.refs_3_
  67.7 0.2 shard_map.56.refs_0_.refs_1_
  68.0 0.1 collective-permute-start.11
  68.0 0.0 copy-done.1
  68.0 6.0 %shard_map.57.refs_0_ = f32[512,256]{1,0:T(8,128)S(1)} custom-call(bf16[3,8,256,256]{3,2,1,0:T(8,128)(2,1)S(1)} %shard_map.56.refs_0_.refs_1_, bf16[3,8,256,256]{3,2,1,0:T(8,128)(2,1)S(1)} %copy-done.1, bf16[3,8,256,256]{3,2,1,0:T(8,128)(2,1)S(1)} %collective-permute-done.3.refs_2_.refs_3_, bf16[4,256,256]{2,1,0:T(8,128)(2,1)S(1)} %get-tuple-element.20.refs_3_, ...), custom_call_target="tpu_custom_call" | custom-call | bytes 1000 | tf_op jit(solution)/shard_map/pallas_call | solution.py:220
  74.1 0.0 collective-permute-done.7.refs_5_
  74.1 4.6 %collective-permute-start.13 = (bf16[4,256,256]{2,1,0:T(8,128)(2,1)S(1)}, bf16[4,256,256]{2,1,0:T(8,128)(2,1)S(1)}, u32[]{:S(2)}, u32[]{:S(2)}) collective-permute-start(bf16[4,256,256]{2,1,0:T(8,128)(2,1)S(1)} %collective-permute-done.4.refs_6_.odd_ref), channel_id=1, source_target_pairs={{0,4},{8,12},{16,20},{24,28},{1,5},{9,13},{17,21},{25,29},{2,6},{1... | collective-permute-start | bytes 1572872 | tf_op jit(solution)/shard_map/ppermute | solution.py:29
  78.7 0.0 collective-permute-done.10.refs_7_
  78.7 0.0 collective-permute-done.6.refs_4_
  78.7 0.3 collective-permute-done.8.refs_6_
  79.1 1.3 %collective-permute-start.12 = (bf16[4,256,256]{2,1,0:T(8,128)(2,1)S(1)}, bf16[4,256,256]{2,1,0:T(8,128)(2,1)S(1)}, u32[]{:S(2)}, u32[]{:S(2)}) collective-permute-start(bf16[4,256,256]{2,1,0:T(8,128)(2,1)S(1)} %collective-permute-done.10.refs_7_), channel_id=1, source_target_pairs={{4,0},{12,8},{20,16},{28,24},{5,1},{13,9},{21,17},{29,25},{6,2},{1... | collective-permute-start | bytes 1572872 | tf_op jit(solution)/shard_map/ppermute | solution.py:29
  80.4 8.4 %shard_map.59.refs_0_ = f32[512,256]{1,0:T(8,128)S(1)} custom-call(f32[512,256]{1,0:T(8,128)S(1)} %shard_map.57.refs_0_, bf16[3,8,256,256]{3,2,1,0:T(8,128)(2,1)S(1)} %shard_map.56.refs_0_.refs_1_, bf16[3,8,256,256]{3,2,1,0:T(8,128)(2,1)S(1)} %copy-done.1, bf16[3,8,256,256]{3,2,1,0:T(8,128)(2,1)S(1)} %collective-permute-done.3.refs_2_.refs_3_, ...), custom_call_target="tpu_custom_call" | custom-call | bytes 1000 | tf_op jit(solution)/shard_map/pallas_call | solution.py:220
  88.8 0.0 copy-start.3
  88.8 0.0 collective-permute-done.11.refs_4_
  88.8 0.0 collective-permute-done.13.refs_6_
  88.8 2.0 %collective-permute-done.12.refs_5_ = bf16[4,256,256]{2,1,0:T(8,128)(2,1)S(1)} collective-permute-done((bf16[4,256,256]{2,1,0:T(8,128)(2,1)S(1)}, bf16[4,256,256]{2,1,0:T(8,128)(2,1)S(1)}, u32[]{:S(2)}, u32[]{:S(2)}) %collective-permute-start.12) | collective-permute-done | bytes 524320 | tf_op jit(solution)/shard_map/ppermute | solution.py:29
  90.8 4.5 %shard_map.60 = f32[32,16]{1,0:T(8,128)S(1)} custom-call(f32[512,256]{1,0:T(8,128)S(1)} %shard_map.59.refs_0_, bf16[3,8,256,256]{3,2,1,0:T(8,128)(2,1)S(1)} %shard_map.56.refs_0_.refs_1_, bf16[3,8,256,256]{3,2,1,0:T(8,128)(2,1)S(1)} %copy-done.1, bf16[3,8,256,256]{3,2,1,0:T(8,128)(2,1)S(1)} %collective-permute-done.3.refs_2_.refs_3_, ...), custom_call_target="tpu_custom_call" | custom-call | bytes 1000 | tf_op jit(solution)/shard_map/pallas_call | solution.py:220
  95.3 0.8 collective-permute-start.14
  96.1 3.0 %collective-permute-done.14 = f32[32,16]{1,0:T(8,128)S(1)} collective-permute-done((f32[32,16]{1,0:T(8,128)S(1)}, f32[32,16]{1,0:T(8,128)S(1)}, u32[]{:S(2)}, u32[]{:S(2)}) %collective-permute-start.14) | collective-permute-done | bytes 2080 | tf_op jit(solution)/shard_map/ppermute | solution.py:23
  99.1 3.1 %collective-permute-start.15 = (f32[32,16]{1,0:T(8,128)S(1)}, f32[32,16]{1,0:T(8,128)S(1)}, u32[]{:S(2)}, u32[]{:S(2)}) collective-permute-start(f32[32,16]{1,0:T(8,128)S(1)} %add.36), channel_id=1, source_target_pairs={{0,8},{4,12},{8,0},{12,4},{16,24},{20,28},{24,16},{28,20},{1,9},{5... | collective-permute-start | bytes 6152 | tf_op jit(solution)/shard_map/ppermute | solution.py:23
  102.1 1.7 %collective-permute-done.15 = f32[32,16]{1,0:T(8,128)S(1)} collective-permute-done((f32[32,16]{1,0:T(8,128)S(1)}, f32[32,16]{1,0:T(8,128)S(1)}, u32[]{:S(2)}, u32[]{:S(2)}) %collective-permute-start.15) | collective-permute-done | bytes 2080 | tf_op jit(solution)/shard_map/ppermute | solution.py:23
  103.8 4.1 %collective-permute-start.16 = (f32[32,16]{1,0:T(8,128)S(1)}, f32[32,16]{1,0:T(8,128)S(1)}, u32[]{:S(2)}, u32[]{:S(2)}) collective-permute-start(f32[32,16]{1,0:T(8,128)S(1)} %add.37), channel_id=1, source_target_pairs={{0,16},{4,20},{8,24},{12,28},{16,0},{20,4},{24,8},{28,12},{1,17},{... | collective-permute-start | bytes 6152 | tf_op jit(solution)/shard_map/ppermute | solution.py:23
  108.0 0.0 copy-done.3
  108.0 0.1 dynamic_slice.7
  108.1 1.6 %collective-permute-done.16 = f32[32,16]{1,0:T(8,128)S(1)} collective-permute-done((f32[32,16]{1,0:T(8,128)S(1)}, f32[32,16]{1,0:T(8,128)S(1)}, u32[]{:S(2)}, u32[]{:S(2)}) %collective-permute-start.16) | collective-permute-done | bytes 2080 | tf_op jit(solution)/shard_map/ppermute | solution.py:23
  109.7 0.1 copy.13
  109.8 4.4 %all-gather.1 = f32[2,32,16]{1,2,0:T(8,128)S(1)} all-gather(f32[1,32,16]{1,2,0:T(8,128)S(1)} %copy.13), channel_id=2, replica_groups=mesh['src'=8,'snk'=2,'mom'=2] {'snk'}, dimensions={0}, use_global_device_ids=true | all-gather | bytes 6144 | tf_op jit(solution)/shard_map/all_gather | solution.py:345
  114.1 0.1 copy.14
  114.2 0.2 convolution_multiply_fusion
  114.4 0.1 copy.16
  114.5 0.0 copy-done
  114.5 0.8 fusion.1
  (4 shorter events, 0.0 us)
Async XLA Ops:
  0.0 114.5 %copy-start = (f32[8,128]{1,0:T(8,128)S(1)}, f32[8,128]{1,0:T(8,128)}, u32[]{:S(2)}) copy-start(f32[8,128]{1,0:T(8,128)} %param.9) | copy-start | bytes 12292
  0.0 32.5 %collective-permute-start.3 = (bf16[3,8,256,256]{3,2,1,0:T(8,128)(2,1)}, bf16[3,8,256,256]{3,2,1,0:T(8,128)(2,1)S(1)}, u32[]{:S(2)}, u32[]{:S(2)}) collective-permute-start(bf16[3,8,256,256]{3,2,1,0:T(8,128)(2,1)} %refs_2_.3), channel_id=1, source_target_pairs={{0,1},{1,0},{2,3},{3,2},{4,5},{5,4},{6,7},{7,6},{8,9},{9,8},{10,11... | collective-permute-start | bytes 9437192 | tf_op jit(solution)/shard_map/ppermute | solution.py:18
  0.5 2.9 %copy-start.2 = (bf16[24,4,32,256]{3,2,1,0:T(8,128)(2,1)S(1)}, bf16[24,4,32,256]{3,2,1,0:T(8,128)(2,1)}, u32[]{:S(2)}) copy-start(bf16[24,4,32,256]{3,2,1,0:T(8,128)(2,1)} %peramb_ref) | copy-start | bytes 4718596
  30.9 18.9 %collective-permute-start = (bf16[3,2,256,256]{3,2,1,0:T(8,128)(2,1)S(1)}, bf16[3,2,256,256]{3,2,1,0:T(8,128)(2,1)S(1)}, u32[]{:S(2)}, u32[]{:S(2)}) collective-permute-start(bf16[3,2,256,256]{3,2,1,0:T(8,128)(2,1)S(1)} %bitcast.23), channel_id=1, source_target_pairs={{0,2},{2,0},{1,3},{3,1},{4,6},{6,4},{5,7},{7,5},{8,10},{10,8},{9,1... | collective-permute-start | bytes 2359304 | tf_op jit(solution)/shard_map/ppermute | solution.py:18
  32.5 17.8 %collective-permute-start.4 = (bf16[4,256,256]{2,1,0:T(8,128)(2,1)S(1)}, bf16[4,256,256]{2,1,0:T(8,128)(2,1)S(1)}, u32[]{:S(2)}, u32[]{:S(2)}) collective-permute-start(bf16[4,256,256]{2,1,0:T(8,128)(2,1)S(1)} %get-tuple-element.20.refs_3_), channel_id=1, source_target_pairs={{0,8},{4,12},{8,16},{12,20},{16,24},{20,28},{24,0},{28,4},{1,9},{5... | collective-permute-start | bytes 1572872 | tf_op jit(solution)/shard_map/ppermute | solution.py:29
  33.6 18.3 %collective-permute-start.1 = (bf16[3,2,256,256]{3,2,1,0:T(8,128)(2,1)S(1)}, bf16[3,2,256,256]{3,2,1,0:T(8,128)(2,1)S(1)}, u32[]{:S(2)}, u32[]{:S(2)}) collective-permute-start(bf16[3,2,256,256]{3,2,1,0:T(8,128)(2,1)S(1)} %bitcast.24), channel_id=1, source_target_pairs={{0,1},{1,0},{2,3},{3,2},{4,5},{5,4},{6,7},{7,6},{8,9},{9,8},{10,11... | collective-permute-start | bytes 2359304 | tf_op jit(solution)/shard_map/ppermute | solution.py:18
  33.6 16.7 %collective-permute-start.9 = (bf16[4,256,256]{2,1,0:T(8,128)(2,1)S(1)}, bf16[4,256,256]{2,1,0:T(8,128)(2,1)S(1)}, u32[]{:S(2)}, u32[]{:S(2)}) collective-permute-start(bf16[4,256,256]{2,1,0:T(8,128)(2,1)S(1)} %get-tuple-element.28.refs_5_), channel_id=1, source_target_pairs={{0,4},{4,0},{8,12},{12,8},{16,20},{20,16},{24,28},{28,24},{1,5},{5... | collective-permute-start | bytes 1572872 | tf_op jit(solution)/shard_map/ppermute | solution.py:23
  34.0 40.1 %collective-permute-start.7 = (bf16[2,4,256,256]{3,2,1,0:T(8,128)(2,1)S(1)}, bf16[2,4,256,256]{3,2,1,0:T(8,128)(2,1)S(1)}, u32[]{:S(2)}, u32[]{:S(2)}) collective-permute-start(bf16[2,4,256,256]{3,2,1,0:T(8,128)(2,1)S(1)} %constant_dynamic-slice_fusion), channel_id=1, source_target_pairs={{0,4},{8,12},{16,20},{24,28},{1,5},{9,13},{17,21},{25,29},{2,6},{1... | collective-permute-start | bytes 3145736 | tf_op jit(solution)/shard_map/ppermute | solution.py:29
  49.8 16.7 %collective-permute-start.5 = (bf16[4,256,256]{2,1,0:T(8,128)(2,1)S(1)}, bf16[4,256,256]{2,1,0:T(8,128)(2,1)S(1)}, u32[]{:S(2)}, u32[]{:S(2)}) collective-permute-start(bf16[4,256,256]{2,1,0:T(8,128)(2,1)S(1)} %get-tuple-element.22.refs_4_), channel_id=1, source_target_pairs={{0,8},{4,12},{8,16},{12,20},{16,24},{20,28},{24,0},{28,4},{1,9},{5... | collective-permute-start | bytes 1572872 | tf_op jit(solution)/shard_map/ppermute | solution.py:29
  50.2 17.5 %collective-permute-start.2 = (bf16[3,2,256,256]{3,2,1,0:T(8,128)(2,1)S(1)}, bf16[3,2,256,256]{3,2,1,0:T(8,128)(2,1)S(1)}, u32[]{:S(2)}, u32[]{:S(2)}) collective-permute-start(bf16[3,2,256,256]{3,2,1,0:T(8,128)(2,1)S(1)} %collective-permute-done.refs_1_), channel_id=1, source_target_pairs={{0,1},{1,0},{2,3},{3,2},{4,5},{5,4},{6,7},{7,6},{8,9},{9,8},{10,11... | collective-permute-start | bytes 2359304 | tf_op jit(solution)/shard_map/ppermute | solution.py:18
  50.3 17.7 %copy-start.1 = (bf16[3,8,256,256]{3,2,1,0:T(8,128)(2,1)S(1)}, bf16[3,8,256,256]{3,2,1,0:T(8,128)(2,1)}, u32[]{:S(2)}) copy-start(bf16[3,8,256,256]{3,2,1,0:T(8,128)(2,1)} %refs_2_.3) | copy-start | bytes 9437188
  50.3 28.4 %collective-permute-start.10 = (bf16[4,256,256]{2,1,0:T(8,128)(2,1)S(1)}, bf16[4,256,256]{2,1,0:T(8,128)(2,1)S(1)}, u32[]{:S(2)}, u32[]{:S(2)}) collective-permute-start(bf16[4,256,256]{2,1,0:T(8,128)(2,1)S(1)} %shard_map.58), channel_id=1, source_target_pairs={{0,8},{4,12},{8,16},{12,20},{16,24},{20,28},{24,0},{28,4},{1,9},{5... | collective-permute-start | bytes 1572872 | tf_op jit(solution)/shard_map/ppermute | solution.py:29
  51.9 26.8 %collective-permute-start.6 = (bf16[4,256,256]{2,1,0:T(8,128)(2,1)S(1)}, bf16[4,256,256]{2,1,0:T(8,128)(2,1)S(1)}, u32[]{:S(2)}, u32[]{:S(2)}) collective-permute-start(bf16[4,256,256]{2,1,0:T(8,128)(2,1)S(1)} %collective-permute-done.4.refs_6_.odd_ref), channel_id=1, source_target_pairs={{4,0},{12,8},{20,16},{28,24},{5,1},{13,9},{21,17},{29,25},{6,2},{1... | collective-permute-start | bytes 1572872 | tf_op jit(solution)/shard_map/ppermute | solution.py:29
  66.4 12.6 %collective-permute-start.8 = (bf16[4,256,256]{2,1,0:T(8,128)(2,1)S(1)}, bf16[4,256,256]{2,1,0:T(8,128)(2,1)S(1)}, u32[]{:S(2)}, u32[]{:S(2)}) collective-permute-start(bf16[4,256,256]{2,1,0:T(8,128)(2,1)S(1)} %collective-permute-done.5.refs_7_), channel_id=1, source_target_pairs={{4,0},{12,8},{20,16},{28,24},{5,1},{13,9},{21,17},{29,25},{6,2},{1... | collective-permute-start | bytes 1572872 | tf_op jit(solution)/shard_map/ppermute | solution.py:29
  68.0 20.9 %collective-permute-start.11 = (bf16[4,256,256]{2,1,0:T(8,128)(2,1)S(1)}, bf16[4,256,256]{2,1,0:T(8,128)(2,1)S(1)}, u32[]{:S(2)}, u32[]{:S(2)}) collective-permute-start(bf16[4,256,256]{2,1,0:T(8,128)(2,1)S(1)} %get-tuple-element.28.refs_5_), channel_id=1, source_target_pairs={{0,8},{4,12},{8,16},{12,20},{16,24},{20,28},{24,0},{28,4},{1,9},{5... | collective-permute-start | bytes 1572872 | tf_op jit(solution)/shard_map/ppermute | solution.py:29
  74.1 14.7 %collective-permute-start.13 = (bf16[4,256,256]{2,1,0:T(8,128)(2,1)S(1)}, bf16[4,256,256]{2,1,0:T(8,128)(2,1)S(1)}, u32[]{:S(2)}, u32[]{:S(2)}) collective-permute-start(bf16[4,256,256]{2,1,0:T(8,128)(2,1)S(1)} %collective-permute-done.4.refs_6_.odd_ref), channel_id=1, source_target_pairs={{0,4},{8,12},{16,20},{24,28},{1,5},{9,13},{17,21},{25,29},{2,6},{1... | collective-permute-start | bytes 1572872 | tf_op jit(solution)/shard_map/ppermute | solution.py:29
  79.1 11.7 %collective-permute-start.12 = (bf16[4,256,256]{2,1,0:T(8,128)(2,1)S(1)}, bf16[4,256,256]{2,1,0:T(8,128)(2,1)S(1)}, u32[]{:S(2)}, u32[]{:S(2)}) collective-permute-start(bf16[4,256,256]{2,1,0:T(8,128)(2,1)S(1)} %collective-permute-done.10.refs_7_), channel_id=1, source_target_pairs={{4,0},{12,8},{20,16},{28,24},{5,1},{13,9},{21,17},{29,25},{6,2},{1... | collective-permute-start | bytes 1572872 | tf_op jit(solution)/shard_map/ppermute | solution.py:29
  88.8 19.2 %copy-start.3 = (s32[64]{0:T(128)S(1)}, s32[64]{0:T(128)}, u32[]{:S(2)}) copy-start(s32[64]{0:T(128)} %param.8) | copy-start | bytes 772
  95.3 3.8 %collective-permute-start.14 = (f32[32,16]{1,0:T(8,128)S(1)}, f32[32,16]{1,0:T(8,128)S(1)}, u32[]{:S(2)}, u32[]{:S(2)}) collective-permute-start(f32[32,16]{1,0:T(8,128)S(1)} %shard_map.60), channel_id=1, source_target_pairs={{0,4},{4,0},{8,12},{12,8},{16,20},{20,16},{24,28},{28,24},{1,5},{5... | collective-permute-start | bytes 6152 | tf_op jit(solution)/shard_map/ppermute | solution.py:23
  99.1 4.8 %collective-permute-start.15 = (f32[32,16]{1,0:T(8,128)S(1)}, f32[32,16]{1,0:T(8,128)S(1)}, u32[]{:S(2)}, u32[]{:S(2)}) collective-permute-start(f32[32,16]{1,0:T(8,128)S(1)} %add.36), channel_id=1, source_target_pairs={{0,8},{4,12},{8,0},{12,4},{16,24},{20,28},{24,16},{28,20},{1,9},{5... | collective-permute-start | bytes 6152 | tf_op jit(solution)/shard_map/ppermute | solution.py:23
  103.8 5.9 %collective-permute-start.16 = (f32[32,16]{1,0:T(8,128)S(1)}, f32[32,16]{1,0:T(8,128)S(1)}, u32[]{:S(2)}, u32[]{:S(2)}) collective-permute-start(f32[32,16]{1,0:T(8,128)S(1)} %add.37), channel_id=1, source_target_pairs={{0,16},{4,20},{8,24},{12,28},{16,0},{20,4},{24,8},{28,12},{1,17},{... | collective-permute-start | bytes 6152 | tf_op jit(solution)/shard_map/ppermute | solution.py:23

commit v5 on v4

--- a/solution.py
+++ b/solution.py
@@ -337,12 +337,14 @@
     total = traces(total, next_ones)
     total = traces(total, blocks, last=True)
 
-    if n_src == 8:
-        for step in (1, 2, 4):
-            total = total + crossed(total, "src", step)
+    if n_src == 8 and n_snk == 2:
+        pairs = [(at, at ^ 3) for at in range(n_src * n_snk)]
+        other = shifted(total, "snk", 1) + lax.ppermute(total, ("src", "snk"), pairs)
+        mine = total + crossed(total, "src", 1)
+        both = jnp.where(y == 0, jnp.stack([mine, other]), jnp.stack([other, mine]))
+        gathered = both + crossed(both, "src", 2) + crossed(both, "src", 4) + crossed(both, "src", 6)
     else:
-        total = lax.psum(total, "src")
-    gathered = lax.all_gather(total, "snk", axis=0)
+        gathered = lax.all_gather(lax.psum(total, "src"), "snk", axis=0)
     pair_traces = gathered.reshape(n_snk, n_sep, nf, ne_part * n_mom)
     n_ops = op_elem.shape[0] // n_src
     ops = lax.dynamic_slice_in_dim(op_elem, s * n_ops, n_ops, 0)

time: 116 us -> 114 us (0.983)
  blocking collectives: 31.7 us -> 27.4 us
  waiting for transfers between devices: 34.1 us -> 35.8 us
  starting transfers between devices: 25.7 us -> 27.3 us
    all_gather x1 -> x0, blocking collectives: 4.36 us -> none  [body(): gathered = lax.all_gather(total, 'snk', axis=0)]
    ppermute x0 -> x1, waiting for transfers between devices: none -> 2.42 us  [body(): lax.ppermute(total, ('src', 'snk'), pairs)]
    ppermute x4 -> x5, starting transfers between devices: 2.04 us -> 3.56 us  [shifted(): return lax.ppermute(value, axis, pairs)]
    ppermute x4 -> x5, waiting for transfers between devices: 6.34 us -> 4.87 us  [crossed(): lax.ppermute(value, axis, [(source, source ^ mask) for source in range(co...]
    ppermute x0 -> x1, starting transfers between devices: none -> 1.23 us  [body(): lax.ppermute(total, ('src', 'snk'), pairs)]
    ppermute x4 -> x5, starting transfers between devices: 8.43 us -> 7.28 us  [crossed(): lax.ppermute(value, axis, [(source, source ^ mask) for source in range(co...]
    ppermute x4 -> x5, waiting for transfers between devices: 12.2 us -> 12.9 us  [shifted(): return lax.ppermute(value, axis, pairs)]
  transfers between devices with their start and end apart: 17 -> 20, of which waited for: 7 -> 9; matrix products, arithmetic and copies ran while one was open for 3% -> 3% of each run, Pallas kernels for 13% -> 13%
where the time goes in v5:
time: 114 us
  waiting for transfers between devices  35.8 us (31%)
  blocking collectives  27.4 us (24%)
  starting transfers between devices  27.3 us (24%)
  Pallas kernels  19.3 us (17%)
  local copies, waits for them, and re-layouts  3.12 us (3%)
    all_to_all x1, blocking collectives, body(): rows_in = lax.all_to_all(sheared, 'src', 0, 0)  27.4 us
    pallas_call x3, Pallas kernels, add_traces(): pl.pallas_call(functools.partial(trace_kernel, units, bool(before), len(e...  18.9 us
    ppermute x9, waiting for transfers between devices, sent(): lax.ppermute(value, 'src', [(at, (at + steps) % count) for at in sources])  15.5 us
    ppermute x9, starting transfers between devices, sent(): lax.ppermute(value, 'src', [(at, (at + steps) % count) for at in sources])  15.2 us
    ppermute x5, waiting for transfers between devices, shifted(): return lax.ppermute(value, axis, pairs)  12.9 us
    ppermute x5, starting transfers between devices, crossed(): lax.ppermute(value, axis, [(source, source ^ mask) for source in range(co...  7.28 us
    ppermute x5, waiting for transfers between devices, crossed(): lax.ppermute(value, axis, [(source, source ^ mask) for source in range(co...  4.87 us
    ppermute x5, starting transfers between devices, shifted(): return lax.ppermute(value, axis, pairs)  3.56 us
  transfers between devices with their start and end apart: 20, of which 9 were waited for; matrix products, arithmetic and copies ran while one was open for 3% of the time, Pallas kernels for 13%

profile of v5, /device:TPU:0, one launch (start us, length us, event | category | flops | bytes accessed | tf_op | source)
XLA Modules:
  0.0 114.1 jit_solution(17845234034863079787)
XLA Ops:
  0.0 0.0 copy-start
  0.0 0.5 collective-permute-start.3
  0.5 0.0 copy-start.2
  0.5 1.4 %constant_dynamic-slice_fusion = bf16[2,4,256,256]{3,2,1,0:T(8,128)(2,1)S(1)} fusion(bf16[3,8,256,256]{3,2,1,0:T(8,128)(2,1)} %param.6, s32[]{:T(128)S(6)} %add.51, s32[]{:T(128)S(6)} %select_n.26), kind=kLoop, calls=%fused_computation.18 | loop fusion | bytes 2097160 | tf_op jit(solution)/shard_map/slice | solution.py:309
  1.9 1.5 %dynamic-slice_bitcast_fusion = (bf16[4,256,256]{2,1,0:T(8,128)(2,1)S(1)}, bf16[4,256,256]{2,1,0:T(8,128)(2,1)S(1)}, bf16[4,256,256]{2,1,0:T(8,128)(2,1)S(1)}) fusion(bf16[3,8,256,256]{3,2,1,0:T(8,128)(2,1)} %param.6, s32[]{:T(128)S(6)} %add.53, s32[]{:T(128)S(6)} %select_n.26, s32[]{:T(128)S(6)} %add.51), kind=kLoop, calls=%fused_computation.1 | loop fusion | bytes 3145740 | tf_op jit(solution)/shard_map/squeeze | solution.py:308
  3.3 0.0 copy-done.2
  3.4 0.1 shard_map.55
  3.4 27.4 %all_to_all.5 = bf16[8,3,2,32,256]{4,3,2,1,0:T(8,128)(2,1)S(1)} all-to-all(bf16[8,3,2,32,256]{4,3,2,1,0:T(8,128)(2,1)S(1)} %shard_map.55), channel_id=1, replica_groups=mesh['src'=8,'snk'=2,'mom'=2] {'src'}, dimensions={0} | all-to-all | bytes 1572864 | tf_op jit(solution)/shard_map/all_to_all | solution.py:312
  30.8 0.1 copy.6
  30.9 1.6 %collective-permute-start = (bf16[3,2,256,256]{3,2,1,0:T(8,128)(2,1)S(1)}, bf16[3,2,256,256]{3,2,1,0:T(8,128)(2,1)S(1)}, u32[]{:S(2)}, u32[]{:S(2)}) collective-permute-start(bf16[3,2,256,256]{3,2,1,0:T(8,128)(2,1)S(1)} %bitcast.25), channel_id=1, source_target_pairs={{0,2},{2,0},{1,3},{3,1},{4,6},{6,4},{5,7},{7,5},{8,10},{10,8},{9,1... | collective-permute-start | bytes 2359304 | tf_op jit(solution)/shard_map/ppermute | solution.py:18
  32.5 0.0 collective-permute-done.3.refs_2_.refs_3_
  32.5 1.1 collective-permute-start.4
  33.6 0.0 collective-permute-start.1
  33.6 0.4 collective-permute-start.9
  34.0 3.6 %collective-permute-start.7 = (bf16[2,4,256,256]{3,2,1,0:T(8,128)(2,1)S(1)}, bf16[2,4,256,256]{3,2,1,0:T(8,128)(2,1)S(1)}, u32[]{:S(2)}, u32[]{:S(2)}) collective-permute-start(bf16[2,4,256,256]{3,2,1,0:T(8,128)(2,1)S(1)} %constant_dynamic-slice_fusion), channel_id=1, source_target_pairs={{0,4},{8,12},{16,20},{24,28},{1,5},{9,13},{17,21},{25,29},{2,6},{1... | collective-permute-start | bytes 3145736 | tf_op jit(solution)/shard_map/ppermute | solution.py:29
  37.6 12.2 %collective-permute-done.refs_1_ = bf16[3,2,256,256]{3,2,1,0:T(8,128)(2,1)S(1)} collective-permute-done((bf16[3,2,256,256]{3,2,1,0:T(8,128)(2,1)S(1)}, bf16[3,2,256,256]{3,2,1,0:T(8,128)(2,1)S(1)}, u32[]{:S(2)}, u32[]{:S(2)}) %collective-permute-start) | collective-permute-done | bytes 786464 | tf_op jit(solution)/shard_map/ppermute | solution.py:18
  49.8 0.5 collective-permute-start.5
  50.2 0.0 collective-permute-done.4.refs_6_.odd_ref
  50.2 0.0 collective-permute-start.2
  50.2 0.0 collective-permute-done.9.even_ref.refs_8_
  50.3 0.1 shard_map.58
  50.3 0.0 copy-start.1
  50.3 1.6 %collective-permute-start.10 = (bf16[4,256,256]{2,1,0:T(8,128)(2,1)S(1)}, bf16[4,256,256]{2,1,0:T(8,128)(2,1)S(1)}, u32[]{:S(2)}, u32[]{:S(2)}) collective-permute-start(bf16[4,256,256]{2,1,0:T(8,128)(2,1)S(1)} %shard_map.58), channel_id=1, source_target_pairs={{0,8},{4,12},{8,16},{12,20},{16,24},{20,28},{24,0},{28,4},{1,9},{5... | collective-permute-start | bytes 1572872 | tf_op jit(solution)/shard_map/ppermute | solution.py:29
  51.9 0.0 collective-permute-done.1.refs_2_
  51.9 1.3 %collective-permute-start.6 = (bf16[4,256,256]{2,1,0:T(8,128)(2,1)S(1)}, bf16[4,256,256]{2,1,0:T(8,128)(2,1)S(1)}, u32[]{:S(2)}, u32[]{:S(2)}) collective-permute-start(bf16[4,256,256]{2,1,0:T(8,128)(2,1)S(1)} %collective-permute-done.4.refs_6_.odd_ref), channel_id=1, source_target_pairs={{4,0},{12,8},{20,16},{28,24},{5,1},{13,9},{21,17},{29,25},{6,2},{1... | collective-permute-start | bytes 1572872 | tf_op jit(solution)/shard_map/ppermute | solution.py:29
  53.2 13.2 %collective-permute-done.5.refs_7_ = bf16[4,256,256]{2,1,0:T(8,128)(2,1)S(1)} collective-permute-done((bf16[4,256,256]{2,1,0:T(8,128)(2,1)S(1)}, bf16[4,256,256]{2,1,0:T(8,128)(2,1)S(1)}, u32[]{:S(2)}, u32[]{:S(2)}) %collective-permute-start.5) | collective-permute-done | bytes 524320 | tf_op jit(solution)/shard_map/ppermute | solution.py:29
  66.4 1.3 %collective-permute-start.8 = (bf16[4,256,256]{2,1,0:T(8,128)(2,1)S(1)}, bf16[4,256,256]{2,1,0:T(8,128)(2,1)S(1)}, u32[]{:S(2)}, u32[]{:S(2)}) collective-permute-start(bf16[4,256,256]{2,1,0:T(8,128)(2,1)S(1)} %collective-permute-done.5.refs_7_), channel_id=1, source_target_pairs={{4,0},{12,8},{20,16},{28,24},{5,1},{13,9},{21,17},{29,25},{6,2},{1... | collective-permute-start | bytes 1572872 | tf_op jit(solution)/shard_map/ppermute | solution.py:29
  67.7 0.0 collective-permute-done.2.refs_3_
  67.7 0.2 shard_map.56.refs_0_.refs_1_
  68.0 0.1 collective-permute-start.11
  68.0 0.0 copy-done.1
  68.0 6.0 %shard_map.57.refs_0_ = f32[512,256]{1,0:T(8,128)S(1)} custom-call(bf16[3,8,256,256]{3,2,1,0:T(8,128)(2,1)S(1)} %shard_map.56.refs_0_.refs_1_, bf16[3,8,256,256]{3,2,1,0:T(8,128)(2,1)S(1)} %copy-done.1, bf16[3,8,256,256]{3,2,1,0:T(8,128)(2,1)S(1)} %collective-permute-done.3.refs_2_.refs_3_, bf16[4,256,256]{2,1,0:T(8,128)(2,1)S(1)} %get-tuple-element.20.refs_3_, ...), custom_call_target="tpu_custom_call" | custom-call | bytes 1000 | tf_op jit(solution)/shard_map/pallas_call | solution.py:220
  74.1 0.0 collective-permute-done.7.refs_5_
  74.1 4.6 %collective-permute-start.13 = (bf16[4,256,256]{2,1,0:T(8,128)(2,1)S(1)}, bf16[4,256,256]{2,1,0:T(8,128)(2,1)S(1)}, u32[]{:S(2)}, u32[]{:S(2)}) collective-permute-start(bf16[4,256,256]{2,1,0:T(8,128)(2,1)S(1)} %collective-permute-done.4.refs_6_.odd_ref), channel_id=1, source_target_pairs={{0,4},{8,12},{16,20},{24,28},{1,5},{9,13},{17,21},{25,29},{2,6},{1... | collective-permute-start | bytes 1572872 | tf_op jit(solution)/shard_map/ppermute | solution.py:29
  78.7 0.0 collective-permute-done.10.refs_7_
  78.7 0.0 collective-permute-done.6.refs_4_
  78.7 0.3 collective-permute-done.8.refs_6_
  79.1 1.3 %collective-permute-start.12 = (bf16[4,256,256]{2,1,0:T(8,128)(2,1)S(1)}, bf16[4,256,256]{2,1,0:T(8,128)(2,1)S(1)}, u32[]{:S(2)}, u32[]{:S(2)}) collective-permute-start(bf16[4,256,256]{2,1,0:T(8,128)(2,1)S(1)} %collective-permute-done.10.refs_7_), channel_id=1, source_target_pairs={{4,0},{12,8},{20,16},{28,24},{5,1},{13,9},{21,17},{29,25},{6,2},{1... | collective-permute-start | bytes 1572872 | tf_op jit(solution)/shard_map/ppermute | solution.py:29
  80.4 8.4 %shard_map.59.refs_0_ = f32[512,256]{1,0:T(8,128)S(1)} custom-call(f32[512,256]{1,0:T(8,128)S(1)} %shard_map.57.refs_0_, bf16[3,8,256,256]{3,2,1,0:T(8,128)(2,1)S(1)} %shard_map.56.refs_0_.refs_1_, bf16[3,8,256,256]{3,2,1,0:T(8,128)(2,1)S(1)} %copy-done.1, bf16[3,8,256,256]{3,2,1,0:T(8,128)(2,1)S(1)} %collective-permute-done.3.refs_2_.refs_3_, ...), custom_call_target="tpu_custom_call" | custom-call | bytes 1000 | tf_op jit(solution)/shard_map/pallas_call | solution.py:220
  88.8 0.0 copy-start.3
  88.8 0.0 collective-permute-done.11.refs_4_
  88.8 0.0 collective-permute-done.13.refs_6_
  88.8 2.0 %collective-permute-done.12.refs_5_ = bf16[4,256,256]{2,1,0:T(8,128)(2,1)S(1)} collective-permute-done((bf16[4,256,256]{2,1,0:T(8,128)(2,1)S(1)}, bf16[4,256,256]{2,1,0:T(8,128)(2,1)S(1)}, u32[]{:S(2)}, u32[]{:S(2)}) %collective-permute-start.12) | collective-permute-done | bytes 524320 | tf_op jit(solution)/shard_map/ppermute | solution.py:29
  90.8 4.5 %shard_map.60 = f32[32,16]{1,0:T(8,128)S(1)} custom-call(f32[512,256]{1,0:T(8,128)S(1)} %shard_map.59.refs_0_, bf16[3,8,256,256]{3,2,1,0:T(8,128)(2,1)S(1)} %shard_map.56.refs_0_.refs_1_, bf16[3,8,256,256]{3,2,1,0:T(8,128)(2,1)S(1)} %copy-done.1, bf16[3,8,256,256]{3,2,1,0:T(8,128)(2,1)S(1)} %collective-permute-done.3.refs_2_.refs_3_, ...), custom_call_target="tpu_custom_call" | custom-call | bytes 1000 | tf_op jit(solution)/shard_map/pallas_call | solution.py:220
  95.3 0.8 collective-permute-start.14
  96.1 1.5 %collective-permute-start.15 = (f32[32,16]{1,0:T(8,128)S(1)}, f32[32,16]{1,0:T(8,128)S(1)}, u32[]{:S(2)}, u32[]{:S(2)}) collective-permute-start(f32[32,16]{1,0:T(8,128)S(1)} %shard_map.60), channel_id=1, source_target_pairs={{0,2},{2,0},{1,3},{3,1},{4,6},{6,4},{5,7},{7,5},{8,10},{10,8},{9,1... | collective-permute-start | bytes 6152 | tf_op jit(solution)/shard_map/ppermute | solution.py:18
  97.6 1.2 %collective-permute-start.16 = (f32[32,16]{1,0:T(8,128)S(1)}, f32[32,16]{1,0:T(8,128)S(1)}, u32[]{:S(2)}, u32[]{:S(2)}) collective-permute-start(f32[32,16]{1,0:T(8,128)S(1)} %shard_map.60), channel_id=1, source_target_pairs={{0,6},{2,4},{4,2},{6,0},{8,14},{10,12},{12,10},{14,8},{16,22},{18,... | collective-permute-start | bytes 6152 | tf_op jit(solution)/shard_map/ppermute | solution.py:342
  98.8 0.2 collective-permute-done.14
  99.1 0.7 collective-permute-done.15
  99.8 2.4 %collective-permute-done.16 = f32[32,16]{1,0:T(8,128)S(1)} collective-permute-done((f32[32,16]{1,0:T(8,128)S(1)}, f32[32,16]{1,0:T(8,128)S(1)}, u32[]{:S(2)}, u32[]{:S(2)}) %collective-permute-start.16) | collective-permute-done | bytes 2080 | tf_op jit(solution)/shard_map/ppermute | solution.py:342
  102.2 2.5 %collective-permute-start.17 = (f32[2,32,16]{2,1,0:T(8,128)S(1)}, f32[2,32,16]{2,1,0:T(8,128)S(1)}, u32[]{:S(2)}, u32[]{:S(2)}) collective-permute-start(f32[2,32,16]{2,1,0:T(8,128)S(1)} %maximum_select_fusion), channel_id=1, source_target_pairs={{0,8},{4,12},{8,0},{12,4},{16,24},{20,28},{24,16},{28,20},{1,9},{5... | collective-permute-start | bytes 12296 | tf_op jit(solution)/shard_map/ppermute | solution.py:23
  104.7 2.6 %collective-permute-start.18 = (f32[2,32,16]{2,1,0:T(8,128)S(1)}, f32[2,32,16]{2,1,0:T(8,128)S(1)}, u32[]{:S(2)}, u32[]{:S(2)}) collective-permute-start(f32[2,32,16]{2,1,0:T(8,128)S(1)} %maximum_select_fusion), channel_id=1, source_target_pairs={{0,16},{4,20},{8,24},{12,28},{16,0},{20,4},{24,8},{28,12},{1,17},{... | collective-permute-start | bytes 12296 | tf_op jit(solution)/shard_map/ppermute | solution.py:23
  107.3 1.0 collective-permute-start.19
  108.3 0.0 copy-done.3
  108.3 0.1 dynamic_slice.7
  108.4 0.0 collective-permute-done.17
  108.4 1.1 collective-permute-done.18
  109.5 3.5 %collective-permute-done.19 = f32[2,32,16]{2,1,0:T(8,128)S(1)} collective-permute-done((f32[2,32,16]{2,1,0:T(8,128)S(1)}, f32[2,32,16]{2,1,0:T(8,128)S(1)}, u32[]{:S(2)}, u32[]{:S(2)}) %collective-permute-start.19) | collective-permute-done | bytes 4128 | tf_op jit(solution)/shard_map/ppermute | solution.py:23
  113.0 0.2 convolution_multiply_fusion
  113.2 0.1 copy.8
  113.3 0.0 copy-done
  113.3 0.8 fusion.1
  (5 shorter events, 0.0 us)
Async XLA Ops:
  0.0 113.3 %copy-start = (f32[8,128]{1,0:T(8,128)S(1)}, f32[8,128]{1,0:T(8,128)}, u32[]{:S(2)}) copy-start(f32[8,128]{1,0:T(8,128)} %param.9) | copy-start | bytes 12292
  0.0 32.5 %collective-permute-start.3 = (bf16[3,8,256,256]{3,2,1,0:T(8,128)(2,1)}, bf16[3,8,256,256]{3,2,1,0:T(8,128)(2,1)S(1)}, u32[]{:S(2)}, u32[]{:S(2)}) collective-permute-start(bf16[3,8,256,256]{3,2,1,0:T(8,128)(2,1)} %refs_2_.3), channel_id=1, source_target_pairs={{0,1},{1,0},{2,3},{3,2},{4,5},{5,4},{6,7},{7,6},{8,9},{9,8},{10,11... | collective-permute-start | bytes 9437192 | tf_op jit(solution)/shard_map/ppermute | solution.py:18
  0.5 2.9 %copy-start.2 = (bf16[24,4,32,256]{3,2,1,0:T(8,128)(2,1)S(1)}, bf16[24,4,32,256]{3,2,1,0:T(8,128)(2,1)}, u32[]{:S(2)}) copy-start(bf16[24,4,32,256]{3,2,1,0:T(8,128)(2,1)} %peramb_ref) | copy-start | bytes 4718596
  30.9 18.9 %collective-permute-start = (bf16[3,2,256,256]{3,2,1,0:T(8,128)(2,1)S(1)}, bf16[3,2,256,256]{3,2,1,0:T(8,128)(2,1)S(1)}, u32[]{:S(2)}, u32[]{:S(2)}) collective-permute-start(bf16[3,2,256,256]{3,2,1,0:T(8,128)(2,1)S(1)} %bitcast.25), channel_id=1, source_target_pairs={{0,2},{2,0},{1,3},{3,1},{4,6},{6,4},{5,7},{7,5},{8,10},{10,8},{9,1... | collective-permute-start | bytes 2359304 | tf_op jit(solution)/shard_map/ppermute | solution.py:18
  32.5 17.8 %collective-permute-start.4 = (bf16[4,256,256]{2,1,0:T(8,128)(2,1)S(1)}, bf16[4,256,256]{2,1,0:T(8,128)(2,1)S(1)}, u32[]{:S(2)}, u32[]{:S(2)}) collective-permute-start(bf16[4,256,256]{2,1,0:T(8,128)(2,1)S(1)} %get-tuple-element.20.refs_3_), channel_id=1, source_target_pairs={{0,8},{4,12},{8,16},{12,20},{16,24},{20,28},{24,0},{28,4},{1,9},{5... | collective-permute-start | bytes 1572872 | tf_op jit(solution)/shard_map/ppermute | solution.py:29
  33.6 18.3 %collective-permute-start.1 = (bf16[3,2,256,256]{3,2,1,0:T(8,128)(2,1)S(1)}, bf16[3,2,256,256]{3,2,1,0:T(8,128)(2,1)S(1)}, u32[]{:S(2)}, u32[]{:S(2)}) collective-permute-start(bf16[3,2,256,256]{3,2,1,0:T(8,128)(2,1)S(1)} %bitcast.26), channel_id=1, source_target_pairs={{0,1},{1,0},{2,3},{3,2},{4,5},{5,4},{6,7},{7,6},{8,9},{9,8},{10,11... | collective-permute-start | bytes 2359304 | tf_op jit(solution)/shard_map/ppermute | solution.py:18
  33.6 16.7 %collective-permute-start.9 = (bf16[4,256,256]{2,1,0:T(8,128)(2,1)S(1)}, bf16[4,256,256]{2,1,0:T(8,128)(2,1)S(1)}, u32[]{:S(2)}, u32[]{:S(2)}) collective-permute-start(bf16[4,256,256]{2,1,0:T(8,128)(2,1)S(1)} %get-tuple-element.28.refs_5_), channel_id=1, source_target_pairs={{0,4},{4,0},{8,12},{12,8},{16,20},{20,16},{24,28},{28,24},{1,5},{5... | collective-permute-start | bytes 1572872 | tf_op jit(solution)/shard_map/ppermute | solution.py:23
  34.0 40.1 %collective-permute-start.7 = (bf16[2,4,256,256]{3,2,1,0:T(8,128)(2,1)S(1)}, bf16[2,4,256,256]{3,2,1,0:T(8,128)(2,1)S(1)}, u32[]{:S(2)}, u32[]{:S(2)}) collective-permute-start(bf16[2,4,256,256]{3,2,1,0:T(8,128)(2,1)S(1)} %constant_dynamic-slice_fusion), channel_id=1, source_target_pairs={{0,4},{8,12},{16,20},{24,28},{1,5},{9,13},{17,21},{25,29},{2,6},{1... | collective-permute-start | bytes 3145736 | tf_op jit(solution)/shard_map/ppermute | solution.py:29
  49.8 16.7 %collective-permute-start.5 = (bf16[4,256,256]{2,1,0:T(8,128)(2,1)S(1)}, bf16[4,256,256]{2,1,0:T(8,128)(2,1)S(1)}, u32[]{:S(2)}, u32[]{:S(2)}) collective-permute-start(bf16[4,256,256]{2,1,0:T(8,128)(2,1)S(1)} %get-tuple-element.22.refs_4_), channel_id=1, source_target_pairs={{0,8},{4,12},{8,16},{12,20},{16,24},{20,28},{24,0},{28,4},{1,9},{5... | collective-permute-start | bytes 1572872 | tf_op jit(solution)/shard_map/ppermute | solution.py:29
  50.2 17.5 %collective-permute-start.2 = (bf16[3,2,256,256]{3,2,1,0:T(8,128)(2,1)S(1)}, bf16[3,2,256,256]{3,2,1,0:T(8,128)(2,1)S(1)}, u32[]{:S(2)}, u32[]{:S(2)}) collective-permute-start(bf16[3,2,256,256]{3,2,1,0:T(8,128)(2,1)S(1)} %collective-permute-done.refs_1_), channel_id=1, source_target_pairs={{0,1},{1,0},{2,3},{3,2},{4,5},{5,4},{6,7},{7,6},{8,9},{9,8},{10,11... | collective-permute-start | bytes 2359304 | tf_op jit(solution)/shard_map/ppermute | solution.py:18
  50.3 17.7 %copy-start.1 = (bf16[3,8,256,256]{3,2,1,0:T(8,128)(2,1)S(1)}, bf16[3,8,256,256]{3,2,1,0:T(8,128)(2,1)}, u32[]{:S(2)}) copy-start(bf16[3,8,256,256]{3,2,1,0:T(8,128)(2,1)} %refs_2_.3) | copy-start | bytes 9437188
  50.3 28.4 %collective-permute-start.10 = (bf16[4,256,256]{2,1,0:T(8,128)(2,1)S(1)}, bf16[4,256,256]{2,1,0:T(8,128)(2,1)S(1)}, u32[]{:S(2)}, u32[]{:S(2)}) collective-permute-start(bf16[4,256,256]{2,1,0:T(8,128)(2,1)S(1)} %shard_map.58), channel_id=1, source_target_pairs={{0,8},{4,12},{8,16},{12,20},{16,24},{20,28},{24,0},{28,4},{1,9},{5... | collective-permute-start | bytes 1572872 | tf_op jit(solution)/shard_map/ppermute | solution.py:29
  51.9 26.8 %collective-permute-start.6 = (bf16[4,256,256]{2,1,0:T(8,128)(2,1)S(1)}, bf16[4,256,256]{2,1,0:T(8,128)(2,1)S(1)}, u32[]{:S(2)}, u32[]{:S(2)}) collective-permute-start(bf16[4,256,256]{2,1,0:T(8,128)(2,1)S(1)} %collective-permute-done.4.refs_6_.odd_ref), channel_id=1, source_target_pairs={{4,0},{12,8},{20,16},{28,24},{5,1},{13,9},{21,17},{29,25},{6,2},{1... | collective-permute-start | bytes 1572872 | tf_op jit(solution)/shard_map/ppermute | solution.py:29
  66.4 12.6 %collective-permute-start.8 = (bf16[4,256,256]{2,1,0:T(8,128)(2,1)S(1)}, bf16[4,256,256]{2,1,0:T(8,128)(2,1)S(1)}, u32[]{:S(2)}, u32[]{:S(2)}) collective-permute-start(bf16[4,256,256]{2,1,0:T(8,128)(2,1)S(1)} %collective-permute-done.5.refs_7_), channel_id=1, source_target_pairs={{4,0},{12,8},{20,16},{28,24},{5,1},{13,9},{21,17},{29,25},{6,2},{1... | collective-permute-start | bytes 1572872 | tf_op jit(solution)/shard_map/ppermute | solution.py:29
  68.0 20.9 %collective-permute-start.11 = (bf16[4,256,256]{2,1,0:T(8,128)(2,1)S(1)}, bf16[4,256,256]{2,1,0:T(8,128)(2,1)S(1)}, u32[]{:S(2)}, u32[]{:S(2)}) collective-permute-start(bf16[4,256,256]{2,1,0:T(8,128)(2,1)S(1)} %get-tuple-element.28.refs_5_), channel_id=1, source_target_pairs={{0,8},{4,12},{8,16},{12,20},{16,24},{20,28},{24,0},{28,4},{1,9},{5... | collective-permute-start | bytes 1572872 | tf_op jit(solution)/shard_map/ppermute | solution.py:29
  74.1 14.7 %collective-permute-start.13 = (bf16[4,256,256]{2,1,0:T(8,128)(2,1)S(1)}, bf16[4,256,256]{2,1,0:T(8,128)(2,1)S(1)}, u32[]{:S(2)}, u32[]{:S(2)}) collective-permute-start(bf16[4,256,256]{2,1,0:T(8,128)(2,1)S(1)} %collective-permute-done.4.refs_6_.odd_ref), channel_id=1, source_target_pairs={{0,4},{8,12},{16,20},{24,28},{1,5},{9,13},{17,21},{25,29},{2,6},{1... | collective-permute-start | bytes 1572872 | tf_op jit(solution)/shard_map/ppermute | solution.py:29
  79.1 11.7 %collective-permute-start.12 = (bf16[4,256,256]{2,1,0:T(8,128)(2,1)S(1)}, bf16[4,256,256]{2,1,0:T(8,128)(2,1)S(1)}, u32[]{:S(2)}, u32[]{:S(2)}) collective-permute-start(bf16[4,256,256]{2,1,0:T(8,128)(2,1)S(1)} %collective-permute-done.10.refs_7_), channel_id=1, source_target_pairs={{4,0},{12,8},{20,16},{28,24},{5,1},{13,9},{21,17},{29,25},{6,2},{1... | collective-permute-start | bytes 1572872 | tf_op jit(solution)/shard_map/ppermute | solution.py:29
  88.8 19.5 %copy-start.3 = (s32[64]{0:T(128)S(1)}, s32[64]{0:T(128)}, u32[]{:S(2)}) copy-start(s32[64]{0:T(128)} %param.8) | copy-start | bytes 772
  95.3 3.8 %collective-permute-start.14 = (f32[32,16]{1,0:T(8,128)S(1)}, f32[32,16]{1,0:T(8,128)S(1)}, u32[]{:S(2)}, u32[]{:S(2)}) collective-permute-start(f32[32,16]{1,0:T(8,128)S(1)} %shard_map.60), channel_id=1, source_target_pairs={{0,4},{4,0},{8,12},{12,8},{16,20},{20,16},{24,28},{28,24},{1,5},{5... | collective-permute-start | bytes 6152 | tf_op jit(solution)/shard_map/ppermute | solution.py:23
  96.1 3.7 %collective-permute-start.15 = (f32[32,16]{1,0:T(8,128)S(1)}, f32[32,16]{1,0:T(8,128)S(1)}, u32[]{:S(2)}, u32[]{:S(2)}) collective-permute-start(f32[32,16]{1,0:T(8,128)S(1)} %shard_map.60), channel_id=1, source_target_pairs={{0,2},{2,0},{1,3},{3,1},{4,6},{6,4},{5,7},{7,5},{8,10},{10,8},{9,1... | collective-permute-start | bytes 6152 | tf_op jit(solution)/shard_map/ppermute | solution.py:18
  97.6 4.6 %collective-permute-start.16 = (f32[32,16]{1,0:T(8,128)S(1)}, f32[32,16]{1,0:T(8,128)S(1)}, u32[]{:S(2)}, u32[]{:S(2)}) collective-permute-start(f32[32,16]{1,0:T(8,128)S(1)} %shard_map.60), channel_id=1, source_target_pairs={{0,6},{2,4},{4,2},{6,0},{8,14},{10,12},{12,10},{14,8},{16,22},{18,... | collective-permute-start | bytes 6152 | tf_op jit(solution)/shard_map/ppermute | solution.py:342
  102.2 6.1 %collective-permute-start.17 = (f32[2,32,16]{2,1,0:T(8,128)S(1)}, f32[2,32,16]{2,1,0:T(8,128)S(1)}, u32[]{:S(2)}, u32[]{:S(2)}) collective-permute-start(f32[2,32,16]{2,1,0:T(8,128)S(1)} %maximum_select_fusion), channel_id=1, source_target_pairs={{0,8},{4,12},{8,0},{12,4},{16,24},{20,28},{24,16},{28,20},{1,9},{5... | collective-permute-start | bytes 12296 | tf_op jit(solution)/shard_map/ppermute | solution.py:23
  104.7 4.8 %collective-permute-start.18 = (f32[2,32,16]{2,1,0:T(8,128)S(1)}, f32[2,32,16]{2,1,0:T(8,128)S(1)}, u32[]{:S(2)}, u32[]{:S(2)}) collective-permute-start(f32[2,32,16]{2,1,0:T(8,128)S(1)} %maximum_select_fusion), channel_id=1, source_target_pairs={{0,16},{4,20},{8,24},{12,28},{16,0},{20,4},{24,8},{28,12},{1,17},{... | collective-permute-start | bytes 12296 | tf_op jit(solution)/shard_map/ppermute | solution.py:23
  107.3 5.7 %collective-permute-start.19 = (f32[2,32,16]{2,1,0:T(8,128)S(1)}, f32[2,32,16]{2,1,0:T(8,128)S(1)}, u32[]{:S(2)}, u32[]{:S(2)}) collective-permute-start(f32[2,32,16]{2,1,0:T(8,128)S(1)} %maximum_select_fusion), channel_id=1, source_target_pairs={{0,24},{4,28},{8,16},{12,20},{16,8},{20,12},{24,0},{28,4},{1,25},{... | collective-permute-start | bytes 12296 | tf_op jit(solution)/shard_map/ppermute | solution.py:23

commit v6 on v5

--- a/solution.py
+++ b/solution.py
@@ -342,7 +342,8 @@
         other = shifted(total, "snk", 1) + lax.ppermute(total, ("src", "snk"), pairs)
         mine = total + crossed(total, "src", 1)
         both = jnp.where(y == 0, jnp.stack([mine, other]), jnp.stack([other, mine]))
-        gathered = both + crossed(both, "src", 2) + crossed(both, "src", 4) + crossed(both, "src", 6)
+        both = both + crossed(both, "src", 2)
+        gathered = both + crossed(both, "src", 4)
     else:
         gathered = lax.all_gather(lax.psum(total, "src"), "snk", axis=0)
     pair_traces = gathered.reshape(n_snk, n_sep, nf, ne_part * n_mom)

time: 114 us -> 114 us (level)
    ppermute x5 -> x4, starting transfers between devices: 7.28 us -> 7.9 us  [crossed(): lax.ppermute(value, axis, [(source, source ^ mask) for source in range(co...]
    ppermute x5 -> x4, waiting for transfers between devices: 4.87 us -> 4.3 us  [crossed(): lax.ppermute(value, axis, [(source, source ^ mask) for source in range(co...]
  transfers between devices with their start and end apart: 20 -> 19, of which waited for: 9 -> 9; matrix products, arithmetic and copies ran while one was open for 3% -> 3% of each run, Pallas kernels for 13% -> 13%
where the time goes in v6:
time: 114 us
  waiting for transfers between devices  35.2 us (31%)
  starting transfers between devices  27.9 us (24%)
  blocking collectives  27.4 us (24%)
  Pallas kernels  19.3 us (17%)
  local copies, waits for them, and re-layouts  3.12 us (3%)
    all_to_all x1, blocking collectives, body(): rows_in = lax.all_to_all(sheared, 'src', 0, 0)  27.4 us
    pallas_call x3, Pallas kernels, add_traces(): pl.pallas_call(functools.partial(trace_kernel, units, bool(before), len(e...  18.9 us
    ppermute x9, waiting for transfers between devices, sent(): lax.ppermute(value, 'src', [(at, (at + steps) % count) for at in sources])  15.5 us
    ppermute x9, starting transfers between devices, sent(): lax.ppermute(value, 'src', [(at, (at + steps) % count) for at in sources])  15.2 us
    ppermute x5, waiting for transfers between devices, shifted(): return lax.ppermute(value, axis, pairs)  12.9 us
    ppermute x4, starting transfers between devices, crossed(): lax.ppermute(value, axis, [(source, source ^ mask) for source in range(co...  7.9 us
    ppermute x4, waiting for transfers between devices, crossed(): lax.ppermute(value, axis, [(source, source ^ mask) for source in range(co...  4.3 us
    ppermute x5, starting transfers between devices, shifted(): return lax.ppermute(value, axis, pairs)  3.56 us
  transfers between devices with their start and end apart: 19, of which 9 were waited for; matrix products, arithmetic and copies ran while one was open for 3% of the time, Pallas kernels for 13%

profile of v6, /device:TPU:0, one launch (start us, length us, event | category | flops | bytes accessed | tf_op | source)
XLA Modules:
  0.0 114.1 jit_solution(3552078799289571246)
XLA Ops:
  0.0 0.0 copy-start
  0.0 0.5 collective-permute-start.3
  0.5 0.0 copy-start.2
  0.5 1.4 %constant_dynamic-slice_fusion = bf16[2,4,256,256]{3,2,1,0:T(8,128)(2,1)S(1)} fusion(bf16[3,8,256,256]{3,2,1,0:T(8,128)(2,1)} %param.6, s32[]{:T(128)S(6)} %add.47, s32[]{:T(128)S(6)} %select_n.26), kind=kLoop, calls=%fused_computation.17 | loop fusion | bytes 2097160 | tf_op jit(solution)/shard_map/slice | solution.py:309
  1.9 1.5 %dynamic-slice_bitcast_fusion = (bf16[4,256,256]{2,1,0:T(8,128)(2,1)S(1)}, bf16[4,256,256]{2,1,0:T(8,128)(2,1)S(1)}, bf16[4,256,256]{2,1,0:T(8,128)(2,1)S(1)}) fusion(bf16[3,8,256,256]{3,2,1,0:T(8,128)(2,1)} %param.6, s32[]{:T(128)S(6)} %add.49, s32[]{:T(128)S(6)} %select_n.26, s32[]{:T(128)S(6)} %add.47), kind=kLoop, calls=%fused_computation.1 | loop fusion | bytes 3145740 | tf_op jit(solution)/shard_map/squeeze | solution.py:308
  3.3 0.0 copy-done.2
  3.4 0.1 shard_map.55
  3.4 27.4 %all_to_all.5 = bf16[8,3,2,32,256]{4,3,2,1,0:T(8,128)(2,1)S(1)} all-to-all(bf16[8,3,2,32,256]{4,3,2,1,0:T(8,128)(2,1)S(1)} %shard_map.55), channel_id=1, replica_groups=mesh['src'=8,'snk'=2,'mom'=2] {'src'}, dimensions={0} | all-to-all | bytes 1572864 | tf_op jit(solution)/shard_map/all_to_all | solution.py:312
  30.8 0.1 copy.6
  30.9 1.6 %collective-permute-start = (bf16[3,2,256,256]{3,2,1,0:T(8,128)(2,1)S(1)}, bf16[3,2,256,256]{3,2,1,0:T(8,128)(2,1)S(1)}, u32[]{:S(2)}, u32[]{:S(2)}) collective-permute-start(bf16[3,2,256,256]{3,2,1,0:T(8,128)(2,1)S(1)} %bitcast.25), channel_id=1, source_target_pairs={{0,2},{2,0},{1,3},{3,1},{4,6},{6,4},{5,7},{7,5},{8,10},{10,8},{9,1... | collective-permute-start | bytes 2359304 | tf_op jit(solution)/shard_map/ppermute | solution.py:18
  32.5 0.0 collective-permute-done.3.refs_2_.refs_3_
  32.5 1.1 collective-permute-start.4
  33.6 0.0 collective-permute-start.1
  33.6 0.4 collective-permute-start.9
  34.0 3.6 %collective-permute-start.7 = (bf16[2,4,256,256]{3,2,1,0:T(8,128)(2,1)S(1)}, bf16[2,4,256,256]{3,2,1,0:T(8,128)(2,1)S(1)}, u32[]{:S(2)}, u32[]{:S(2)}) collective-permute-start(bf16[2,4,256,256]{3,2,1,0:T(8,128)(2,1)S(1)} %constant_dynamic-slice_fusion), channel_id=1, source_target_pairs={{0,4},{8,12},{16,20},{24,28},{1,5},{9,13},{17,21},{25,29},{2,6},{1... | collective-permute-start | bytes 3145736 | tf_op jit(solution)/shard_map/ppermute | solution.py:29
  37.6 12.2 %collective-permute-done.refs_1_ = bf16[3,2,256,256]{3,2,1,0:T(8,128)(2,1)S(1)} collective-permute-done((bf16[3,2,256,256]{3,2,1,0:T(8,128)(2,1)S(1)}, bf16[3,2,256,256]{3,2,1,0:T(8,128)(2,1)S(1)}, u32[]{:S(2)}, u32[]{:S(2)}) %collective-permute-start) | collective-permute-done | bytes 786464 | tf_op jit(solution)/shard_map/ppermute | solution.py:18
  49.8 0.5 collective-permute-start.5
  50.2 0.0 collective-permute-done.4.refs_6_.odd_ref
  50.2 0.0 collective-permute-start.2
  50.2 0.0 collective-permute-done.9.even_ref.refs_8_
  50.3 0.1 shard_map.58
  50.3 0.0 copy-start.1
  50.3 1.6 %collective-permute-start.10 = (bf16[4,256,256]{2,1,0:T(8,128)(2,1)S(1)}, bf16[4,256,256]{2,1,0:T(8,128)(2,1)S(1)}, u32[]{:S(2)}, u32[]{:S(2)}) collective-permute-start(bf16[4,256,256]{2,1,0:T(8,128)(2,1)S(1)} %shard_map.58), channel_id=1, source_target_pairs={{0,8},{4,12},{8,16},{12,20},{16,24},{20,28},{24,0},{28,4},{1,9},{5... | collective-permute-start | bytes 1572872 | tf_op jit(solution)/shard_map/ppermute | solution.py:29
  51.9 0.0 collective-permute-done.1.refs_2_
  51.9 1.3 %collective-permute-start.6 = (bf16[4,256,256]{2,1,0:T(8,128)(2,1)S(1)}, bf16[4,256,256]{2,1,0:T(8,128)(2,1)S(1)}, u32[]{:S(2)}, u32[]{:S(2)}) collective-permute-start(bf16[4,256,256]{2,1,0:T(8,128)(2,1)S(1)} %collective-permute-done.4.refs_6_.odd_ref), channel_id=1, source_target_pairs={{4,0},{12,8},{20,16},{28,24},{5,1},{13,9},{21,17},{29,25},{6,2},{1... | collective-permute-start | bytes 1572872 | tf_op jit(solution)/shard_map/ppermute | solution.py:29
  53.2 13.2 %collective-permute-done.5.refs_7_ = bf16[4,256,256]{2,1,0:T(8,128)(2,1)S(1)} collective-permute-done((bf16[4,256,256]{2,1,0:T(8,128)(2,1)S(1)}, bf16[4,256,256]{2,1,0:T(8,128)(2,1)S(1)}, u32[]{:S(2)}, u32[]{:S(2)}) %collective-permute-start.5) | collective-permute-done | bytes 524320 | tf_op jit(solution)/shard_map/ppermute | solution.py:29
  66.4 1.3 %collective-permute-start.8 = (bf16[4,256,256]{2,1,0:T(8,128)(2,1)S(1)}, bf16[4,256,256]{2,1,0:T(8,128)(2,1)S(1)}, u32[]{:S(2)}, u32[]{:S(2)}) collective-permute-start(bf16[4,256,256]{2,1,0:T(8,128)(2,1)S(1)} %collective-permute-done.5.refs_7_), channel_id=1, source_target_pairs={{4,0},{12,8},{20,16},{28,24},{5,1},{13,9},{21,17},{29,25},{6,2},{1... | collective-permute-start | bytes 1572872 | tf_op jit(solution)/shard_map/ppermute | solution.py:29
  67.7 0.0 collective-permute-done.2.refs_3_
  67.7 0.2 shard_map.56.refs_0_.refs_1_
  68.0 0.1 collective-permute-start.11
  68.0 0.0 copy-done.1
  68.0 6.0 %shard_map.57.refs_0_ = f32[512,256]{1,0:T(8,128)S(1)} custom-call(bf16[3,8,256,256]{3,2,1,0:T(8,128)(2,1)S(1)} %shard_map.56.refs_0_.refs_1_, bf16[3,8,256,256]{3,2,1,0:T(8,128)(2,1)S(1)} %copy-done.1, bf16[3,8,256,256]{3,2,1,0:T(8,128)(2,1)S(1)} %collective-permute-done.3.refs_2_.refs_3_, bf16[4,256,256]{2,1,0:T(8,128)(2,1)S(1)} %get-tuple-element.20.refs_3_, ...), custom_call_target="tpu_custom_call" | custom-call | bytes 1000 | tf_op jit(solution)/shard_map/pallas_call | solution.py:220
  74.1 0.0 collective-permute-done.7.refs_5_
  74.1 4.6 %collective-permute-start.13 = (bf16[4,256,256]{2,1,0:T(8,128)(2,1)S(1)}, bf16[4,256,256]{2,1,0:T(8,128)(2,1)S(1)}, u32[]{:S(2)}, u32[]{:S(2)}) collective-permute-start(bf16[4,256,256]{2,1,0:T(8,128)(2,1)S(1)} %collective-permute-done.4.refs_6_.odd_ref), channel_id=1, source_target_pairs={{0,4},{8,12},{16,20},{24,28},{1,5},{9,13},{17,21},{25,29},{2,6},{1... | collective-permute-start | bytes 1572872 | tf_op jit(solution)/shard_map/ppermute | solution.py:29
  78.7 0.0 collective-permute-done.10.refs_7_
  78.7 0.0 collective-permute-done.6.refs_4_
  78.7 0.3 collective-permute-done.8.refs_6_
  79.1 1.3 %collective-permute-start.12 = (bf16[4,256,256]{2,1,0:T(8,128)(2,1)S(1)}, bf16[4,256,256]{2,1,0:T(8,128)(2,1)S(1)}, u32[]{:S(2)}, u32[]{:S(2)}) collective-permute-start(bf16[4,256,256]{2,1,0:T(8,128)(2,1)S(1)} %collective-permute-done.10.refs_7_), channel_id=1, source_target_pairs={{4,0},{12,8},{20,16},{28,24},{5,1},{13,9},{21,17},{29,25},{6,2},{1... | collective-permute-start | bytes 1572872 | tf_op jit(solution)/shard_map/ppermute | solution.py:29
  80.4 8.4 %shard_map.59.refs_0_ = f32[512,256]{1,0:T(8,128)S(1)} custom-call(f32[512,256]{1,0:T(8,128)S(1)} %shard_map.57.refs_0_, bf16[3,8,256,256]{3,2,1,0:T(8,128)(2,1)S(1)} %shard_map.56.refs_0_.refs_1_, bf16[3,8,256,256]{3,2,1,0:T(8,128)(2,1)S(1)} %copy-done.1, bf16[3,8,256,256]{3,2,1,0:T(8,128)(2,1)S(1)} %collective-permute-done.3.refs_2_.refs_3_, ...), custom_call_target="tpu_custom_call" | custom-call | bytes 1000 | tf_op jit(solution)/shard_map/pallas_call | solution.py:220
  88.8 0.0 copy-start.3
  88.8 0.0 collective-permute-done.11.refs_4_
  88.8 0.0 collective-permute-done.13.refs_6_
  88.8 2.0 %collective-permute-done.12.refs_5_ = bf16[4,256,256]{2,1,0:T(8,128)(2,1)S(1)} collective-permute-done((bf16[4,256,256]{2,1,0:T(8,128)(2,1)S(1)}, bf16[4,256,256]{2,1,0:T(8,128)(2,1)S(1)}, u32[]{:S(2)}, u32[]{:S(2)}) %collective-permute-start.12) | collective-permute-done | bytes 524320 | tf_op jit(solution)/shard_map/ppermute | solution.py:29
  90.8 4.5 %shard_map.60 = f32[32,16]{1,0:T(8,128)S(1)} custom-call(f32[512,256]{1,0:T(8,128)S(1)} %shard_map.59.refs_0_, bf16[3,8,256,256]{3,2,1,0:T(8,128)(2,1)S(1)} %shard_map.56.refs_0_.refs_1_, bf16[3,8,256,256]{3,2,1,0:T(8,128)(2,1)S(1)} %copy-done.1, bf16[3,8,256,256]{3,2,1,0:T(8,128)(2,1)S(1)} %collective-permute-done.3.refs_2_.refs_3_, ...), custom_call_target="tpu_custom_call" | custom-call | bytes 1000 | tf_op jit(solution)/shard_map/pallas_call | solution.py:220
  95.3 0.8 collective-permute-start.14
  96.1 1.5 %collective-permute-start.15 = (f32[32,16]{1,0:T(8,128)S(1)}, f32[32,16]{1,0:T(8,128)S(1)}, u32[]{:S(2)}, u32[]{:S(2)}) collective-permute-start(f32[32,16]{1,0:T(8,128)S(1)} %shard_map.60), channel_id=1, source_target_pairs={{0,2},{2,0},{1,3},{3,1},{4,6},{6,4},{5,7},{7,5},{8,10},{10,8},{9,1... | collective-permute-start | bytes 6152 | tf_op jit(solution)/shard_map/ppermute | solution.py:18
  97.6 1.2 %collective-permute-start.16 = (f32[32,16]{1,0:T(8,128)S(1)}, f32[32,16]{1,0:T(8,128)S(1)}, u32[]{:S(2)}, u32[]{:S(2)}) collective-permute-start(f32[32,16]{1,0:T(8,128)S(1)} %shard_map.60), channel_id=1, source_target_pairs={{0,6},{2,4},{4,2},{6,0},{8,14},{10,12},{12,10},{14,8},{16,22},{18,... | collective-permute-start | bytes 6152 | tf_op jit(solution)/shard_map/ppermute | solution.py:342
  98.8 0.2 collective-permute-done.14
  99.1 0.7 collective-permute-done.15
  99.8 2.4 %collective-permute-done.16 = f32[32,16]{1,0:T(8,128)S(1)} collective-permute-done((f32[32,16]{1,0:T(8,128)S(1)}, f32[32,16]{1,0:T(8,128)S(1)}, u32[]{:S(2)}, u32[]{:S(2)}) %collective-permute-start.16) | collective-permute-done | bytes 2080 | tf_op jit(solution)/shard_map/ppermute | solution.py:342
  102.2 2.5 %collective-permute-start.17 = (f32[2,32,16]{2,1,0:T(8,128)S(1)}, f32[2,32,16]{2,1,0:T(8,128)S(1)}, u32[]{:S(2)}, u32[]{:S(2)}) collective-permute-start(f32[2,32,16]{2,1,0:T(8,128)S(1)} %maximum_select_fusion), channel_id=1, source_target_pairs={{0,8},{4,12},{8,0},{12,4},{16,24},{20,28},{24,16},{28,20},{1,9},{5... | collective-permute-start | bytes 12296 | tf_op jit(solution)/shard_map/ppermute | solution.py:23
  104.7 1.9 %collective-permute-done.17 = f32[2,32,16]{2,1,0:T(8,128)S(1)} collective-permute-done((f32[2,32,16]{2,1,0:T(8,128)S(1)}, f32[2,32,16]{2,1,0:T(8,128)S(1)}, u32[]{:S(2)}, u32[]{:S(2)}) %collective-permute-start.17) | collective-permute-done | bytes 4128 | tf_op jit(solution)/shard_map/ppermute | solution.py:23
  106.6 4.2 %collective-permute-start.18 = (f32[2,32,16]{2,1,0:T(8,128)S(1)}, f32[2,32,16]{2,1,0:T(8,128)S(1)}, u32[]{:S(2)}, u32[]{:S(2)}) collective-permute-start(f32[2,32,16]{2,1,0:T(8,128)S(1)} %fusion.9), channel_id=1, source_target_pairs={{0,16},{4,20},{8,24},{12,28},{16,0},{20,4},{24,8},{28,12},{1,17},{... | collective-permute-start | bytes 12296 | tf_op jit(solution)/shard_map/ppermute | solution.py:23
  110.8 0.0 copy-done.3
  110.8 0.1 dynamic_slice.7
  110.9 2.2 %collective-permute-done.18 = f32[2,32,16]{2,1,0:T(8,128)S(1)} collective-permute-done((f32[2,32,16]{2,1,0:T(8,128)S(1)}, f32[2,32,16]{2,1,0:T(8,128)S(1)}, u32[]{:S(2)}, u32[]{:S(2)}) %collective-permute-start.18) | collective-permute-done | bytes 4128 | tf_op jit(solution)/shard_map/ppermute | solution.py:23
  113.1 0.2 convolution_multiply_fusion
  113.3 0.1 copy.8
  113.4 0.0 copy-done
  113.4 0.8 fusion.1
  (6 shorter events, 0.0 us)
Async XLA Ops:
  0.0 113.4 %copy-start = (f32[8,128]{1,0:T(8,128)S(1)}, f32[8,128]{1,0:T(8,128)}, u32[]{:S(2)}) copy-start(f32[8,128]{1,0:T(8,128)} %param.9) | copy-start | bytes 12292
  0.0 32.5 %collective-permute-start.3 = (bf16[3,8,256,256]{3,2,1,0:T(8,128)(2,1)}, bf16[3,8,256,256]{3,2,1,0:T(8,128)(2,1)S(1)}, u32[]{:S(2)}, u32[]{:S(2)}) collective-permute-start(bf16[3,8,256,256]{3,2,1,0:T(8,128)(2,1)} %refs_2_.3), channel_id=1, source_target_pairs={{0,1},{1,0},{2,3},{3,2},{4,5},{5,4},{6,7},{7,6},{8,9},{9,8},{10,11... | collective-permute-start | bytes 9437192 | tf_op jit(solution)/shard_map/ppermute | solution.py:18
  0.5 2.9 %copy-start.2 = (bf16[24,4,32,256]{3,2,1,0:T(8,128)(2,1)S(1)}, bf16[24,4,32,256]{3,2,1,0:T(8,128)(2,1)}, u32[]{:S(2)}) copy-start(bf16[24,4,32,256]{3,2,1,0:T(8,128)(2,1)} %peramb_ref) | copy-start | bytes 4718596
  30.9 18.9 %collective-permute-start = (bf16[3,2,256,256]{3,2,1,0:T(8,128)(2,1)S(1)}, bf16[3,2,256,256]{3,2,1,0:T(8,128)(2,1)S(1)}, u32[]{:S(2)}, u32[]{:S(2)}) collective-permute-start(bf16[3,2,256,256]{3,2,1,0:T(8,128)(2,1)S(1)} %bitcast.25), channel_id=1, source_target_pairs={{0,2},{2,0},{1,3},{3,1},{4,6},{6,4},{5,7},{7,5},{8,10},{10,8},{9,1... | collective-permute-start | bytes 2359304 | tf_op jit(solution)/shard_map/ppermute | solution.py:18
  32.5 17.8 %collective-permute-start.4 = (bf16[4,256,256]{2,1,0:T(8,128)(2,1)S(1)}, bf16[4,256,256]{2,1,0:T(8,128)(2,1)S(1)}, u32[]{:S(2)}, u32[]{:S(2)}) collective-permute-start(bf16[4,256,256]{2,1,0:T(8,128)(2,1)S(1)} %get-tuple-element.20.refs_3_), channel_id=1, source_target_pairs={{0,8},{4,12},{8,16},{12,20},{16,24},{20,28},{24,0},{28,4},{1,9},{5... | collective-permute-start | bytes 1572872 | tf_op jit(solution)/shard_map/ppermute | solution.py:29
  33.6 18.3 %collective-permute-start.1 = (bf16[3,2,256,256]{3,2,1,0:T(8,128)(2,1)S(1)}, bf16[3,2,256,256]{3,2,1,0:T(8,128)(2,1)S(1)}, u32[]{:S(2)}, u32[]{:S(2)}) collective-permute-start(bf16[3,2,256,256]{3,2,1,0:T(8,128)(2,1)S(1)} %bitcast.26), channel_id=1, source_target_pairs={{0,1},{1,0},{2,3},{3,2},{4,5},{5,4},{6,7},{7,6},{8,9},{9,8},{10,11... | collective-permute-start | bytes 2359304 | tf_op jit(solution)/shard_map/ppermute | solution.py:18
  33.6 16.7 %collective-permute-start.9 = (bf16[4,256,256]{2,1,0:T(8,128)(2,1)S(1)}, bf16[4,256,256]{2,1,0:T(8,128)(2,1)S(1)}, u32[]{:S(2)}, u32[]{:S(2)}) collective-permute-start(bf16[4,256,256]{2,1,0:T(8,128)(2,1)S(1)} %get-tuple-element.28.refs_5_), channel_id=1, source_target_pairs={{0,4},{4,0},{8,12},{12,8},{16,20},{20,16},{24,28},{28,24},{1,5},{5... | collective-permute-start | bytes 1572872 | tf_op jit(solution)/shard_map/ppermute | solution.py:23
  34.0 40.1 %collective-permute-start.7 = (bf16[2,4,256,256]{3,2,1,0:T(8,128)(2,1)S(1)}, bf16[2,4,256,256]{3,2,1,0:T(8,128)(2,1)S(1)}, u32[]{:S(2)}, u32[]{:S(2)}) collective-permute-start(bf16[2,4,256,256]{3,2,1,0:T(8,128)(2,1)S(1)} %constant_dynamic-slice_fusion), channel_id=1, source_target_pairs={{0,4},{8,12},{16,20},{24,28},{1,5},{9,13},{17,21},{25,29},{2,6},{1... | collective-permute-start | bytes 3145736 | tf_op jit(solution)/shard_map/ppermute | solution.py:29
  49.8 16.7 %collective-permute-start.5 = (bf16[4,256,256]{2,1,0:T(8,128)(2,1)S(1)}, bf16[4,256,256]{2,1,0:T(8,128)(2,1)S(1)}, u32[]{:S(2)}, u32[]{:S(2)}) collective-permute-start(bf16[4,256,256]{2,1,0:T(8,128)(2,1)S(1)} %get-tuple-element.22.refs_4_), channel_id=1, source_target_pairs={{0,8},{4,12},{8,16},{12,20},{16,24},{20,28},{24,0},{28,4},{1,9},{5... | collective-permute-start | bytes 1572872 | tf_op jit(solution)/shard_map/ppermute | solution.py:29
  50.2 17.5 %collective-permute-start.2 = (bf16[3,2,256,256]{3,2,1,0:T(8,128)(2,1)S(1)}, bf16[3,2,256,256]{3,2,1,0:T(8,128)(2,1)S(1)}, u32[]{:S(2)}, u32[]{:S(2)}) collective-permute-start(bf16[3,2,256,256]{3,2,1,0:T(8,128)(2,1)S(1)} %collective-permute-done.refs_1_), channel_id=1, source_target_pairs={{0,1},{1,0},{2,3},{3,2},{4,5},{5,4},{6,7},{7,6},{8,9},{9,8},{10,11... | collective-permute-start | bytes 2359304 | tf_op jit(solution)/shard_map/ppermute | solution.py:18
  50.3 17.7 %copy-start.1 = (bf16[3,8,256,256]{3,2,1,0:T(8,128)(2,1)S(1)}, bf16[3,8,256,256]{3,2,1,0:T(8,128)(2,1)}, u32[]{:S(2)}) copy-start(bf16[3,8,256,256]{3,2,1,0:T(8,128)(2,1)} %refs_2_.3) | copy-start | bytes 9437188
  50.3 28.4 %collective-permute-start.10 = (bf16[4,256,256]{2,1,0:T(8,128)(2,1)S(1)}, bf16[4,256,256]{2,1,0:T(8,128)(2,1)S(1)}, u32[]{:S(2)}, u32[]{:S(2)}) collective-permute-start(bf16[4,256,256]{2,1,0:T(8,128)(2,1)S(1)} %shard_map.58), channel_id=1, source_target_pairs={{0,8},{4,12},{8,16},{12,20},{16,24},{20,28},{24,0},{28,4},{1,9},{5... | collective-permute-start | bytes 1572872 | tf_op jit(solution)/shard_map/ppermute | solution.py:29
  51.9 26.8 %collective-permute-start.6 = (bf16[4,256,256]{2,1,0:T(8,128)(2,1)S(1)}, bf16[4,256,256]{2,1,0:T(8,128)(2,1)S(1)}, u32[]{:S(2)}, u32[]{:S(2)}) collective-permute-start(bf16[4,256,256]{2,1,0:T(8,128)(2,1)S(1)} %collective-permute-done.4.refs_6_.odd_ref), channel_id=1, source_target_pairs={{4,0},{12,8},{20,16},{28,24},{5,1},{13,9},{21,17},{29,25},{6,2},{1... | collective-permute-start | bytes 1572872 | tf_op jit(solution)/shard_map/ppermute | solution.py:29
  66.4 12.6 %collective-permute-start.8 = (bf16[4,256,256]{2,1,0:T(8,128)(2,1)S(1)}, bf16[4,256,256]{2,1,0:T(8,128)(2,1)S(1)}, u32[]{:S(2)}, u32[]{:S(2)}) collective-permute-start(bf16[4,256,256]{2,1,0:T(8,128)(2,1)S(1)} %collective-permute-done.5.refs_7_), channel_id=1, source_target_pairs={{4,0},{12,8},{20,16},{28,24},{5,1},{13,9},{21,17},{29,25},{6,2},{1... | collective-permute-start | bytes 1572872 | tf_op jit(solution)/shard_map/ppermute | solution.py:29
  68.0 20.9 %collective-permute-start.11 = (bf16[4,256,256]{2,1,0:T(8,128)(2,1)S(1)}, bf16[4,256,256]{2,1,0:T(8,128)(2,1)S(1)}, u32[]{:S(2)}, u32[]{:S(2)}) collective-permute-start(bf16[4,256,256]{2,1,0:T(8,128)(2,1)S(1)} %get-tuple-element.28.refs_5_), channel_id=1, source_target_pairs={{0,8},{4,12},{8,16},{12,20},{16,24},{20,28},{24,0},{28,4},{1,9},{5... | collective-permute-start | bytes 1572872 | tf_op jit(solution)/shard_map/ppermute | solution.py:29
  74.1 14.7 %collective-permute-start.13 = (bf16[4,256,256]{2,1,0:T(8,128)(2,1)S(1)}, bf16[4,256,256]{2,1,0:T(8,128)(2,1)S(1)}, u32[]{:S(2)}, u32[]{:S(2)}) collective-permute-start(bf16[4,256,256]{2,1,0:T(8,128)(2,1)S(1)} %collective-permute-done.4.refs_6_.odd_ref), channel_id=1, source_target_pairs={{0,4},{8,12},{16,20},{24,28},{1,5},{9,13},{17,21},{25,29},{2,6},{1... | collective-permute-start | bytes 1572872 | tf_op jit(solution)/shard_map/ppermute | solution.py:29
  79.1 11.7 %collective-permute-start.12 = (bf16[4,256,256]{2,1,0:T(8,128)(2,1)S(1)}, bf16[4,256,256]{2,1,0:T(8,128)(2,1)S(1)}, u32[]{:S(2)}, u32[]{:S(2)}) collective-permute-start(bf16[4,256,256]{2,1,0:T(8,128)(2,1)S(1)} %collective-permute-done.10.refs_7_), channel_id=1, source_target_pairs={{4,0},{12,8},{20,16},{28,24},{5,1},{13,9},{21,17},{29,25},{6,2},{1... | collective-permute-start | bytes 1572872 | tf_op jit(solution)/shard_map/ppermute | solution.py:29
  88.8 22.0 %copy-start.3 = (s32[64]{0:T(128)S(1)}, s32[64]{0:T(128)}, u32[]{:S(2)}) copy-start(s32[64]{0:T(128)} %param.8) | copy-start | bytes 772
  95.3 3.8 %collective-permute-start.14 = (f32[32,16]{1,0:T(8,128)S(1)}, f32[32,16]{1,0:T(8,128)S(1)}, u32[]{:S(2)}, u32[]{:S(2)}) collective-permute-start(f32[32,16]{1,0:T(8,128)S(1)} %shard_map.60), channel_id=1, source_target_pairs={{0,4},{4,0},{8,12},{12,8},{16,20},{20,16},{24,28},{28,24},{1,5},{5... | collective-permute-start | bytes 6152 | tf_op jit(solution)/shard_map/ppermute | solution.py:23
  96.1 3.7 %collective-permute-start.15 = (f32[32,16]{1,0:T(8,128)S(1)}, f32[32,16]{1,0:T(8,128)S(1)}, u32[]{:S(2)}, u32[]{:S(2)}) collective-permute-start(f32[32,16]{1,0:T(8,128)S(1)} %shard_map.60), channel_id=1, source_target_pairs={{0,2},{2,0},{1,3},{3,1},{4,6},{6,4},{5,7},{7,5},{8,10},{10,8},{9,1... | collective-permute-start | bytes 6152 | tf_op jit(solution)/shard_map/ppermute | solution.py:18
  97.6 4.6 %collective-permute-start.16 = (f32[32,16]{1,0:T(8,128)S(1)}, f32[32,16]{1,0:T(8,128)S(1)}, u32[]{:S(2)}, u32[]{:S(2)}) collective-permute-start(f32[32,16]{1,0:T(8,128)S(1)} %shard_map.60), channel_id=1, source_target_pairs={{0,6},{2,4},{4,2},{6,0},{8,14},{10,12},{12,10},{14,8},{16,22},{18,... | collective-permute-start | bytes 6152 | tf_op jit(solution)/shard_map/ppermute | solution.py:342
  102.2 4.4 %collective-permute-start.17 = (f32[2,32,16]{2,1,0:T(8,128)S(1)}, f32[2,32,16]{2,1,0:T(8,128)S(1)}, u32[]{:S(2)}, u32[]{:S(2)}) collective-permute-start(f32[2,32,16]{2,1,0:T(8,128)S(1)} %maximum_select_fusion), channel_id=1, source_target_pairs={{0,8},{4,12},{8,0},{12,4},{16,24},{20,28},{24,16},{28,20},{1,9},{5... | collective-permute-start | bytes 12296 | tf_op jit(solution)/shard_map/ppermute | solution.py:23
  106.6 6.5 %collective-permute-start.18 = (f32[2,32,16]{2,1,0:T(8,128)S(1)}, f32[2,32,16]{2,1,0:T(8,128)S(1)}, u32[]{:S(2)}, u32[]{:S(2)}) collective-permute-start(f32[2,32,16]{2,1,0:T(8,128)S(1)} %fusion.9), channel_id=1, source_target_pairs={{0,16},{4,20},{8,24},{12,28},{16,0},{20,4},{24,8},{28,12},{1,17},{... | collective-permute-start | bytes 12296 | tf_op jit(solution)/shard_map/ppermute | solution.py:23
